TPU v7x, 1024 devices: a whole 4x4x32 slice. The times are simulated.
1024 devices in a mesh: row: 32 (over z_lo, core), col: 32 (over y, z_hi, x).
Axes of the slice: x: 4, y: 4, z: 32 (z_hi: 2, z_lo: 16; z = z_hi * 16 + z_lo), core: 2. Of those that a mesh axis runs over, the one named last changes fastest.
Arguments:
- left_blocks: float32 [32, 32, 8, 128, 128], P('row', 'col'), may hold values from -6 to 6
- left_rows: int32 [32, 32, 8], P('row', 'col'), may hold values from 0 to 7
- left_cols: int32 [32, 32, 8], P('row', 'col'), may hold values from 0 to 31
- left_count: int32 [32, 32], P('row', 'col'), may hold values from 4 to 8, as said below
- right_blocks: float32 [32, 32, 20, 128, 128], P('row', 'col'), may hold values from -0.5 to 0.5
- right_rows: int32 [32, 32, 20], P('row', 'col'), may hold values from 0 to 31, as said below
- right_cols: int32 [32, 32, 20], P('row', 'col'), may hold values from 0 to 31
- right_count: int32 [32, 32], P('row', 'col'), may hold values from 10 to 20, as said below
- out_rows: int32 [32, 32, 24], P('row', 'col'), may hold values from 0 to 7, as said below
- out_cols: int32 [32, 32, 24], P('row', 'col'), may hold values from 0 to 31
Outputs:
- product_blocks: float32 [32, 32, 24, 128, 128], P('row', 'col')
Inputs may be any that keep to these rules, and one draw needn't show every extreme that they name: `left_count`: the live slots of one left list name distinct block rows and distinct inner indices; every left list has at least half of its 8 slots live and some list has all live. `right_rows`: the live slots of one right list name distinct positions, and at most 2 of them share an inner block index; the first two slots of every list share one. `right_count`: some right list has all 20 slots live. `out_rows`: the 24 product slots of one tile name distinct positions.
All inputs are finite; a program needn't handle non-finite values.
Results may differ from a plain program's by a relative error of at most 0.0003.
Values sent between devices are 32-bit elements; how exact they have to be, the bound alone decides.
No kernel may reach another device: no remote copies, remote signals or barrier semaphores. Data moves between devices by JAX's collectives and lax.ppermute only.
A program may use at most 32 MiB of HBM per device.

v0:
```python
import jax
import jax.numpy as jnp
from jax import lax
from jax.sharding import PartitionSpec as P

STEPS = 3


def passed_along(block, axis, distance):
    devices = range(lax.axis_size(axis))
    route = [((i - distance) % len(devices), i) for i in devices]
    return lax.ppermute(block, axis, route)


def local_terms(left_list, right_list, out_rows, out_cols):
    left_blocks, left_rows, left_cols, left_count = left_list
    right_blocks, right_rows, right_cols, right_count = right_list
    left_live = jnp.arange(left_rows.shape[0], dtype=jnp.int32) < left_count[0]
    right_live = jnp.arange(right_rows.shape[0], dtype=jnp.int32) < right_count[0]
    matched = (
        (left_cols[:, None] == right_rows[None, :]) & left_live[:, None] & right_live[None, :]
    ).astype(jnp.int32)
    ranking = jnp.cumsum(matched, axis=1) * matched
    chosen = jnp.stack([ranking == 1, ranking == 2], axis=1)
    positions = jnp.arange(right_rows.shape[0], dtype=jnp.int32)
    picks = jnp.sum(jnp.where(chosen, positions, 0), axis=2)
    present = jnp.any(chosen, axis=2)
    picked = right_blocks[picks]
    products = jnp.einsum("acd,amdf->amcf", left_blocks, picked, precision=lax.Precision.HIGHEST)
    pick_cols = right_cols[picks]
    weight = (
        present[None]
        & (left_rows[None, :, None] == out_rows[:, None, None])
        & (pick_cols[None] == out_cols[:, None, None])
    )
    slots = out_rows.shape[0]
    block_size = left_blocks.shape[1]
    flat_weight = weight.astype(jnp.float32).reshape(slots, -1)
    flat_products = products.reshape(-1, block_size * block_size)
    summed = jnp.dot(
        flat_weight,
        flat_products,
        precision=lax.Precision.HIGHEST,
        preferred_element_type=jnp.float32,
    )
    return summed.reshape(slots, block_size, block_size)


def shards(
    left_blocks,
    left_rows,
    left_cols,
    left_count,
    right_blocks,
    right_rows,
    right_cols,
    right_count,
    out_rows,
    out_cols,
):
    left_list = (left_blocks[0, 0], left_rows[0, 0], left_cols[0, 0], left_count[0])
    right_list = (right_blocks[0, 0], right_rows[0, 0], right_cols[0, 0], right_count[0])
    target_rows = out_rows[0, 0]
    target_cols = out_cols[0, 0]
    running = local_terms(left_list, right_list, target_rows, target_cols)
    moving_left = left_list
    moving_right = right_list
    for offset in range(1, STEPS):
        moving_left = passed_along(
            (moving_left[0], moving_left[1], moving_left[2], moving_left[3]), "col", -1
        )
        moving_right = passed_along(
            (moving_right[0], moving_right[1], moving_right[2], moving_right[3]), "row", -1
        )
        running = running + local_terms(moving_left, moving_right, target_rows, target_cols)
    return running[None, None]


def solution(mesh):
    in_specs = (
        P("row", "col", None, None, None),
        P("row", "col", None),
        P("row", "col", None),
        P("row", "col"),
        P("row", "col", None, None, None),
        P("row", "col", None),
        P("row", "col", None),
        P("row", "col"),
        P("row", "col", None),
        P("row", "col", None),
    )
    out_specs = P("row", "col", None, None, None)
    return jax.shard_map(shards, mesh=mesh, in_specs=in_specs, out_specs=out_specs, check_vma=False)
```

profile of v0, /device:TPU:97, one launch (start us, length us, event | category | flops | bytes accessed | tf_op | source)
XLA Modules:
  0.0 380.2 jit_solution(13600503914632073502)
XLA Ops:
  0.0 30.8 %collective-permute-start = (s32[8]{0:T(128)}, s32[8]{0:T(128)S(1)}, u32[]{:S(2)}, u32[]{:S(2)}) collective-permute-start(s32[8]{0:T(128)} %bitcast.140), channel_id=1, source_target_pairs={{1,0},{2,1},{3,2},{4,3},{5,4},{6,5},{7,6},{8,7},{9,8},{10,9},{11,1... | collective-permute-start | bytes 104 | tf_op jit(solution)/shard_map/ppermute | solution.py:12
  30.8 2.9 collective-permute-start.1
  33.6 2.1 collective-permute-start.5
  35.7 2.5 collective-permute-start.2
  38.2 3.1 collective-permute-start.6
  47.2 2.9 convolution_bitcast_fusion.2
  54.3 4.5 %collective-permute-done.3 = s32[1]{0:T(128)} collective-permute-done((s32[1]{0:T(128)}, s32[1]{0:T(128)}, u32[]{:S(2)}, u32[]{:S(2)}) %collective-permute-start.3) | collective-permute-done | bytes 36 | tf_op jit(solution)/shard_map/ppermute | solution.py:12
  59.5 13.7 %collective-permute-start.10 = (s32[1]{0:T(128)}, s32[1]{0:T(128)}, u32[]{:S(2)}, u32[]{:S(2)}) collective-permute-start(s32[1]{0:T(128)} %collective-permute-done.2), channel_id=1, source_target_pairs={{1,0},{2,1},{3,2},{4,3},{5,4},{6,5},{7,6},{8,7},{9,8},{10,9},{11,1... | collective-permute-start | bytes 20 | tf_op jit(solution)/shard_map/ppermute | solution.py:12
  76.5 3.6 collective-permute-done.11
  80.1 26.1 %collective-permute-start.4 = (s32[8]{0:T(128)S(1)}, s32[8]{0:T(128)S(1)}, u32[]{:S(2)}, u32[]{:S(2)}) collective-permute-start(s32[8]{0:T(128)S(1)} %bitcast.148), channel_id=1, source_target_pairs={{1,0},{2,1},{3,2},{4,3},{5,4},{6,5},{7,6},{8,7},{9,8},{10,9},{11,1... | collective-permute-start | bytes 104 | tf_op jit(solution)/shard_map/ppermute | solution.py:12
  106.9 26.3 %collective-permute-start.7 = (f32[8,128,128]{2,1,0:T(8,128)S(1)}, f32[8,128,128]{2,1,0:T(8,128)}, u32[]{:S(2)}, u32[]{:S(2)}) collective-permute-start(f32[8,128,128]{2,1,0:T(8,128)S(1)} %bitcast.139), channel_id=1, source_target_pairs={{1,0},{2,1},{3,2},{4,3},{5,4},{6,5},{7,6},{8,7},{9,8},{10,9},{11,1... | collective-permute-start | bytes 1572872 | tf_op jit(solution)/shard_map/ppermute | solution.py:12
  135.1 87.0 %collective-permute-done.12 = s32[8]{0:T(128)S(1)} collective-permute-done((s32[8]{0:T(128)S(1)}, s32[8]{0:T(128)S(1)}, u32[]{:S(2)}, u32[]{:S(2)}) %collective-permute-start.12) | collective-permute-done | bytes 64 | tf_op jit(solution)/shard_map/ppermute | solution.py:12
  222.1 26.8 %collective-permute-start.8 = (s32[8]{0:T(128)S(1)}, s32[8]{0:T(128)S(1)}, u32[]{:S(2)}, u32[]{:S(2)}) collective-permute-start(s32[8]{0:T(128)S(1)} %collective-permute-done), channel_id=1, source_target_pairs={{1,0},{2,1},{3,2},{4,3},{5,4},{6,5},{7,6},{8,7},{9,8},{10,9},{11,1... | collective-permute-start | bytes 104 | tf_op jit(solution)/shard_map/ppermute | solution.py:12
  250.6 2.8 collective-permute-start.9
  261.9 21.3 %collective-permute-start.15 = (f32[8,128,128]{2,1,0:T(8,128)}, f32[8,128,128]{2,1,0:T(8,128)}, u32[]{:S(2)}, u32[]{:S(2)}) collective-permute-start(f32[8,128,128]{2,1,0:T(8,128)} %collective-permute-done.7), channel_id=1, source_target_pairs={{1,0},{2,1},{3,2},{4,3},{5,4},{6,5},{7,6},{8,7},{9,8},{10,9},{11,1... | collective-permute-start | bytes 1572872 | tf_op jit(solution)/shard_map/ppermute | solution.py:12
  283.2 1.9 gather_fusion.3
  285.2 4.0 %convolution_bitcast_fusion.1 = f32[8,2,128,128]{2,3,1,0:T(8,128)} fusion(f32[8,2,128,128]{3,2,1,0:T(8,128)S(1)} %bitcast.135, f32[8,128,128]{2,1,0:T(8,128)} %collective-permute-done.7), kind=kOutput, calls=%fused_computation.8 | convolution fusion | flops 402653184 | bytes 2621440 | tf_op jit(solution)/shard_map/acd,amdf->amcf/dot_general | solution.py:29
  289.1 2.5 copy.39
  291.7 2.5 fusion.2
  294.2 72.2 %collective-permute-done.14 = f32[20,128,128]{2,1,0:T(8,128)} collective-permute-done((f32[20,128,128]{2,1,0:T(8,128)}, f32[20,128,128]{2,1,0:T(8,128)}, u32[]{:S(2)}, u32[]{:S(2)}) %collective-permute-start.14) | collective-permute-done | bytes 1310752 | tf_op jit(solution)/shard_map/ppermute | solution.py:12
  366.4 2.9 gather_fusion.5
  369.3 4.3 %convolution_bitcast_fusion = f32[8,2,128,128]{2,3,1,0:T(8,128)} fusion(f32[8,2,128,128]{3,2,1,0:T(8,128)} %bitcast.132, f32[8,128,128]{2,1,0:T(8,128)} %collective-permute-done.15), kind=kOutput, calls=%fused_computation.7 | convolution fusion | flops 402653184 | bytes 2621440 | tf_op jit(solution)/shard_map/acd,amdf->amcf/dot_general | solution.py:29
  373.6 2.5 copy.44
  376.1 2.6 add_bitcast_fusion
  (80 shorter events, 26.7 us)
Async XLA Ops:
  0.0 44.8 %copy-start = (s32[1,1,20]{2,1,0:T(1,128)S(1)}, s32[1,1,20]{2,1,0:T(1,128)}, u32[]{:S(2)}) copy-start(s32[1,1,20]{2,1,0:T(1,128)} %param.16) | copy-start | bytes 244
  0.0 133.1 %collective-permute-start = (s32[8]{0:T(128)}, s32[8]{0:T(128)S(1)}, u32[]{:S(2)}, u32[]{:S(2)}) collective-permute-start(s32[8]{0:T(128)} %bitcast.140), channel_id=1, source_target_pairs={{1,0},{2,1},{3,2},{4,3},{5,4},{6,5},{7,6},{8,7},{9,8},{10,9},{11,1... | collective-permute-start | bytes 104 | tf_op jit(solution)/shard_map/ppermute | solution.py:12
  30.8 218.2 %collective-permute-start.1 = (s32[20]{0:T(128)}, s32[20]{0:T(128)S(1)}, u32[]{:S(2)}, u32[]{:S(2)}) collective-permute-start(s32[20]{0:T(128)} %bitcast.143), channel_id=1, source_target_pairs={{32,0},{64,32},{96,64},{128,96},{160,128},{192,160},{224,192},{256... | collective-permute-start | bytes 248 | tf_op jit(solution)/shard_map/ppermute | solution.py:12
  33.6 216.3 %collective-permute-start.5 = (s32[20]{0:T(128)}, s32[20]{0:T(128)S(1)}, u32[]{:S(2)}, u32[]{:S(2)}) collective-permute-start(s32[20]{0:T(128)} %bitcast.129), channel_id=1, source_target_pairs={{32,0},{64,32},{96,64},{128,96},{160,128},{192,160},{224,192},{256... | collective-permute-start | bytes 248 | tf_op jit(solution)/shard_map/ppermute | solution.py:12
  35.7 16.0 %collective-permute-start.2 = (s32[1]{0:T(128)}, s32[1]{0:T(128)}, u32[]{:S(2)}, u32[]{:S(2)}) collective-permute-start(s32[1]{0:T(128)} %bitcast.17), channel_id=1, source_target_pairs={{1,0},{2,1},{3,2},{4,3},{5,4},{6,5},{7,6},{8,7},{9,8},{10,9},{11,1... | collective-permute-start | bytes 20 | tf_op jit(solution)/shard_map/ppermute | solution.py:12
  38.2 219.0 %collective-permute-start.6 = (f32[20,128,128]{2,1,0:T(8,128)}, f32[20,128,128]{2,1,0:T(8,128)}, u32[]{:S(2)}, u32[]{:S(2)}) collective-permute-start(f32[20,128,128]{2,1,0:T(8,128)} %bitcast.137), channel_id=1, source_target_pairs={{32,0},{64,32},{96,64},{128,96},{160,128},{192,160},{224,192},{256... | collective-permute-start | bytes 3932168 | tf_op jit(solution)/shard_map/ppermute | solution.py:12
  44.8 1.3 copy-start.1
  46.2 1.0 copy-start.2
  50.1 29.9 %copy-start.5 = (s32[1,1,8]{2,1,0:T(1,128)S(1)}, s32[1,1,8]{2,1,0:T(1,128)}, u32[]{:S(2)}) copy-start(s32[1,1,8]{2,1,0:T(1,128)} %param.11) | copy-start | bytes 100
  50.1 198.8 %copy-start.4 = (s32[1,1,24]{2,1,0:T(1,128)S(1)}, s32[1,1,24]{2,1,0:T(1,128)}, u32[]{:S(2)}) copy-start(s32[1,1,24]{2,1,0:T(1,128)} %param.18) | copy-start | bytes 292
  51.7 7.1 %collective-permute-start.3 = (s32[1]{0:T(128)}, s32[1]{0:T(128)}, u32[]{:S(2)}, u32[]{:S(2)}) collective-permute-start(s32[1]{0:T(128)} %bitcast.19), channel_id=1, source_target_pairs={{32,0},{64,32},{96,64},{128,96},{160,128},{192,160},{224,192},{256... | collective-permute-start | bytes 20 | tf_op jit(solution)/shard_map/ppermute | solution.py:12
  59.5 14.5 %collective-permute-start.10 = (s32[1]{0:T(128)}, s32[1]{0:T(128)}, u32[]{:S(2)}, u32[]{:S(2)}) collective-permute-start(s32[1]{0:T(128)} %collective-permute-done.2), channel_id=1, source_target_pairs={{1,0},{2,1},{3,2},{4,3},{5,4},{6,5},{7,6},{8,7},{9,8},{10,9},{11,1... | collective-permute-start | bytes 20 | tf_op jit(solution)/shard_map/ppermute | solution.py:12
  74.0 6.1 %collective-permute-start.11 = (s32[1]{0:T(128)}, s32[1]{0:T(128)}, u32[]{:S(2)}, u32[]{:S(2)}) collective-permute-start(s32[1]{0:T(128)} %collective-permute-done.3), channel_id=1, source_target_pairs={{32,0},{64,32},{96,64},{128,96},{160,128},{192,160},{224,192},{256... | collective-permute-start | bytes 20 | tf_op jit(solution)/shard_map/ppermute | solution.py:12
  80.1 26.8 %collective-permute-start.4 = (s32[8]{0:T(128)S(1)}, s32[8]{0:T(128)S(1)}, u32[]{:S(2)}, u32[]{:S(2)}) collective-permute-start(s32[8]{0:T(128)S(1)} %bitcast.148), channel_id=1, source_target_pairs={{1,0},{2,1},{3,2},{4,3},{5,4},{6,5},{7,6},{8,7},{9,8},{10,9},{11,1... | collective-permute-start | bytes 104 | tf_op jit(solution)/shard_map/ppermute | solution.py:12
  106.9 155.0 %collective-permute-start.7 = (f32[8,128,128]{2,1,0:T(8,128)S(1)}, f32[8,128,128]{2,1,0:T(8,128)}, u32[]{:S(2)}, u32[]{:S(2)}) collective-permute-start(f32[8,128,128]{2,1,0:T(8,128)S(1)} %bitcast.139), channel_id=1, source_target_pairs={{1,0},{2,1},{3,2},{4,3},{5,4},{6,5},{7,6},{8,7},{9,8},{10,9},{11,1... | collective-permute-start | bytes 1572872 | tf_op jit(solution)/shard_map/ppermute | solution.py:12
  133.1 88.9 %collective-permute-start.12 = (s32[8]{0:T(128)S(1)}, s32[8]{0:T(128)S(1)}, u32[]{:S(2)}, u32[]{:S(2)}) collective-permute-start(s32[8]{0:T(128)S(1)} %collective-permute-done.4), channel_id=1, source_target_pairs={{1,0},{2,1},{3,2},{4,3},{5,4},{6,5},{7,6},{8,7},{9,8},{10,9},{11,1... | collective-permute-start | bytes 104 | tf_op jit(solution)/shard_map/ppermute | solution.py:12
  222.1 33.3 %collective-permute-start.8 = (s32[8]{0:T(128)S(1)}, s32[8]{0:T(128)S(1)}, u32[]{:S(2)}, u32[]{:S(2)}) collective-permute-start(s32[8]{0:T(128)S(1)} %collective-permute-done), channel_id=1, source_target_pairs={{1,0},{2,1},{3,2},{4,3},{5,4},{6,5},{7,6},{8,7},{9,8},{10,9},{11,1... | collective-permute-start | bytes 104 | tf_op jit(solution)/shard_map/ppermute | solution.py:12
  250.6 6.1 %collective-permute-start.9 = (s32[20]{0:T(128)S(1)}, s32[20]{0:T(128)S(1)}, u32[]{:S(2)}, u32[]{:S(2)}) collective-permute-start(s32[20]{0:T(128)S(1)} %collective-permute-done.1), channel_id=1, source_target_pairs={{32,0},{64,32},{96,64},{128,96},{160,128},{192,160},{224,192},{256... | collective-permute-start | bytes 248 | tf_op jit(solution)/shard_map/ppermute | solution.py:12
  253.4 6.1 %collective-permute-start.13 = (s32[20]{0:T(128)S(1)}, s32[20]{0:T(128)S(1)}, u32[]{:S(2)}, u32[]{:S(2)}) collective-permute-start(s32[20]{0:T(128)S(1)} %collective-permute-done.5), channel_id=1, source_target_pairs={{32,0},{64,32},{96,64},{128,96},{160,128},{192,160},{224,192},{256... | collective-permute-start | bytes 248 | tf_op jit(solution)/shard_map/ppermute | solution.py:12
  257.2 109.2 %collective-permute-start.14 = (f32[20,128,128]{2,1,0:T(8,128)}, f32[20,128,128]{2,1,0:T(8,128)}, u32[]{:S(2)}, u32[]{:S(2)}) collective-permute-start(f32[20,128,128]{2,1,0:T(8,128)} %collective-permute-done.6), channel_id=1, source_target_pairs={{32,0},{64,32},{96,64},{128,96},{160,128},{192,160},{224,192},{256... | collective-permute-start | bytes 3932168 | tf_op jit(solution)/shard_map/ppermute | solution.py:12
  259.6 0.8 copy-start.3
  261.9 107.4 %collective-permute-start.15 = (f32[8,128,128]{2,1,0:T(8,128)}, f32[8,128,128]{2,1,0:T(8,128)}, u32[]{:S(2)}, u32[]{:S(2)}) collective-permute-start(f32[8,128,128]{2,1,0:T(8,128)} %collective-permute-done.7), channel_id=1, source_target_pairs={{1,0},{2,1},{3,2},{4,3},{5,4},{6,5},{7,6},{8,7},{9,8},{10,9},{11,1... | collective-permute-start | bytes 1572872 | tf_op jit(solution)/shard_map/ppermute | solution.py:12
where the time goes:
time: 381 us; the launch traced here: 380 us
  waiting for transfers between devices  169 us (44%)
  starting transfers between devices  168 us (44%)
  matrix products  17.7 us (5%)
  local copies, waits for them, and re-layouts  17.5 us (5%)
  other arithmetic  5.99 us (2%)
    ppermute x16, waiting for transfers between devices, passed_along(): return lax.ppermute(block, axis, route)  169 us
    ppermute x16, starting transfers between devices, passed_along(): return lax.ppermute(block, axis, route)  168 us
    dot_general x3, matrix products, local_terms(): jnp.einsum('acd,amdf->amcf', left_blocks, picked, precision=lax.Precision...  11.2 us
  transfers between devices with their start and end apart: 16, of which 7 were waited for; matrix products, arithmetic and copies ran while one was open for 8% of the time, Pallas kernels for 0%

commit v1 on v0

v1 whole, which is shorter than its diff:
```python
import jax
import jax.numpy as jnp
from jax import lax
from jax.experimental import pallas as pl
from jax.experimental.pallas import tpu as pltpu
from jax.sharding import PartitionSpec as P

BS = 128
MAXA = 8
MAXB = 20
CMAX = 24
ROWB = 8
INB = 32
COLB = 32
HALF = MAXA // 2 * BS
PAD = 8
LEFT_HALF = HALF + PAD
RIGHT_ROWS = MAXB * BS
N_ROW = 32
N_COL = 32
AXES = ("row", "col")

GROUP = 4
N_GROUP = N_COL // GROUP


def route(place):
    pairs = []
    for row in range(N_ROW):
        for col in range(N_COL):
            target = place(row, col // GROUP, col % GROUP)
            if target is not None:
                r, g, x = target
                pairs.append((row * N_COL + col, (r % N_ROW) * N_COL + (g % N_GROUP) * GROUP + x))
    return pairs


def along_x(moves):
    return route(lambda r, g, x: (r, g, moves[x]) if x in moves else None)


def to_previous_group(moves):
    return route(lambda r, g, x: (r, g - 1, moves[x]) if x in moves else None)


def send(block, pairs):
    return lax.ppermute(block, AXES, pairs)


def clear(table, size):
    def body(i, carry):
        table[i] = -1
        return carry

    lax.fori_loop(0, size, body, 0, unroll=8)


def mark_slots(out_rows, out_cols, slot_of):
    clear(slot_of, ROWB * COLB)
    for c in range(CMAX):
        slot_of[out_rows[c] * COLB + out_cols[c]] = c


def list_products(left_meta, right_meta, slot_of, by_inner, products, start):
    def left_int(i):
        return left_meta[0, i].astype(jnp.int32)

    def right_int(i):
        return right_meta[0, i].astype(jnp.int32)

    left_count = left_int(2 * MAXA)
    right_count = right_int(2 * MAXB)
    clear(by_inner, 2 * INB)
    for b in range(MAXB):
        place = jnp.where(b < right_count, right_int(b) * 2, 2 * INB)
        taken = (by_inner[place] >= 0) & (b < right_count)
        by_inner[place + taken.astype(jnp.int32)] = b
    count = start
    for a in range(MAXA):
        row, inner = left_int(a), left_int(MAXA + a)
        for m in range(2):
            b = by_inner[inner * 2 + m]
            column = right_int(MAXB + jnp.maximum(b, 0))
            c = slot_of[row * COLB + column]
            products[count] = (a * 32 + b) * 32 + c
            valid = (a < left_count) & (b >= 0) & (c >= 0)
            count = count + valid.astype(jnp.int32)
    return count


def split(value):
    high = value.astype(jnp.bfloat16)
    low = (value - high.astype(jnp.float32)).astype(jnp.bfloat16)
    return high, low


def multiply(products, first, last, left, right, total):
    def body(i, carry):
        code = products[i]
        a = code // 1024
        b = (code // 32) % 32
        c = code % 32
        left_high, left_low = split(left[pl.ds(pl.multiple_of(a * BS, BS), BS), :])
        right_high, right_low = split(right[pl.ds(pl.multiple_of(b * BS, BS), BS), :])
        lhs = jnp.concatenate([left_high, left_low], axis=1)
        both = jnp.concatenate([right_high, right_low], axis=1)
        rhs = jnp.concatenate([both, both], axis=0)
        pair = jnp.dot(lhs, rhs, preferred_element_type=jnp.float32)
        place = pl.ds(pl.multiple_of(c * BS, BS), BS)
        total[place, :] = total[place, :] + (pair[:, :BS] + pair[:, BS:])
        return carry

    lax.fori_loop(first, last, body, 0)


def first_kernel(
    out_rows, out_cols, left_hbm, right_hbm, out_hbm, left, right, total, left_meta, right_meta, slot_of, by_inner, products, sems
):
    copies = [
        pltpu.make_async_copy(left_hbm.at[pl.ds(HALF, PAD)], left_meta, sems.at[0]),
        pltpu.make_async_copy(right_hbm.at[pl.ds(RIGHT_ROWS, PAD)], right_meta, sems.at[1]),
        pltpu.make_async_copy(left_hbm.at[pl.ds(0, HALF)], left.at[pl.ds(0, HALF)], sems.at[2]),
        pltpu.make_async_copy(left_hbm.at[pl.ds(LEFT_HALF, HALF)], left.at[pl.ds(HALF, HALF)], sems.at[3]),
        pltpu.make_async_copy(right_hbm.at[pl.ds(0, RIGHT_ROWS)], right, sems.at[4]),
    ]
    for copy in copies:
        copy.start()
    mark_slots(out_rows, out_cols, slot_of)
    total[...] = jnp.zeros_like(total)
    copies[0].wait()
    copies[1].wait()
    count = list_products(left_meta, right_meta, slot_of, by_inner, products, 0)
    for copy in copies[2:]:
        copy.wait()
    multiply(products, 0, count, left, right, total)
    out = pltpu.make_async_copy(total, out_hbm, sems.at[0])
    out.start()
    out.wait()


def last_kernel(
    place, out_rows, out_cols, near, far, across_low, across_high, over_low, over_high, right_core, right_next, right_both, total_hbm, out_hbm,
    left, right, total, left_meta, right_meta, slot_of, by_inner, products, sems,
):
    x, core = place[0], place[1]

    def left_copies(step, low, low_at, high, high_at):
        base = step * MAXA * BS
        return [
            pltpu.make_async_copy(low.at[pl.ds(low_at + HALF, PAD)], left_meta.at[step], sems.at[step, 0]),
            pltpu.make_async_copy(low.at[pl.ds(low_at, HALF)], left.at[pl.ds(base, HALF)], sems.at[step, 1]),
            pltpu.make_async_copy(high.at[pl.ds(high_at, HALF)], left.at[pl.ds(base + HALF, HALF)], sems.at[step, 2]),
        ]

    def right_copies(step, source):
        return [
            pltpu.make_async_copy(source.at[pl.ds(RIGHT_ROWS, PAD)], right_meta.at[step], sems.at[step, 3]),
            pltpu.make_async_copy(
                source.at[pl.ds(0, RIGHT_ROWS)], right.at[pl.ds(step * RIGHT_ROWS, RIGHT_ROWS)], sems.at[step, 4]
            ),
        ]

    def start(copies):
        for copy in copies:
            copy.start()

    base_copy = pltpu.make_async_copy(total_hbm, total, sems.at[2, 0])
    one_left = left_copies(0, over_low, 0, over_high, 0)
    two_left = left_copies(1, across_low, 0, across_high, 0)
    one_right = right_copies(0, right_core)
    two_right = right_copies(1, right_next)

    pl.when(x < 3)(lambda: start(left_copies(0, near, 0, near, LEFT_HALF)))
    pl.when(x == 3)(lambda: start(one_left))
    pl.when(core == 0)(lambda: start(one_right))
    pl.when(core == 1)(lambda: start(right_copies(0, right_both)))
    base_copy.start()
    pl.when(x < 2)(lambda: start(left_copies(1, far, 0, far, LEFT_HALF)))
    pl.when(x >= 2)(lambda: start(two_left))
    start(two_right)

    mark_slots(out_rows, out_cols, slot_of)
    one_left[0].wait()
    one_right[0].wait()
    middle = list_products(left_meta.at[0], right_meta.at[0], slot_of, by_inner, products, 0)
    two_left[0].wait()
    two_right[0].wait()
    end = list_products(left_meta.at[1], right_meta.at[1], slot_of, by_inner, products, middle)
    base_copy.wait()
    for copy in one_left[1:] + one_right[1:]:
        copy.wait()
    multiply(products, 0, middle, left, right, total)
    for copy in two_left[1:] + two_right[1:]:
        copy.wait()
    multiply(
        products, middle, end, left.at[pl.ds(MAXA * BS, MAXA * BS)], right.at[pl.ds(RIGHT_ROWS, RIGHT_ROWS)], total
    )
    out = pltpu.make_async_copy(total, out_hbm, sems.at[2, 1])
    out.start()
    out.wait()


SMEM_SPEC = pl.BlockSpec(memory_space=pltpu.SMEM)
ANY_SPEC = pl.BlockSpec(memory_space=pl.ANY)


def tables():
    return [
        pltpu.SMEM((ROWB * COLB,), jnp.int32),
        pltpu.SMEM((2 * INB + 8,), jnp.int32),
        pltpu.SMEM((64,), jnp.int32),
    ]


def first_step(out_rows, out_cols, left, right):
    return pl.pallas_call(
        first_kernel,
        out_shape=jax.ShapeDtypeStruct((CMAX * BS, BS), jnp.float32),
        in_specs=[SMEM_SPEC] * 2 + [ANY_SPEC] * 2,
        out_specs=ANY_SPEC,
        scratch_shapes=[
            pltpu.VMEM((MAXA * BS, BS), jnp.float32),
            pltpu.VMEM((RIGHT_ROWS, BS), jnp.float32),
            pltpu.VMEM((CMAX * BS, BS), jnp.float32),
            pltpu.SMEM((PAD, BS), jnp.float32),
            pltpu.SMEM((PAD, BS), jnp.float32),
        ]
        + tables()
        + [pltpu.SemaphoreType.DMA((5,))],
        compiler_params=pltpu.CompilerParams(vmem_limit_bytes=16 * 2**20),
        name="first_step",
    )(out_rows, out_cols, left, right)


def last_steps(place, out_rows, out_cols, buffers, total):
    return pl.pallas_call(
        last_kernel,
        out_shape=jax.ShapeDtypeStruct((CMAX * BS, BS), jnp.float32),
        in_specs=[SMEM_SPEC] * 3 + [ANY_SPEC] * (len(buffers) + 1),
        out_specs=ANY_SPEC,
        input_output_aliases={3 + len(buffers): 0},
        scratch_shapes=[
            pltpu.VMEM((2 * MAXA * BS, BS), jnp.float32),
            pltpu.VMEM((2 * RIGHT_ROWS, BS), jnp.float32),
            pltpu.VMEM((CMAX * BS, BS), jnp.float32),
            pltpu.SMEM((2, PAD, BS), jnp.float32),
            pltpu.SMEM((2, PAD, BS), jnp.float32),
        ]
        + tables()
        + [pltpu.SemaphoreType.DMA((3, 5))],
        compiler_params=pltpu.CompilerParams(vmem_limit_bytes=16 * 2**20),
        name="last_steps",
    )(place, out_rows, out_cols, *buffers, total)


def meta_rows(*parts):
    line = jnp.concatenate(parts).astype(jnp.float32)
    return jnp.pad(line[None], ((0, PAD - 1), (0, BS - line.shape[0])))


def shards(
    left_blocks,
    left_rows,
    left_cols,
    left_count,
    right_blocks,
    right_rows,
    right_cols,
    right_count,
    out_rows,
    out_cols,
):
    left_meta = meta_rows(left_rows[0, 0], left_cols[0, 0], left_count[0])
    right_meta = meta_rows(right_rows[0, 0], right_cols[0, 0], right_count[0])
    blocks = left_blocks.reshape(MAXA * BS, BS)
    low = jnp.concatenate([blocks[:HALF], left_meta])
    high = jnp.concatenate([blocks[HALF:], left_meta])
    left = jnp.concatenate([low, high])
    right = jnp.concatenate([right_blocks.reshape(RIGHT_ROWS, BS), right_meta])
    place = jnp.stack([lax.axis_index("col") % GROUP, lax.axis_index("row") % 2]).astype(jnp.int32)

    spread = send(high, along_x({0: 3, 1: 2}))
    across_low = send(low, to_previous_group({0: 2, 1: 3}))
    right_next = send(right, route(lambda r, g, x: (r - 2, g, x)))
    near = send(left, along_x({1: 0, 2: 1, 3: 2}))
    far = send(left, along_x({2: 0, 3: 1}))
    across_high = send(spread, to_previous_group({3: 2, 2: 3}))
    left, right, _ = lax.optimization_barrier((left, right, spread))
    total = first_step(out_rows[0, 0], out_cols[0, 0], left, right)
    right, total, near, far, across_low, across_high = lax.optimization_barrier(
        (right, total, near, far, across_low, across_high)
    )
    over_low = send(across_low, along_x({2: 3}))
    over_high = send(across_high, along_x({2: 3}))
    right_core = send(right, route(lambda r, g, x: (r - 1, g, x) if r % 2 else None))
    right_next, right_core, over_low, over_high = lax.optimization_barrier(
        (right_next, right_core, over_low, over_high)
    )
    right_both = send(right_next, route(lambda r, g, x: (r + 1, g, x) if r % 2 == 0 else None))
    buffers = [near, far, across_low, across_high, over_low, over_high, right_core, right_next, right_both]
    total = last_steps(place, out_rows[0, 0], out_cols[0, 0], buffers, total)
    return total.reshape(1, 1, CMAX, BS, BS)


def solution(mesh):
    in_specs = (
        P("row", "col", None, None, None),
        P("row", "col", None),
        P("row", "col", None),
        P("row", "col"),
        P("row", "col", None, None, None),
        P("row", "col", None),
        P("row", "col", None),
        P("row", "col"),
        P("row", "col", None),
        P("row", "col", None),
    )
    out_specs = P("row", "col", None, None, None)
    return jax.shard_map(shards, mesh=mesh, in_specs=in_specs, out_specs=out_specs, check_vma=False)
```

time: 381 us -> 149 us (0.39)
  the two profiles are of different devices: /device:TPU:97 before, /device:TPU:71 now
where the time goes in v1:
time: 149 us
  waiting for transfers between devices  77.9 us (52%)
  starting transfers between devices  49.6 us (33%)
  Pallas kernels  10.7 us (7%)
  local copies, waits for them, and re-layouts  7.91 us (5%)
  between operations  1.54 us (1%)
    ppermute x10, waiting for transfers between devices, send(): return lax.ppermute(block, AXES, pairs)  77.9 us
    ppermute x10, starting transfers between devices, send(): return lax.ppermute(block, AXES, pairs)  49.6 us
    pallas_call x1, Pallas kernels, last_steps(): pl.pallas_call(last_kernel, out_shape=jax.ShapeDtypeStruct((CMAX * BS, BS...  6.87 us
    unnamed x26, local copies, waits for them, and re-layouts  6.83 us
    pallas_call x1, Pallas kernels, first_step(): pl.pallas_call(first_kernel, out_shape=jax.ShapeDtypeStruct((CMAX * BS, B...  3.83 us
  transfers between devices with their start and end apart: 10, of which 4 were waited for; matrix products, arithmetic and copies ran while one was open for 0% of the time, Pallas kernels for 3%

profile of v1, /device:TPU:71, one launch (start us, length us, event | category | flops | bytes accessed | tf_op | source)
XLA Modules:
  0.0 148.8 jit_solution(17120963904950560259)
XLA Ops:
  0.7 1.1 fusion
  1.8 0.9 add_convert_fusion
  2.7 1.3 collective-permute-start
  4.0 4.9 %collective-permute-start.2 = (f32[1040,128]{1,0:T(8,128)S(1)}, f32[1040,128]{1,0:T(8,128)S(1)}, u32[]{:S(2)}, u32[]{:S(2)}) collective-permute-start(f32[1040,128]{1,0:T(8,128)S(1)} %pad_maximum_fusion.left_hbm), channel_id=1, source_target_pairs={{2,0},{3,1},{6,4},{7,5},{10,8},{11,9},{14,12},{15,13},{18,16},{19,... | collective-permute-start | bytes 1597448 | tf_op jit(solution)/shard_map/ppermute | solution.py:47
  8.9 2.9 %collective-permute-start.1 = (f32[1040,128]{1,0:T(8,128)S(1)}, f32[1040,128]{1,0:T(8,128)S(1)}, u32[]{:S(2)}, u32[]{:S(2)}) collective-permute-start(f32[1040,128]{1,0:T(8,128)S(1)} %pad_maximum_fusion.left_hbm), channel_id=1, source_target_pairs={{1,0},{2,1},{3,2},{5,4},{6,5},{7,6},{9,8},{10,9},{11,10},{13,12},{... | collective-permute-start | bytes 1597448 | tf_op jit(solution)/shard_map/ppermute | solution.py:47
  11.8 1.3 collective-permute-start.3
  13.8 29.0 %collective-permute-start.4 = (f32[520,128]{1,0:T(8,128)S(1)}, f32[520,128]{1,0:T(8,128)S(1)}, u32[]{:S(2)}, u32[]{:S(2)}) collective-permute-start(f32[520,128]{1,0:T(8,128)S(1)} %collective-permute-done), channel_id=1, source_target_pairs={{2,31},{3,30},{6,3},{7,2},{10,7},{11,6},{14,11},{15,10},{18,15},{1... | collective-permute-start | bytes 798728 | tf_op jit(solution)/shard_map/ppermute | solution.py:47
  43.0 2.6 %collective-permute-start.5 = (f32[2568,128]{1,0:T(8,128)S(1)}, f32[2568,128]{1,0:T(8,128)S(1)}, u32[]{:S(2)}, u32[]{:S(2)}) collective-permute-start(f32[2568,128]{1,0:T(8,128)S(1)} %select_maximum_fusion.right_hbm), channel_id=1, source_target_pairs={{0,960},{1,961},{2,962},{3,963},{4,964},{5,965},{6,966},{7,967},{8... | collective-permute-start | bytes 3944456 | tf_op jit(solution)/shard_map/ppermute | solution.py:47
  45.7 3.8 %first_step.1.total_hbm = f32[3072,128]{1,0:T(8,128)} custom-call(s32[24]{0:T(128)S(1)} %bitcast.12, s32[24]{0:T(128)S(1)} %bitcast.14, f32[1040,128]{1,0:T(8,128)S(1)} %pad_maximum_fusion.left_hbm, f32[2568,128]{1,0:T(8,128)S(1)} %select_maximum_fusion.right_hbm), custom_call_target="tpu_custom_call" | custom-call | tf_op jit(solution)/shard_map/first_step/pallas_call | solution.py:216
  49.5 3.0 %collective-permute-done.4.across_high = f32[520,128]{1,0:T(8,128)S(1)} collective-permute-done((f32[520,128]{1,0:T(8,128)S(1)}, f32[520,128]{1,0:T(8,128)S(1)}, u32[]{:S(2)}, u32[]{:S(2)}) %collective-permute-start.4) | collective-permute-done | bytes 266272 | tf_op jit(solution)/shard_map/ppermute | solution.py:47
  52.5 0.8 copy-done
  53.3 3.7 %collective-permute-start.6 = (f32[2568,128]{1,0:T(8,128)S(1)}, f32[2568,128]{1,0:T(8,128)S(1)}, u32[]{:S(2)}, u32[]{:S(2)}) collective-permute-start(f32[2568,128]{1,0:T(8,128)S(1)} %select_maximum_fusion.right_hbm), channel_id=1, source_target_pairs={{32,0},{33,1},{34,2},{35,3},{36,4},{37,5},{38,6},{39,7},{40,8},{41... | collective-permute-start | bytes 3944456 | tf_op jit(solution)/shard_map/ppermute | solution.py:47
  57.0 1.3 collective-permute-start.7
  58.3 1.3 collective-permute-start.8
  60.3 67.0 %collective-permute-done.7.over_low = f32[520,128]{1,0:T(8,128)S(1)} collective-permute-done((f32[520,128]{1,0:T(8,128)S(1)}, f32[520,128]{1,0:T(8,128)S(1)}, u32[]{:S(2)}, u32[]{:S(2)}) %collective-permute-start.7) | collective-permute-done | bytes 266272 | tf_op jit(solution)/shard_map/ppermute | solution.py:47
  128.0 4.3 %collective-permute-done.8.over_high = f32[520,128]{1,0:T(8,128)S(1)} collective-permute-done((f32[520,128]{1,0:T(8,128)S(1)}, f32[520,128]{1,0:T(8,128)S(1)}, u32[]{:S(2)}, u32[]{:S(2)}) %collective-permute-start.8) | collective-permute-done | bytes 266272 | tf_op jit(solution)/shard_map/ppermute | solution.py:47
  132.3 0.7 copy-done.6
  133.0 1.3 collective-permute-start.9
  134.4 3.7 %collective-permute-done.9.right_both = f32[2568,128]{1,0:T(8,128)} collective-permute-done((f32[2568,128]{1,0:T(8,128)S(1)}, f32[2568,128]{1,0:T(8,128)}, u32[]{:S(2)}, u32[]{:S(2)}) %collective-permute-start.9) | collective-permute-done | bytes 1314848 | tf_op jit(solution)/shard_map/ppermute | solution.py:47
  138.0 1.0 copy-done.1
  139.1 0.9 copy-done.3
  140.0 0.9 copy-done.5
  141.0 0.9 copy-done.7
  141.9 6.9 %last_steps.1 = f32[3072,128]{1,0:T(8,128)} custom-call(s32[2]{0:T(128)S(1)} %pad_add_fusion.place, s32[24]{0:T(128)S(1)} %bitcast.13, s32[24]{0:T(128)S(1)} %bitcast.15, f32[1040,128]{1,0:T(8,128)S(1)} %copy-done.1, f32[1040,128]{1,0:T(8,128)S(1)} %collective-permute-done.2.far, ...), custom_call_target="tpu_custom_call", output_to_operand_aliasing={{}: (12, {})} | custom-call | tf_op jit(solution)/shard_map/last_steps/pallas_call | solution.py:236
  (32 shorter events, 1.8 us)
Async XLA Ops:
  1.7 12.0 %copy-start.11 = (s32[1,1,20]{2,1,0:T(1,128)S(1)}, s32[1,1,20]{2,1,0:T(1,128)}, u32[]{:S(2)}) copy-start(s32[1,1,20]{2,1,0:T(1,128)} %param.16) | copy-start | bytes 244
  1.7 12.0 %copy-start.12 = (s32[1,1,20]{2,1,0:T(1,128)S(1)}, s32[1,1,20]{2,1,0:T(1,128)}, u32[]{:S(2)}) copy-start(s32[1,1,20]{2,1,0:T(1,128)} %param.15) | copy-start | bytes 244
  1.7 41.1 %copy-start.10 = (f32[1,1,20,128,128]{4,3,2,1,0:T(8,128)S(1)}, f32[1,1,20,128,128]{4,3,2,1,0:T(8,128)}, u32[]{:S(2)}) copy-start(f32[1,1,20,128,128]{4,3,2,1,0:T(8,128)} %param.14) | copy-start | bytes 3932164
  2.7 11.2 %collective-permute-start = (f32[520,128]{1,0:T(8,128)S(1)}, f32[520,128]{1,0:T(8,128)S(1)}, u32[]{:S(2)}, u32[]{:S(2)}) collective-permute-start(f32[520,128]{1,0:T(8,128)S(1)} %get-tuple-element.32), channel_id=1, source_target_pairs={{0,3},{1,2},{4,7},{5,6},{8,11},{9,10},{12,15},{13,14},{16,19},{17,... | collective-permute-start | bytes 798728 | tf_op jit(solution)/shard_map/ppermute | solution.py:47
  4.0 48.5 %collective-permute-start.2 = (f32[1040,128]{1,0:T(8,128)S(1)}, f32[1040,128]{1,0:T(8,128)S(1)}, u32[]{:S(2)}, u32[]{:S(2)}) collective-permute-start(f32[1040,128]{1,0:T(8,128)S(1)} %pad_maximum_fusion.left_hbm), channel_id=1, source_target_pairs={{2,0},{3,1},{6,4},{7,5},{10,8},{11,9},{14,12},{15,13},{18,16},{19,... | collective-permute-start | bytes 1597448 | tf_op jit(solution)/shard_map/ppermute | solution.py:47
  8.9 43.6 %collective-permute-start.1 = (f32[1040,128]{1,0:T(8,128)S(1)}, f32[1040,128]{1,0:T(8,128)S(1)}, u32[]{:S(2)}, u32[]{:S(2)}) collective-permute-start(f32[1040,128]{1,0:T(8,128)S(1)} %pad_maximum_fusion.left_hbm), channel_id=1, source_target_pairs={{1,0},{2,1},{3,2},{5,4},{6,5},{7,6},{9,8},{10,9},{11,10},{13,12},{... | collective-permute-start | bytes 1597448 | tf_op jit(solution)/shard_map/ppermute | solution.py:47
  11.8 37.7 %collective-permute-start.3 = (f32[520,128]{1,0:T(8,128)S(1)}, f32[520,128]{1,0:T(8,128)S(1)}, u32[]{:S(2)}, u32[]{:S(2)}) collective-permute-start(f32[520,128]{1,0:T(8,128)S(1)} %get-tuple-element.31), channel_id=1, source_target_pairs={{0,30},{1,31},{4,2},{5,3},{8,6},{9,7},{12,10},{13,11},{16,14},{17,... | collective-permute-start | bytes 798728 | tf_op jit(solution)/shard_map/ppermute | solution.py:47
  13.8 38.6 %collective-permute-start.4 = (f32[520,128]{1,0:T(8,128)S(1)}, f32[520,128]{1,0:T(8,128)S(1)}, u32[]{:S(2)}, u32[]{:S(2)}) collective-permute-start(f32[520,128]{1,0:T(8,128)S(1)} %collective-permute-done), channel_id=1, source_target_pairs={{2,31},{3,30},{6,3},{7,2},{10,7},{11,6},{14,11},{15,10},{18,15},{1... | collective-permute-start | bytes 798728 | tf_op jit(solution)/shard_map/ppermute | solution.py:47
  42.9 2.8 %copy-start.8 = (s32[1,1,24]{2,1,0:T(1,128)S(1)}, s32[1,1,24]{2,1,0:T(1,128)}, u32[]{:S(2)}) copy-start(s32[1,1,24]{2,1,0:T(1,128)} %param.18) | copy-start | bytes 292
  42.9 2.8 %copy-start.9 = (s32[1,1,24]{2,1,0:T(1,128)S(1)}, s32[1,1,24]{2,1,0:T(1,128)}, u32[]{:S(2)}) copy-start(s32[1,1,24]{2,1,0:T(1,128)} %param.19) | copy-start | bytes 292
  43.0 90.0 %collective-permute-start.5 = (f32[2568,128]{1,0:T(8,128)S(1)}, f32[2568,128]{1,0:T(8,128)S(1)}, u32[]{:S(2)}, u32[]{:S(2)}) collective-permute-start(f32[2568,128]{1,0:T(8,128)S(1)} %select_maximum_fusion.right_hbm), channel_id=1, source_target_pairs={{0,960},{1,961},{2,962},{3,963},{4,964},{5,965},{6,966},{7,967},{8... | collective-permute-start | bytes 3944456 | tf_op jit(solution)/shard_map/ppermute | solution.py:47
  52.5 0.8 copy-start
  53.3 79.7 %collective-permute-start.6 = (f32[2568,128]{1,0:T(8,128)S(1)}, f32[2568,128]{1,0:T(8,128)S(1)}, u32[]{:S(2)}, u32[]{:S(2)}) collective-permute-start(f32[2568,128]{1,0:T(8,128)S(1)} %select_maximum_fusion.right_hbm), channel_id=1, source_target_pairs={{32,0},{33,1},{34,2},{35,3},{36,4},{37,5},{38,6},{39,7},{40,8},{41... | collective-permute-start | bytes 3944456 | tf_op jit(solution)/shard_map/ppermute | solution.py:47
  57.0 70.3 %collective-permute-start.7 = (f32[520,128]{1,0:T(8,128)S(1)}, f32[520,128]{1,0:T(8,128)S(1)}, u32[]{:S(2)}, u32[]{:S(2)}) collective-permute-start(f32[520,128]{1,0:T(8,128)S(1)} %collective-permute-done.3.across_low), channel_id=1, source_target_pairs={{2,3},{6,7},{10,11},{14,15},{18,19},{22,23},{26,27},{30,31},{34,35... | collective-permute-start | bytes 798728 | tf_op jit(solution)/shard_map/ppermute | solution.py:47
  58.3 74.0 %collective-permute-start.8 = (f32[520,128]{1,0:T(8,128)S(1)}, f32[520,128]{1,0:T(8,128)S(1)}, u32[]{:S(2)}, u32[]{:S(2)}) collective-permute-start(f32[520,128]{1,0:T(8,128)S(1)} %collective-permute-done.4.across_high), channel_id=1, source_target_pairs={{2,3},{6,7},{10,11},{14,15},{18,19},{22,23},{26,27},{30,31},{34,35... | collective-permute-start | bytes 798728 | tf_op jit(solution)/shard_map/ppermute | solution.py:47
  59.6 0.7 copy-start.2
  127.3 0.7 copy-start.4
  132.3 0.7 copy-start.6
  133.0 5.1 %collective-permute-start.9 = (f32[2568,128]{1,0:T(8,128)S(1)}, f32[2568,128]{1,0:T(8,128)}, u32[]{:S(2)}, u32[]{:S(2)}) collective-permute-start(f32[2568,128]{1,0:T(8,128)S(1)} %collective-permute-done.5.right_next), channel_id=1, source_target_pairs={{0,32},{1,33},{2,34},{3,35},{4,36},{5,37},{6,38},{7,39},{8,40},{9,... | collective-permute-start | bytes 3944456 | tf_op jit(solution)/shard_map/ppermute | solution.py:47
  138.0 1.0 copy-start.1
  139.1 1.0 copy-start.3
  140.0 1.0 copy-start.5
  141.0 1.0 copy-start.7

commit v2 on v1

v2 whole, which is shorter than its diff:
```python
import functools

import jax
import jax.numpy as jnp
from jax import lax
from jax.experimental import pallas as pl
from jax.experimental.pallas import tpu as pltpu
from jax.sharding import PartitionSpec as P

BS = 128
MAXA = 8
MAXB = 20
CMAX = 24
ROWB = 8
INB = 32
COLB = 32
HALF = MAXA // 2 * BS
PAD = 8
LEFT_HALF = HALF + PAD
RIGHT_ROWS = MAXB * BS
N_ROW = 32
N_COL = 32
AXES = ("row", "col")

GROUP = 4
N_GROUP = N_COL // GROUP


def route(place):
    pairs = []
    for row in range(N_ROW):
        for col in range(N_COL):
            target = place(row, col // GROUP, col % GROUP)
            if target is not None:
                r, g, x = target
                pairs.append((row * N_COL + col, (r % N_ROW) * N_COL + (g % N_GROUP) * GROUP + x))
    return pairs


def along_x(moves):
    return route(lambda r, g, x: (r, g, moves[x]) if x in moves else None)


def to_previous_group(moves):
    return route(lambda r, g, x: (r, g - 1, moves[x]) if x in moves else None)


def send(block, pairs):
    return lax.ppermute(block, AXES, pairs)


def clear(table, size):
    def body(i, carry):
        table[i] = -1
        return carry

    lax.fori_loop(0, size, body, 0, unroll=8)


def mark_slots(out_rows, out_cols, slot_of):
    clear(slot_of, ROWB * COLB)
    for c in range(CMAX):
        slot_of[out_rows[c] * COLB + out_cols[c]] = c


def list_products(left_meta, right_meta, slot_of, by_inner, products, start):
    def left_int(i):
        return left_meta[0, i].astype(jnp.int32)

    def right_int(i):
        return right_meta[0, i].astype(jnp.int32)

    left_count = left_int(2 * MAXA)
    right_count = right_int(2 * MAXB)
    clear(by_inner, 2 * INB)
    for b in range(MAXB):
        place = jnp.where(b < right_count, right_int(b) * 2, 2 * INB)
        taken = (by_inner[place] >= 0) & (b < right_count)
        by_inner[place + taken.astype(jnp.int32)] = b
    count = start
    for a in range(MAXA):
        row, inner = left_int(a), left_int(MAXA + a)
        for m in range(2):
            b = by_inner[inner * 2 + m]
            column = right_int(MAXB + jnp.maximum(b, 0))
            c = slot_of[row * COLB + column]
            products[count] = (a * 32 + b) * 32 + c
            valid = (a < left_count) & (b >= 0) & (c >= 0)
            count = count + valid.astype(jnp.int32)
    return count


def split(value):
    high = value.astype(jnp.bfloat16)
    low = (value - high.astype(jnp.float32)).astype(jnp.bfloat16)
    return high, low


def step_kernel(picks, n_left, n_right, first, *refs):
    sides, out_rows, out_cols = refs[:3]
    lefts = refs[3 : 3 + n_left]
    rights = refs[3 + n_left : 3 + n_left + n_right]
    (total, left_tile, right_tile, left_meta, right_meta, slot_of, by_inner, products, sems) = refs[-9:]
    other_left, other_right = sides[0] == 1, sides[1] == 1

    def left_at(pick, sem):
        return pltpu.make_async_copy(lefts[pick[0]].at[pl.ds(pick[1] + HALF, PAD)], left_meta, sem)

    def right_at(ref, sem):
        return pltpu.make_async_copy(ref.at[pl.ds(RIGHT_ROWS, PAD)], right_meta, sem)

    def either(condition, same, no, yes):
        if same:
            no()
        else:
            pl.when(condition)(yes)
            pl.when(jnp.logical_not(condition))(no)

    either(
        other_left,
        picks[0][0] == picks[1][0],
        lambda: left_at(picks[0][0], sems.at[0]).start(),
        lambda: left_at(picks[1][0], sems.at[0]).start(),
    )
    either(
        other_right,
        n_right == 1,
        lambda: right_at(rights[0], sems.at[1]).start(),
        lambda: right_at(rights[-1], sems.at[1]).start(),
    )
    mark_slots(out_rows, out_cols, slot_of)
    total[...] = jnp.zeros_like(total) if first else refs[3 + n_left + n_right][...]
    left_at(picks[0][0], sems.at[0]).wait()
    right_at(rights[0], sems.at[1]).wait()
    count = list_products(left_meta, right_meta, slot_of, by_inner, products, 0)

    def copy_tile(tile, ref, start):
        tile[...] = ref[pl.ds(pl.multiple_of(start, 8), BS), :]

    def copy_half(pick, start):
        copy_tile(left_tile, lefts[pick[0]], pick[1] + start)

    def body(i, carry):
        code = products[i]
        a = code // 1024
        b = (code // 32) % 32
        c = code % 32
        upper = a // (MAXA // 2)
        at = (a % (MAXA // 2)) * BS
        for half in range(2):

            @pl.when(upper == half)
            def _():
                one, other = picks[0][half], picks[1][half]
                either(other_left, one == other, lambda: copy_half(one, at), lambda: copy_half(other, at))

        either(
            other_right,
            n_right == 1,
            lambda: copy_tile(right_tile, rights[0], b * BS),
            lambda: copy_tile(right_tile, rights[-1], b * BS),
        )
        left_high_part, left_low_part = split(left_tile[...])
        right_high_part, right_low_part = split(right_tile[...])
        lhs = jnp.concatenate([left_high_part, left_low_part], axis=1)
        both = jnp.concatenate([right_high_part, right_low_part], axis=1)
        rhs = jnp.concatenate([both, both], axis=0)
        pair = jnp.dot(lhs, rhs, preferred_element_type=jnp.float32)
        place = pl.ds(pl.multiple_of(c * BS, BS), BS)
        total[place, :] = total[place, :] + (pair[:, :BS] + pair[:, BS:])
        return carry

    lax.fori_loop(0, count, body, 0)


WHOLE = ((0, 0), (0, LEFT_HALF))
SMEM_SPEC = pl.BlockSpec(memory_space=pltpu.SMEM)
VMEM_SPEC = pl.BlockSpec(memory_space=pltpu.VMEM)


def step_call(name, sides, out_rows, out_cols, lefts, picks, rights, before=None):
    operands = [sides, out_rows, out_cols, *lefts, *rights] + ([] if before is None else [before])
    return pl.pallas_call(
        functools.partial(step_kernel, picks, len(lefts), len(rights), before is None),
        out_shape=jax.ShapeDtypeStruct((CMAX * BS, BS), jnp.float32),
        in_specs=[SMEM_SPEC] * 3 + [VMEM_SPEC] * (len(operands) - 3),
        out_specs=VMEM_SPEC,
        input_output_aliases={} if before is None else {len(operands) - 1: 0},
        scratch_shapes=[
            pltpu.VMEM((BS, BS), jnp.float32),
            pltpu.VMEM((BS, BS), jnp.float32),
            pltpu.SMEM((PAD, BS), jnp.float32),
            pltpu.SMEM((PAD, BS), jnp.float32),
            pltpu.SMEM((ROWB * COLB,), jnp.int32),
            pltpu.SMEM((2 * INB + 8,), jnp.int32),
            pltpu.SMEM((32,), jnp.int32),
            pltpu.SemaphoreType.DMA((2,)),
        ],
        compiler_params=pltpu.CompilerParams(vmem_limit_bytes=24 * 2**20),
        cost_estimate=pl.CostEstimate(flops=10**10 if before is None else 10**8, bytes_accessed=10**6, transcendentals=0),
        name=name,
    )(*operands)


def meta_rows(*parts):
    line = jnp.concatenate(parts).astype(jnp.float32)
    return jnp.pad(line[None], ((0, PAD - 1), (0, BS - line.shape[0])))


def shards(
    left_blocks,
    left_rows,
    left_cols,
    left_count,
    right_blocks,
    right_rows,
    right_cols,
    right_count,
    out_rows,
    out_cols,
):
    left_meta = meta_rows(left_rows[0, 0], left_cols[0, 0], left_count[0])
    right_meta = meta_rows(right_rows[0, 0], right_cols[0, 0], right_count[0])
    blocks = left_blocks.reshape(MAXA * BS, BS)
    low = jnp.concatenate([blocks[:HALF], left_meta])
    high = jnp.concatenate([blocks[HALF:], left_meta])
    left = jnp.concatenate([low, high])
    right = jnp.concatenate([right_blocks.reshape(RIGHT_ROWS, BS), right_meta])
    x = lax.axis_index("col") % GROUP
    row = lax.axis_index("row")
    core = row % 2
    last_chip = (row // 2 == N_ROW // 2 - 1).astype(jnp.int32)
    rows, cols = out_rows[0, 0], out_cols[0, 0]

    right_near = send(right, route(lambda r, g, x: (r - 2, g, x) if r >= 2 else None))
    high_far = send(high, along_x({0: 3, 1: 2, 2: 0, 3: 1}))
    low_far = send(low, route(lambda r, g, x: (r, g - 1, x + 2) if x < 2 else (r, g, x - 2)))
    near = send(left, along_x({1: 0, 2: 1, 3: 2}))
    across_high = send(high_far, to_previous_group({3: 2, 2: 3}))
    left, right, high_far = lax.optimization_barrier((left, right, high_far))
    right_wrap = send(right, route(lambda r, g, x: (r - 2, g, x) if r < 2 else None))
    total = step_call("step_0", jnp.zeros((2,), jnp.int32), rows, cols, [left], (WHOLE, WHOLE), [right])
    right, near, total, low_far = lax.optimization_barrier((right, near, total, low_far))
    across_high, total = lax.optimization_barrier((across_high, total))
    over_low = send(low_far, along_x({2: 3}))
    over_high = send(across_high, along_x({2: 3}))

    right_one = send(
        lax.select(core == 1, right, right_near),
        route(lambda r, g, x: (r ^ 1, g, x)),
    )
    right_wrap, over_low, over_high = lax.optimization_barrier((right_wrap, over_low, over_high))
    edge = send(right_wrap, route(lambda r, g, x: (r + 1, g, x) if r == N_ROW - 2 else None))
    total = step_call(
        "step_2",
        jnp.stack([(x >= 2).astype(jnp.int32), last_chip]),
        rows,
        cols,
        [low_far, high_far, across_high],
        (((0, 0), (1, 0)), ((0, 0), (2, 0))),
        [right_near, right_wrap],
        total,
    )
    total = step_call(
        "step_1",
        jnp.stack([(x == 3).astype(jnp.int32), last_chip * core]),
        rows,
        cols,
        [near, over_low, over_high],
        (WHOLE, ((1, 0), (2, 0))),
        [right_one, edge],
        total,
    )
    return total.reshape(1, 1, CMAX, BS, BS)


def solution(mesh):
    in_specs = (
        P("row", "col", None, None, None),
        P("row", "col", None),
        P("row", "col", None),
        P("row", "col"),
        P("row", "col", None, None, None),
        P("row", "col", None),
        P("row", "col", None),
        P("row", "col"),
        P("row", "col", None),
        P("row", "col", None),
    )
    out_specs = P("row", "col", None, None, None)
    return jax.shard_map(shards, mesh=mesh, in_specs=in_specs, out_specs=out_specs, check_vma=False)
```

time: 149 us -> 165 us (1.11)
  the two profiles are of different devices: /device:TPU:71 before, /device:TPU:6 now
where the time goes in v2:
time: 165 us
  waiting for transfers between devices  69.6 us (42%)
  starting transfers between devices  69 us (42%)
  Pallas kernels  17 us (10%)
  other arithmetic  5.33 us (3%)
  local copies, waits for them, and re-layouts  2.45 us (1%)
    ppermute x10, waiting for transfers between devices, send(): return lax.ppermute(block, AXES, pairs)  69.6 us
    ppermute x10, starting transfers between devices, send(): return lax.ppermute(block, AXES, pairs)  69 us
    pallas_call x3, Pallas kernels, step_call(): pl.pallas_call(functools.partial(step_kernel, picks, len(lefts), len(righ...  17 us
  transfers between devices with their start and end apart: 10, of which 3 were waited for; matrix products, arithmetic and copies ran while one was open for 2% of the time, Pallas kernels for 6%

profile of v2, /device:TPU:6, one launch (start us, length us, event | category | flops | bytes accessed | tf_op | source)
XLA Modules:
  0.0 164.9 jit_solution(17176265885775179533)
XLA Ops:
  0.7 0.8 add_convert_fusion.2
  1.5 1.4 select_maximum_fusion.refs_4_
  2.9 1.3 collective-permute-start.7
  5.1 0.8 pad_maximum_fusion.1
  5.9 3.3 %collective-permute-start = (f32[520,128]{1,0:T(8,128)}, f32[520,128]{1,0:T(8,128)S(1)}, u32[]{:S(2)}, u32[]{:S(2)}) collective-permute-start(f32[520,128]{1,0:T(8,128)} %get-tuple-element.32), channel_id=1, source_target_pairs={{0,3},{1,2},{2,0},{3,1},{4,7},{5,6},{6,4},{7,5},{8,11},{9,10},{10,... | collective-permute-start | bytes 798728 | tf_op jit(solution)/shard_map/ppermute | solution.py:49
  9.2 3.4 %collective-permute-start.2 = (f32[520,128]{1,0:T(8,128)}, f32[520,128]{1,0:T(8,128)}, u32[]{:S(2)}, u32[]{:S(2)}) collective-permute-start(f32[520,128]{1,0:T(8,128)} %get-tuple-element.31), channel_id=1, source_target_pairs={{0,30},{1,31},{2,0},{3,1},{4,2},{5,3},{6,4},{7,5},{8,6},{9,7},{10,... | collective-permute-start | bytes 798728 | tf_op jit(solution)/shard_map/ppermute | solution.py:49
  12.6 0.8 pad_maximum_fusion.refs_3_
  13.4 13.0 %collective-permute-start.1 = (f32[1040,128]{1,0:T(8,128)}, f32[1040,128]{1,0:T(8,128)S(1)}, u32[]{:S(2)}, u32[]{:S(2)}) collective-permute-start(f32[1040,128]{1,0:T(8,128)} %pad_maximum_fusion.refs_3_), channel_id=1, source_target_pairs={{1,0},{2,1},{3,2},{5,4},{6,5},{7,6},{9,8},{10,9},{11,10},{13,12},{... | collective-permute-start | bytes 1597448 | tf_op jit(solution)/shard_map/ppermute | solution.py:49
  26.5 18.8 %collective-permute-start.3 = (f32[2568,128]{1,0:T(8,128)S(1)}, f32[2568,128]{1,0:T(8,128)}, u32[]{:S(2)}, u32[]{:S(2)}) collective-permute-start(f32[2568,128]{1,0:T(8,128)S(1)} %select_maximum_fusion.refs_4_), channel_id=1, source_target_pairs={{0,960},{1,961},{2,962},{3,963},{4,964},{5,965},{6,966},{7,967},{8... | collective-permute-start | bytes 3944456 | tf_op jit(solution)/shard_map/ppermute | solution.py:49
  45.3 23.9 %collective-permute-start.5 = (f32[520,128]{1,0:T(8,128)S(1)}, f32[520,128]{1,0:T(8,128)S(1)}, u32[]{:S(2)}, u32[]{:S(2)}) collective-permute-start(f32[520,128]{1,0:T(8,128)S(1)} %collective-permute-done.refs_4_), channel_id=1, source_target_pairs={{2,31},{3,30},{6,3},{7,2},{10,7},{11,6},{14,11},{15,10},{18,15},{1... | collective-permute-start | bytes 798728 | tf_op jit(solution)/shard_map/ppermute | solution.py:49
  69.3 4.0 %step_0.1.refs_8_ = f32[3072,128]{1,0:T(8,128)} custom-call(s32[2]{0:T(128)S(1)} %broadcast_1_refs_0_.2.refs_0_, s32[24]{0:T(128)S(1)} %bitcast.14, s32[24]{0:T(128)S(1)} %bitcast.17, f32[1040,128]{1,0:T(8,128)} %pad_maximum_fusion.refs_3_, f32[2568,128]{1,0:T(8,128)S(1)} %select_maximum_fusion.refs_4_), custom_call_target="tpu_custom_call" | custom-call | flops 10000000000 | bytes 1000000 | tf_op jit(solution)/shard_map/step_0/pallas_call | solution.py:183
  73.3 60.2 %collective-permute-done.5.refs_5_ = f32[520,128]{1,0:T(8,128)S(1)} collective-permute-done((f32[520,128]{1,0:T(8,128)S(1)}, f32[520,128]{1,0:T(8,128)S(1)}, u32[]{:S(2)}, u32[]{:S(2)}) %collective-permute-start.5) | collective-permute-done | bytes 266272 | tf_op jit(solution)/shard_map/ppermute | solution.py:49
  133.6 1.3 collective-permute-start.6
  134.9 1.3 collective-permute-start.4
  136.2 1.2 broadcast_select_fusion
  137.4 1.9 %collective-permute-start.8 = (f32[2568,128]{1,0:T(8,128)}, f32[2568,128]{1,0:T(8,128)}, u32[]{:S(2)}, u32[]{:S(2)}) collective-permute-start(f32[2568,128]{1,0:T(8,128)} %broadcast_select_fusion), channel_id=1, source_target_pairs={{0,32},{1,33},{2,34},{3,35},{4,36},{5,37},{6,38},{7,39},{8,40},{9,... | collective-permute-start | bytes 3944456 | tf_op jit(solution)/shard_map/ppermute | solution.py:49
  139.3 5.4 %collective-permute-done.6.refs_5_ = f32[520,128]{1,0:T(8,128)S(1)} collective-permute-done((f32[520,128]{1,0:T(8,128)S(1)}, f32[520,128]{1,0:T(8,128)S(1)}, u32[]{:S(2)}, u32[]{:S(2)}) %collective-permute-start.6) | collective-permute-done | bytes 266272 | tf_op jit(solution)/shard_map/ppermute | solution.py:49
  144.7 0.7 copy-done.2
  145.4 3.9 %collective-permute-done.4.refs_4_ = f32[520,128]{1,0:T(8,128)S(1)} collective-permute-done((f32[520,128]{1,0:T(8,128)}, f32[520,128]{1,0:T(8,128)S(1)}, u32[]{:S(2)}, u32[]{:S(2)}) %collective-permute-start.4) | collective-permute-done | bytes 266272 | tf_op jit(solution)/shard_map/ppermute | solution.py:49
  149.3 0.7 copy-done.4
  150.0 0.7 collective-permute-start.9
  151.0 0.9 copy-done.1
  151.9 6.2 %step_2.1.refs_8_ = f32[3072,128]{1,0:T(8,128)} custom-call(s32[2]{0:T(128)S(1)} %add_convert_fusion.refs_0_, s32[24]{0:T(128)S(1)} %bitcast.15, s32[24]{0:T(128)S(1)} %bitcast.18, f32[520,128]{1,0:T(8,128)} %collective-permute-done.2.refs_3_, f32[520,128]{1,0:T(8,128)S(1)} %collective-permute-done.refs_4_, ...), custom_call_target="tpu_custom_call", output_to_operand_aliasing={{}: (8, {})} | custom-call | flops 100000000 | bytes 1000000 | tf_op jit(solution)/shard_map/step_2/pallas_call | solution.py:183
  158.1 6.8 %step_1.1 = f32[3072,128]{1,0:T(8,128)} custom-call(s32[2]{0:T(128)S(1)} %pad_add_fusion.refs_0_, s32[24]{0:T(128)S(1)} %bitcast.16, s32[24]{0:T(128)S(1)} %bitcast.19, f32[1040,128]{1,0:T(8,128)S(1)} %collective-permute-done.1.refs_3_, f32[520,128]{1,0:T(8,128)S(1)} %copy-done.5, f32[520,128]{1,0:T(8,128)S(1)} %copy-done.3, ...), custom_call_target="tpu_custom_call", output_to_operand_aliasing={{}: (8, {})} | custom-call | flops 100000000 | bytes 1000000 | tf_op jit(solution)/shard_map/step_1/pallas_call | solution.py:183
  (32 shorter events, 0.3 us)
Async XLA Ops:
  0.7 3.6 %copy-start.8 = (f32[1,1,8,128,128]{4,3,2,1,0:T(8,128)S(1)}, f32[1,1,8,128,128]{4,3,2,1,0:T(8,128)}, u32[]{:S(2)}) copy-start(f32[1,1,8,128,128]{4,3,2,1,0:T(8,128)} %param.10) | copy-start | bytes 1572868
  1.5 3.5 %copy-start.9 = (s32[1,1,8]{2,1,0:T(1,128)S(1)}, s32[1,1,8]{2,1,0:T(1,128)}, u32[]{:S(2)}) copy-start(s32[1,1,8]{2,1,0:T(1,128)} %param.12) | copy-start | bytes 100
  1.5 3.5 %copy-start.10 = (s32[1,1,8]{2,1,0:T(1,128)S(1)}, s32[1,1,8]{2,1,0:T(1,128)}, u32[]{:S(2)}) copy-start(s32[1,1,8]{2,1,0:T(1,128)} %param.11) | copy-start | bytes 100
  2.9 133.3 %collective-permute-start.7 = (f32[2568,128]{1,0:T(8,128)S(1)}, f32[2568,128]{1,0:T(8,128)S(1)}, u32[]{:S(2)}, u32[]{:S(2)}) collective-permute-start(f32[2568,128]{1,0:T(8,128)S(1)} %select_maximum_fusion.refs_4_), channel_id=1, source_target_pairs={{64,0},{65,1},{66,2},{67,3},{68,4},{69,5},{70,6},{71,7},{72,8},{73... | collective-permute-start | bytes 3944456 | tf_op jit(solution)/shard_map/ppermute | solution.py:49
  4.3 65.0 %copy-start.6 = (s32[1,1,24]{2,1,0:T(1,128)S(1)}, s32[1,1,24]{2,1,0:T(1,128)}, u32[]{:S(2)}) copy-start(s32[1,1,24]{2,1,0:T(1,128)} %param.18) | copy-start | bytes 292
  4.3 65.0 %copy-start.7 = (s32[1,1,24]{2,1,0:T(1,128)S(1)}, s32[1,1,24]{2,1,0:T(1,128)}, u32[]{:S(2)}) copy-start(s32[1,1,24]{2,1,0:T(1,128)} %param.19) | copy-start | bytes 292
  5.9 20.6 %collective-permute-start = (f32[520,128]{1,0:T(8,128)}, f32[520,128]{1,0:T(8,128)S(1)}, u32[]{:S(2)}, u32[]{:S(2)}) collective-permute-start(f32[520,128]{1,0:T(8,128)} %get-tuple-element.32), channel_id=1, source_target_pairs={{0,3},{1,2},{2,0},{3,1},{4,7},{5,6},{6,4},{7,5},{8,11},{9,10},{10,... | collective-permute-start | bytes 798728 | tf_op jit(solution)/shard_map/ppermute | solution.py:49
  9.2 64.1 %collective-permute-start.2 = (f32[520,128]{1,0:T(8,128)}, f32[520,128]{1,0:T(8,128)}, u32[]{:S(2)}, u32[]{:S(2)}) collective-permute-start(f32[520,128]{1,0:T(8,128)} %get-tuple-element.31), channel_id=1, source_target_pairs={{0,30},{1,31},{2,0},{3,1},{4,2},{5,3},{6,4},{7,5},{8,6},{9,7},{10,... | collective-permute-start | bytes 798728 | tf_op jit(solution)/shard_map/ppermute | solution.py:49
  13.4 59.9 %collective-permute-start.1 = (f32[1040,128]{1,0:T(8,128)}, f32[1040,128]{1,0:T(8,128)S(1)}, u32[]{:S(2)}, u32[]{:S(2)}) collective-permute-start(f32[1040,128]{1,0:T(8,128)} %pad_maximum_fusion.refs_3_), channel_id=1, source_target_pairs={{1,0},{2,1},{3,2},{5,4},{6,5},{7,6},{9,8},{10,9},{11,10},{13,12},{... | collective-permute-start | bytes 1597448 | tf_op jit(solution)/shard_map/ppermute | solution.py:49
  26.5 123.5 %collective-permute-start.3 = (f32[2568,128]{1,0:T(8,128)S(1)}, f32[2568,128]{1,0:T(8,128)}, u32[]{:S(2)}, u32[]{:S(2)}) collective-permute-start(f32[2568,128]{1,0:T(8,128)S(1)} %select_maximum_fusion.refs_4_), channel_id=1, source_target_pairs={{0,960},{1,961},{2,962},{3,963},{4,964},{5,965},{6,966},{7,967},{8... | collective-permute-start | bytes 3944456 | tf_op jit(solution)/shard_map/ppermute | solution.py:49
  45.3 88.2 %collective-permute-start.5 = (f32[520,128]{1,0:T(8,128)S(1)}, f32[520,128]{1,0:T(8,128)S(1)}, u32[]{:S(2)}, u32[]{:S(2)}) collective-permute-start(f32[520,128]{1,0:T(8,128)S(1)} %collective-permute-done.refs_4_), channel_id=1, source_target_pairs={{2,31},{3,30},{6,3},{7,2},{10,7},{11,6},{14,11},{15,10},{18,15},{1... | collective-permute-start | bytes 798728 | tf_op jit(solution)/shard_map/ppermute | solution.py:49
  133.6 3.8 %copy-start = (f32[520,128]{1,0:T(8,128)}, f32[520,128]{1,0:T(8,128)S(1)}, u32[]{:S(2)}) copy-start(f32[520,128]{1,0:T(8,128)S(1)} %collective-permute-done.5.refs_5_) | copy-start | bytes 798724
  133.6 11.2 %collective-permute-start.6 = (f32[520,128]{1,0:T(8,128)S(1)}, f32[520,128]{1,0:T(8,128)S(1)}, u32[]{:S(2)}, u32[]{:S(2)}) collective-permute-start(f32[520,128]{1,0:T(8,128)S(1)} %collective-permute-done.5.refs_5_), channel_id=1, source_target_pairs={{2,3},{6,7},{10,11},{14,15},{18,19},{22,23},{26,27},{30,31},{34,35... | collective-permute-start | bytes 798728 | tf_op jit(solution)/shard_map/ppermute | solution.py:49
  134.9 14.4 %collective-permute-start.4 = (f32[520,128]{1,0:T(8,128)}, f32[520,128]{1,0:T(8,128)S(1)}, u32[]{:S(2)}, u32[]{:S(2)}) collective-permute-start(f32[520,128]{1,0:T(8,128)} %collective-permute-done.2.refs_3_), channel_id=1, source_target_pairs={{2,3},{6,7},{10,11},{14,15},{18,19},{22,23},{26,27},{30,31},{34,35... | collective-permute-start | bytes 798728 | tf_op jit(solution)/shard_map/ppermute | solution.py:49
  137.4 20.7 %collective-permute-start.8 = (f32[2568,128]{1,0:T(8,128)}, f32[2568,128]{1,0:T(8,128)}, u32[]{:S(2)}, u32[]{:S(2)}) collective-permute-start(f32[2568,128]{1,0:T(8,128)} %broadcast_select_fusion), channel_id=1, source_target_pairs={{0,32},{1,33},{2,34},{3,35},{4,36},{5,37},{6,38},{7,39},{8,40},{9,... | collective-permute-start | bytes 3944456 | tf_op jit(solution)/shard_map/ppermute | solution.py:49
  144.7 0.7 copy-start.2
  149.3 0.7 copy-start.4
  150.0 8.1 %collective-permute-start.9 = (f32[2568,128]{1,0:T(8,128)}, f32[2568,128]{1,0:T(8,128)S(1)}, u32[]{:S(2)}, u32[]{:S(2)}) collective-permute-start(f32[2568,128]{1,0:T(8,128)} %collective-permute-done.3.refs_7_), channel_id=1, source_target_pairs={{960,992},{961,993},{962,994},{963,995},{964,996},{965,997},{966,9... | collective-permute-start | bytes 3944456 | tf_op jit(solution)/shard_map/ppermute | solution.py:49
  151.0 1.0 copy-start.1
  151.9 6.2 %copy-start.3 = (f32[520,128]{1,0:T(8,128)S(1)}, f32[520,128]{1,0:T(8,128)}, u32[]{:S(2)}) copy-start(f32[520,128]{1,0:T(8,128)} %copy-done.2) | copy-start | bytes 798724
  151.9 6.2 %copy-start.5 = (f32[520,128]{1,0:T(8,128)S(1)}, f32[520,128]{1,0:T(8,128)}, u32[]{:S(2)}) copy-start(f32[520,128]{1,0:T(8,128)} %copy-done.4) | copy-start | bytes 798724

commit v3 on v2

--- a/solution.py
+++ b/solution.py
@@ -178,7 +178,7 @@
 VMEM_SPEC = pl.BlockSpec(memory_space=pltpu.VMEM)
 
 
-def step_call(name, sides, out_rows, out_cols, lefts, picks, rights, before=None):
+def step_call(name, sides, out_rows, out_cols, lefts, picks, rights, before=None, flops=10**8):
     operands = [sides, out_rows, out_cols, *lefts, *rights] + ([] if before is None else [before])
     return pl.pallas_call(
         functools.partial(step_kernel, picks, len(lefts), len(rights), before is None),
@@ -197,7 +197,7 @@
             pltpu.SemaphoreType.DMA((2,)),
         ],
         compiler_params=pltpu.CompilerParams(vmem_limit_bytes=24 * 2**20),
-        cost_estimate=pl.CostEstimate(flops=10**10 if before is None else 10**8, bytes_accessed=10**6, transcendentals=0),
+        cost_estimate=pl.CostEstimate(flops=flops, bytes_accessed=10**6, transcendentals=0),
         name=name,
     )(*operands)
 
@@ -232,24 +232,24 @@
     last_chip = (row // 2 == N_ROW // 2 - 1).astype(jnp.int32)
     rows, cols = out_rows[0, 0], out_cols[0, 0]
 
+    high_far = send(high, along_x({0: 3, 1: 2, 2: 0, 3: 1}))
     right_near = send(right, route(lambda r, g, x: (r - 2, g, x) if r >= 2 else None))
-    high_far = send(high, along_x({0: 3, 1: 2, 2: 0, 3: 1}))
+    near = send(left, along_x({1: 0, 2: 1, 3: 2}))
     low_far = send(low, route(lambda r, g, x: (r, g - 1, x + 2) if x < 2 else (r, g, x - 2)))
-    near = send(left, along_x({1: 0, 2: 1, 3: 2}))
     across_high = send(high_far, to_previous_group({3: 2, 2: 3}))
     left, right, high_far = lax.optimization_barrier((left, right, high_far))
     right_wrap = send(right, route(lambda r, g, x: (r - 2, g, x) if r < 2 else None))
-    total = step_call("step_0", jnp.zeros((2,), jnp.int32), rows, cols, [left], (WHOLE, WHOLE), [right])
-    right, near, total, low_far = lax.optimization_barrier((right, near, total, low_far))
-    across_high, total = lax.optimization_barrier((across_high, total))
+    near, low_far = lax.optimization_barrier((near, low_far))
     over_low = send(low_far, along_x({2: 3}))
+    left, across_high, low_far = lax.optimization_barrier((left, across_high, low_far))
     over_high = send(across_high, along_x({2: 3}))
-
+    total = step_call("step_0", jnp.zeros((2,), jnp.int32), rows, cols, [left], (WHOLE, WHOLE), [right], flops=10000000000)
+    right_near, total = lax.optimization_barrier((right_near, total))
     right_one = send(
         lax.select(core == 1, right, right_near),
         route(lambda r, g, x: (r ^ 1, g, x)),
     )
-    right_wrap, over_low, over_high = lax.optimization_barrier((right_wrap, over_low, over_high))
+    right_wrap, over_low, over_high, total = lax.optimization_barrier((right_wrap, over_low, over_high, total))
     edge = send(right_wrap, route(lambda r, g, x: (r + 1, g, x) if r == N_ROW - 2 else None))
     total = step_call(
         "step_2",

time: 165 us -> 146 us (0.88)
  the two profiles are of different devices: /device:TPU:6 before, /device:TPU:645 now
where the time goes in v3:
time: 146 us
  waiting for transfers between devices  65.8 us (45%)
  starting transfers between devices  54.3 us (37%)
  Pallas kernels  17.7 us (12%)
  other arithmetic  3.95 us (3%)
  local copies, waits for them, and re-layouts  2.51 us (2%)
  between operations  1.59 us (1%)
    ppermute x10, waiting for transfers between devices, send(): return lax.ppermute(block, AXES, pairs)  65.8 us
    ppermute x10, starting transfers between devices, send(): return lax.ppermute(block, AXES, pairs)  54.3 us
    pallas_call x3, Pallas kernels, step_call(): pl.pallas_call(functools.partial(step_kernel, picks, len(lefts), len(righ...  17.7 us
  transfers between devices with their start and end apart: 10, of which 2 were waited for; matrix products, arithmetic and copies ran while one was open for 2% of the time, Pallas kernels for 8%

profile of v3, /device:TPU:645, one launch (start us, length us, event | category | flops | bytes accessed | tf_op | source)
XLA Modules:
  0.0 145.9 jit_solution(1028265324812525525)
XLA Ops:
  0.7 1.1 fusion
  1.8 0.9 add_convert_fusion.1
  2.6 0.7 pad_maximum_fusion.1
  3.4 2.1 %collective-permute-start.2 = (f32[520,128]{1,0:T(8,128)S(1)}, f32[520,128]{1,0:T(8,128)S(1)}, u32[]{:S(2)}, u32[]{:S(2)}) collective-permute-start(f32[520,128]{1,0:T(8,128)S(1)} %get-tuple-element.35), channel_id=1, source_target_pairs={{0,3},{1,2},{2,0},{3,1},{4,7},{5,6},{6,4},{7,5},{8,11},{9,10},{10,... | collective-permute-start | bytes 798728 | tf_op jit(solution)/shard_map/ppermute | solution.py:49
  5.5 0.8 pad_maximum_fusion.refs_3_
  6.3 3.1 %collective-permute-start = (f32[1040,128]{1,0:T(8,128)}, f32[1040,128]{1,0:T(8,128)S(1)}, u32[]{:S(2)}, u32[]{:S(2)}) collective-permute-start(f32[1040,128]{1,0:T(8,128)} %pad_maximum_fusion.refs_3_), channel_id=1, source_target_pairs={{1,0},{2,1},{3,2},{5,4},{6,5},{7,6},{9,8},{10,9},{11,10},{13,12},{... | collective-permute-start | bytes 1597448 | tf_op jit(solution)/shard_map/ppermute | solution.py:49
  10.1 0.1 add_convert_fusion.2
  10.2 0.1 select_maximum_fusion.refs_4_
  10.3 3.8 %collective-permute-start.7 = (f32[2568,128]{1,0:T(8,128)S(1)}, f32[2568,128]{1,0:T(8,128)S(1)}, u32[]{:S(2)}, u32[]{:S(2)}) collective-permute-start(f32[2568,128]{1,0:T(8,128)S(1)} %select_maximum_fusion.refs_4_), channel_id=1, source_target_pairs={{64,0},{65,1},{66,2},{67,3},{68,4},{69,5},{70,6},{71,7},{72,8},{73... | collective-permute-start | bytes 3944456 | tf_op jit(solution)/shard_map/ppermute | solution.py:49
  14.2 2.5 %collective-permute-start.1 = (f32[520,128]{1,0:T(8,128)}, f32[520,128]{1,0:T(8,128)}, u32[]{:S(2)}, u32[]{:S(2)}) collective-permute-start(f32[520,128]{1,0:T(8,128)} %get-tuple-element.36), channel_id=1, source_target_pairs={{0,30},{1,31},{2,0},{3,1},{4,2},{5,3},{6,4},{7,5},{8,6},{9,7},{10,... | collective-permute-start | bytes 798728 | tf_op jit(solution)/shard_map/ppermute | solution.py:49
  16.7 1.9 %collective-permute-start.5 = (f32[520,128]{1,0:T(8,128)S(1)}, f32[520,128]{1,0:T(8,128)}, u32[]{:S(2)}, u32[]{:S(2)}) collective-permute-start(f32[520,128]{1,0:T(8,128)S(1)} %collective-permute-done.2.refs_4_), channel_id=1, source_target_pairs={{2,31},{3,30},{6,3},{7,2},{10,7},{11,6},{14,11},{15,10},{18,15},{1... | collective-permute-start | bytes 798728 | tf_op jit(solution)/shard_map/ppermute | solution.py:49
  18.7 1.7 %collective-permute-start.3 = (f32[2568,128]{1,0:T(8,128)S(1)}, f32[2568,128]{1,0:T(8,128)}, u32[]{:S(2)}, u32[]{:S(2)}) collective-permute-start(f32[2568,128]{1,0:T(8,128)S(1)} %select_maximum_fusion.refs_4_), channel_id=1, source_target_pairs={{0,960},{1,961},{2,962},{3,963},{4,964},{5,965},{6,966},{7,967},{8... | collective-permute-start | bytes 3944456 | tf_op jit(solution)/shard_map/ppermute | solution.py:49
  20.4 47.7 %collective-permute-done.1.refs_3_ = f32[520,128]{1,0:T(8,128)} collective-permute-done((f32[520,128]{1,0:T(8,128)}, f32[520,128]{1,0:T(8,128)}, u32[]{:S(2)}, u32[]{:S(2)}) %collective-permute-start.1) | collective-permute-done | bytes 266272 | tf_op jit(solution)/shard_map/ppermute | solution.py:49
  68.1 8.2 %collective-permute-start.4 = (f32[520,128]{1,0:T(8,128)}, f32[520,128]{1,0:T(8,128)S(1)}, u32[]{:S(2)}, u32[]{:S(2)}) collective-permute-start(f32[520,128]{1,0:T(8,128)} %collective-permute-done.1.refs_3_), channel_id=1, source_target_pairs={{2,3},{6,7},{10,11},{14,15},{18,19},{22,23},{26,27},{30,31},{34,35... | collective-permute-start | bytes 798728 | tf_op jit(solution)/shard_map/ppermute | solution.py:49
  76.3 18.1 %collective-permute-done.5.refs_5_ = f32[520,128]{1,0:T(8,128)} collective-permute-done((f32[520,128]{1,0:T(8,128)S(1)}, f32[520,128]{1,0:T(8,128)}, u32[]{:S(2)}, u32[]{:S(2)}) %collective-permute-start.5) | collective-permute-done | bytes 266272 | tf_op jit(solution)/shard_map/ppermute | solution.py:49
  94.4 25.8 %collective-permute-start.6 = (f32[520,128]{1,0:T(8,128)}, f32[520,128]{1,0:T(8,128)S(1)}, u32[]{:S(2)}, u32[]{:S(2)}) collective-permute-start(f32[520,128]{1,0:T(8,128)} %collective-permute-done.5.refs_5_), channel_id=1, source_target_pairs={{2,3},{6,7},{10,11},{14,15},{18,19},{22,23},{26,27},{30,31},{34,35... | collective-permute-start | bytes 798728 | tf_op jit(solution)/shard_map/ppermute | solution.py:49
  120.3 4.2 %step_0.1.refs_8_ = f32[3072,128]{1,0:T(8,128)} custom-call(s32[2]{0:T(128)S(1)} %broadcast_1_refs_0_.2.refs_0_, s32[24]{0:T(128)S(1)} %bitcast.14, s32[24]{0:T(128)S(1)} %bitcast.17, f32[1040,128]{1,0:T(8,128)} %pad_maximum_fusion.refs_3_, f32[2568,128]{1,0:T(8,128)S(1)} %select_maximum_fusion.refs_4_), custom_call_target="tpu_custom_call" | custom-call | flops 10000000000 | bytes 1000000 | tf_op jit(solution)/shard_map/step_0/pallas_call | solution.py:183
  124.5 1.2 broadcast_select_fusion
  125.7 4.3 %collective-permute-start.8 = (f32[2568,128]{1,0:T(8,128)}, f32[2568,128]{1,0:T(8,128)}, u32[]{:S(2)}, u32[]{:S(2)}) collective-permute-start(f32[2568,128]{1,0:T(8,128)} %broadcast_select_fusion), channel_id=1, source_target_pairs={{0,32},{1,33},{2,34},{3,35},{4,36},{5,37},{6,38},{7,39},{8,40},{9,... | collective-permute-start | bytes 3944456 | tf_op jit(solution)/shard_map/ppermute | solution.py:49
  130.1 0.7 copy-done
  130.8 0.7 copy-done.2
  131.5 0.7 collective-permute-start.9
  132.4 6.9 %step_2.1.refs_8_ = f32[3072,128]{1,0:T(8,128)} custom-call(s32[2]{0:T(128)S(1)} %add_convert_fusion.refs_0_, s32[24]{0:T(128)S(1)} %bitcast.15, s32[24]{0:T(128)S(1)} %bitcast.18, f32[520,128]{1,0:T(8,128)} %collective-permute-done.1.refs_3_, f32[520,128]{1,0:T(8,128)S(1)} %collective-permute-done.2.refs_4_, ...), custom_call_target="tpu_custom_call", output_to_operand_aliasing={{}: (8, {})} | custom-call | flops 100000000 | bytes 1000000 | tf_op jit(solution)/shard_map/step_2/pallas_call | solution.py:183
  139.4 6.6 %step_1.1 = f32[3072,128]{1,0:T(8,128)} custom-call(s32[2]{0:T(128)S(1)} %pad_add_fusion.refs_0_, s32[24]{0:T(128)S(1)} %bitcast.16, s32[24]{0:T(128)S(1)} %bitcast.19, f32[1040,128]{1,0:T(8,128)S(1)} %collective-permute-done.refs_3_, f32[520,128]{1,0:T(8,128)S(1)} %copy-done.1, f32[520,128]{1,0:T(8,128)S(1)} %copy-done.3, ...), custom_call_target="tpu_custom_call", output_to_operand_aliasing={{}: (8, {})} | custom-call | flops 100000000 | bytes 1000000 | tf_op jit(solution)/shard_map/step_1/pallas_call | solution.py:183
  (28 shorter events, 0.2 us)
Async XLA Ops:
  1.7 8.4 %copy-start.7 = (s32[1,1,20]{2,1,0:T(1,128)S(1)}, s32[1,1,20]{2,1,0:T(1,128)}, u32[]{:S(2)}) copy-start(s32[1,1,20]{2,1,0:T(1,128)} %param.16) | copy-start | bytes 244
  1.7 8.4 %copy-start.8 = (s32[1,1,20]{2,1,0:T(1,128)S(1)}, s32[1,1,20]{2,1,0:T(1,128)}, u32[]{:S(2)}) copy-start(s32[1,1,20]{2,1,0:T(1,128)} %param.15) | copy-start | bytes 244
  1.7 8.5 %copy-start.6 = (f32[1,1,20,128,128]{4,3,2,1,0:T(8,128)S(1)}, f32[1,1,20,128,128]{4,3,2,1,0:T(8,128)}, u32[]{:S(2)}) copy-start(f32[1,1,20,128,128]{4,3,2,1,0:T(8,128)} %param.14) | copy-start | bytes 3932164
  3.4 13.4 %collective-permute-start.2 = (f32[520,128]{1,0:T(8,128)S(1)}, f32[520,128]{1,0:T(8,128)S(1)}, u32[]{:S(2)}, u32[]{:S(2)}) collective-permute-start(f32[520,128]{1,0:T(8,128)S(1)} %get-tuple-element.35), channel_id=1, source_target_pairs={{0,3},{1,2},{2,0},{3,1},{4,7},{5,6},{6,4},{7,5},{8,11},{9,10},{10,... | collective-permute-start | bytes 798728 | tf_op jit(solution)/shard_map/ppermute | solution.py:49
  6.3 61.8 %collective-permute-start = (f32[1040,128]{1,0:T(8,128)}, f32[1040,128]{1,0:T(8,128)S(1)}, u32[]{:S(2)}, u32[]{:S(2)}) collective-permute-start(f32[1040,128]{1,0:T(8,128)} %pad_maximum_fusion.refs_3_), channel_id=1, source_target_pairs={{1,0},{2,1},{3,2},{5,4},{6,5},{7,6},{9,8},{10,9},{11,10},{13,12},{... | collective-permute-start | bytes 1597448 | tf_op jit(solution)/shard_map/ppermute | solution.py:49
  10.2 110.0 %copy-start.4 = (s32[1,1,24]{2,1,0:T(1,128)S(1)}, s32[1,1,24]{2,1,0:T(1,128)}, u32[]{:S(2)}) copy-start(s32[1,1,24]{2,1,0:T(1,128)} %param.18) | copy-start | bytes 292
  10.2 110.0 %copy-start.5 = (s32[1,1,24]{2,1,0:T(1,128)S(1)}, s32[1,1,24]{2,1,0:T(1,128)}, u32[]{:S(2)}) copy-start(s32[1,1,24]{2,1,0:T(1,128)} %param.19) | copy-start | bytes 292
  10.3 114.2 %collective-permute-start.7 = (f32[2568,128]{1,0:T(8,128)S(1)}, f32[2568,128]{1,0:T(8,128)S(1)}, u32[]{:S(2)}, u32[]{:S(2)}) collective-permute-start(f32[2568,128]{1,0:T(8,128)S(1)} %select_maximum_fusion.refs_4_), channel_id=1, source_target_pairs={{64,0},{65,1},{66,2},{67,3},{68,4},{69,5},{70,6},{71,7},{72,8},{73... | collective-permute-start | bytes 3944456 | tf_op jit(solution)/shard_map/ppermute | solution.py:49
  14.2 53.9 %collective-permute-start.1 = (f32[520,128]{1,0:T(8,128)}, f32[520,128]{1,0:T(8,128)}, u32[]{:S(2)}, u32[]{:S(2)}) collective-permute-start(f32[520,128]{1,0:T(8,128)} %get-tuple-element.36), channel_id=1, source_target_pairs={{0,30},{1,31},{2,0},{3,1},{4,2},{5,3},{6,4},{7,5},{8,6},{9,7},{10,... | collective-permute-start | bytes 798728 | tf_op jit(solution)/shard_map/ppermute | solution.py:49
  16.7 77.7 %collective-permute-start.5 = (f32[520,128]{1,0:T(8,128)S(1)}, f32[520,128]{1,0:T(8,128)}, u32[]{:S(2)}, u32[]{:S(2)}) collective-permute-start(f32[520,128]{1,0:T(8,128)S(1)} %collective-permute-done.2.refs_4_), channel_id=1, source_target_pairs={{2,31},{3,30},{6,3},{7,2},{10,7},{11,6},{14,11},{15,10},{18,15},{1... | collective-permute-start | bytes 798728 | tf_op jit(solution)/shard_map/ppermute | solution.py:49
  18.7 112.8 %collective-permute-start.3 = (f32[2568,128]{1,0:T(8,128)S(1)}, f32[2568,128]{1,0:T(8,128)}, u32[]{:S(2)}, u32[]{:S(2)}) collective-permute-start(f32[2568,128]{1,0:T(8,128)S(1)} %select_maximum_fusion.refs_4_), channel_id=1, source_target_pairs={{0,960},{1,961},{2,962},{3,963},{4,964},{5,965},{6,966},{7,967},{8... | collective-permute-start | bytes 3944456 | tf_op jit(solution)/shard_map/ppermute | solution.py:49
  68.1 61.9 %collective-permute-start.4 = (f32[520,128]{1,0:T(8,128)}, f32[520,128]{1,0:T(8,128)S(1)}, u32[]{:S(2)}, u32[]{:S(2)}) collective-permute-start(f32[520,128]{1,0:T(8,128)} %collective-permute-done.1.refs_3_), channel_id=1, source_target_pairs={{2,3},{6,7},{10,11},{14,15},{18,19},{22,23},{26,27},{30,31},{34,35... | collective-permute-start | bytes 798728 | tf_op jit(solution)/shard_map/ppermute | solution.py:49
  94.4 36.4 %collective-permute-start.6 = (f32[520,128]{1,0:T(8,128)}, f32[520,128]{1,0:T(8,128)S(1)}, u32[]{:S(2)}, u32[]{:S(2)}) collective-permute-start(f32[520,128]{1,0:T(8,128)} %collective-permute-done.5.refs_5_), channel_id=1, source_target_pairs={{2,3},{6,7},{10,11},{14,15},{18,19},{22,23},{26,27},{30,31},{34,35... | collective-permute-start | bytes 798728 | tf_op jit(solution)/shard_map/ppermute | solution.py:49
  125.7 13.6 %collective-permute-start.8 = (f32[2568,128]{1,0:T(8,128)}, f32[2568,128]{1,0:T(8,128)}, u32[]{:S(2)}, u32[]{:S(2)}) collective-permute-start(f32[2568,128]{1,0:T(8,128)} %broadcast_select_fusion), channel_id=1, source_target_pairs={{0,32},{1,33},{2,34},{3,35},{4,36},{5,37},{6,38},{7,39},{8,40},{9,... | collective-permute-start | bytes 3944456 | tf_op jit(solution)/shard_map/ppermute | solution.py:49
  130.1 0.7 copy-start
  130.8 0.7 copy-start.2
  131.5 7.9 %collective-permute-start.9 = (f32[2568,128]{1,0:T(8,128)}, f32[2568,128]{1,0:T(8,128)S(1)}, u32[]{:S(2)}, u32[]{:S(2)}) collective-permute-start(f32[2568,128]{1,0:T(8,128)} %collective-permute-done.3.refs_7_), channel_id=1, source_target_pairs={{960,992},{961,993},{962,994},{963,995},{964,996},{965,997},{966,9... | collective-permute-start | bytes 3944456 | tf_op jit(solution)/shard_map/ppermute | solution.py:49
  132.4 7.0 %copy-start.1 = (f32[520,128]{1,0:T(8,128)S(1)}, f32[520,128]{1,0:T(8,128)}, u32[]{:S(2)}) copy-start(f32[520,128]{1,0:T(8,128)} %copy-done) | copy-start | bytes 798724
  132.4 7.0 %copy-start.3 = (f32[520,128]{1,0:T(8,128)S(1)}, f32[520,128]{1,0:T(8,128)}, u32[]{:S(2)}) copy-start(f32[520,128]{1,0:T(8,128)} %copy-done.2) | copy-start | bytes 798724

commit v4 on v3

--- a/solution.py
+++ b/solution.py
@@ -233,18 +233,18 @@
     rows, cols = out_rows[0, 0], out_cols[0, 0]
 
     high_far = send(high, along_x({0: 3, 1: 2, 2: 0, 3: 1}))
+    high_far = send(high, along_x({0: 3, 1: 2, 2: 0, 3: 1}))
     right_near = send(right, route(lambda r, g, x: (r - 2, g, x) if r >= 2 else None))
+    right_wrap = send(right, route(lambda r, g, x: (r - 2, g, x) if r < 2 else None))
     near = send(left, along_x({1: 0, 2: 1, 3: 2}))
     low_far = send(low, route(lambda r, g, x: (r, g - 1, x + 2) if x < 2 else (r, g, x - 2)))
     across_high = send(high_far, to_previous_group({3: 2, 2: 3}))
     left, right, high_far = lax.optimization_barrier((left, right, high_far))
-    right_wrap = send(right, route(lambda r, g, x: (r - 2, g, x) if r < 2 else None))
-    near, low_far = lax.optimization_barrier((near, low_far))
     over_low = send(low_far, along_x({2: 3}))
     left, across_high, low_far = lax.optimization_barrier((left, across_high, low_far))
     over_high = send(across_high, along_x({2: 3}))
     total = step_call("step_0", jnp.zeros((2,), jnp.int32), rows, cols, [left], (WHOLE, WHOLE), [right], flops=10000000000)
-    right_near, total = lax.optimization_barrier((right_near, total))
+    right_near, total, near = lax.optimization_barrier((right_near, total, near))
     right_one = send(
         lax.select(core == 1, right, right_near),
         route(lambda r, g, x: (r ^ 1, g, x)),

time: 146 us -> 154 us (1.055)
  the two profiles are of different devices: /device:TPU:645 before, /device:TPU:31 now
where the time goes in v4:
time: 154 us
  waiting for transfers between devices  70 us (45%)
  starting transfers between devices  59.9 us (39%)
  Pallas kernels  17.1 us (11%)
  other arithmetic  3.84 us (2%)
  between operations  1.67 us (1%)
    ppermute x10, waiting for transfers between devices, send(): return lax.ppermute(block, AXES, pairs)  70 us
    ppermute x10, starting transfers between devices, send(): return lax.ppermute(block, AXES, pairs)  59.9 us
    pallas_call x3, Pallas kernels, step_call(): pl.pallas_call(functools.partial(step_kernel, picks, len(lefts), len(righ...  17.1 us
  transfers between devices with their start and end apart: 10, of which 3 were waited for; matrix products, arithmetic and copies ran while one was open for 2% of the time, Pallas kernels for 8%

profile of v4, /device:TPU:31, one launch (start us, length us, event | category | flops | bytes accessed | tf_op | source)
XLA Modules:
  0.0 153.7 jit_solution(7004985625345797863)
XLA Ops:
  0.8 1.1 fusion
  1.8 0.8 add_convert_fusion.2
  2.6 0.7 pad_maximum_fusion.1
  3.3 3.0 %collective-permute-start.1 = (f32[520,128]{1,0:T(8,128)S(1)}, f32[520,128]{1,0:T(8,128)S(1)}, u32[]{:S(2)}, u32[]{:S(2)}) collective-permute-start(f32[520,128]{1,0:T(8,128)S(1)} %get-tuple-element.34), channel_id=1, source_target_pairs={{0,3},{1,2},{2,0},{3,1},{4,7},{5,6},{6,4},{7,5},{8,11},{9,10},{10,... | collective-permute-start | bytes 798728 | tf_op jit(solution)/shard_map/ppermute | solution.py:49
  7.0 0.1 add_convert_fusion.1
  7.1 0.1 select_maximum_fusion.refs_4_
  7.2 1.3 collective-permute-start
  8.5 27.7 %collective-permute-start.5 = (f32[2568,128]{1,0:T(8,128)S(1)}, f32[2568,128]{1,0:T(8,128)}, u32[]{:S(2)}, u32[]{:S(2)}) collective-permute-start(f32[2568,128]{1,0:T(8,128)S(1)} %select_maximum_fusion.refs_4_), channel_id=1, source_target_pairs={{0,960},{1,961},{2,962},{3,963},{4,964},{5,965},{6,966},{7,967},{8... | collective-permute-start | bytes 3944456 | tf_op jit(solution)/shard_map/ppermute | solution.py:49
  36.3 3.1 %collective-permute-start.3 = (f32[520,128]{1,0:T(8,128)}, f32[520,128]{1,0:T(8,128)}, u32[]{:S(2)}, u32[]{:S(2)}) collective-permute-start(f32[520,128]{1,0:T(8,128)} %get-tuple-element.33), channel_id=1, source_target_pairs={{0,30},{1,31},{2,0},{3,1},{4,2},{5,3},{6,4},{7,5},{8,6},{9,7},{10,... | collective-permute-start | bytes 798728 | tf_op jit(solution)/shard_map/ppermute | solution.py:49
  39.4 13.3 %collective-permute-start.2 = (f32[520,128]{1,0:T(8,128)S(1)}, f32[520,128]{1,0:T(8,128)}, u32[]{:S(2)}, u32[]{:S(2)}) collective-permute-start(f32[520,128]{1,0:T(8,128)S(1)} %collective-permute-done.1.refs_4_), channel_id=1, source_target_pairs={{2,31},{3,30},{6,3},{7,2},{10,7},{11,6},{14,11},{15,10},{18,15},{1... | collective-permute-start | bytes 798728 | tf_op jit(solution)/shard_map/ppermute | solution.py:49
  52.7 0.8 pad_maximum_fusion.refs_3_
  53.5 2.5 %collective-permute-start.4 = (f32[1040,128]{1,0:T(8,128)}, f32[1040,128]{1,0:T(8,128)S(1)}, u32[]{:S(2)}, u32[]{:S(2)}) collective-permute-start(f32[1040,128]{1,0:T(8,128)} %pad_maximum_fusion.refs_3_), channel_id=1, source_target_pairs={{1,0},{2,1},{3,2},{5,4},{6,5},{7,6},{9,8},{10,9},{11,10},{13,12},{... | collective-permute-start | bytes 1597448 | tf_op jit(solution)/shard_map/ppermute | solution.py:49
  56.0 60.3 %collective-permute-done.3.refs_3_ = f32[520,128]{1,0:T(8,128)} collective-permute-done((f32[520,128]{1,0:T(8,128)}, f32[520,128]{1,0:T(8,128)}, u32[]{:S(2)}, u32[]{:S(2)}) %collective-permute-start.3) | collective-permute-done | bytes 266272 | tf_op jit(solution)/shard_map/ppermute | solution.py:49
  116.3 1.3 collective-permute-start.6
  117.6 1.3 collective-permute-start.7
  119.0 3.8 %step_0.1.refs_8_ = f32[3072,128]{1,0:T(8,128)} custom-call(s32[2]{0:T(128)S(1)} %broadcast_1_refs_0_.2.refs_0_, s32[24]{0:T(128)S(1)} %bitcast.14, s32[24]{0:T(128)S(1)} %bitcast.17, f32[1040,128]{1,0:T(8,128)} %pad_maximum_fusion.refs_3_, f32[2568,128]{1,0:T(8,128)S(1)} %select_maximum_fusion.refs_4_), custom_call_target="tpu_custom_call" | custom-call | flops 10000000000 | bytes 1000000 | tf_op jit(solution)/shard_map/step_0/pallas_call | solution.py:183
  122.9 3.9 %collective-permute-done.6.refs_4_ = f32[520,128]{1,0:T(8,128)S(1)} collective-permute-done((f32[520,128]{1,0:T(8,128)}, f32[520,128]{1,0:T(8,128)S(1)}, u32[]{:S(2)}, u32[]{:S(2)}) %collective-permute-start.6) | collective-permute-done | bytes 266272 | tf_op jit(solution)/shard_map/ppermute | solution.py:49
  126.8 5.7 %collective-permute-done.7.refs_5_ = f32[520,128]{1,0:T(8,128)S(1)} collective-permute-done((f32[520,128]{1,0:T(8,128)}, f32[520,128]{1,0:T(8,128)S(1)}, u32[]{:S(2)}, u32[]{:S(2)}) %collective-permute-start.7) | collective-permute-done | bytes 266272 | tf_op jit(solution)/shard_map/ppermute | solution.py:49
  132.5 1.7 %collective-permute-start.9 = (f32[2568,128]{1,0:T(8,128)}, f32[2568,128]{1,0:T(8,128)}, u32[]{:S(2)}, u32[]{:S(2)}) collective-permute-start(f32[2568,128]{1,0:T(8,128)} %collective-permute-done.5.refs_7_), channel_id=1, source_target_pairs={{960,992},{961,993},{962,994},{963,995},{964,996},{965,997},{966,9... | collective-permute-start | bytes 3944456 | tf_op jit(solution)/shard_map/ppermute | solution.py:49
  134.2 1.2 broadcast_select_fusion
  135.4 4.7 %collective-permute-start.8 = (f32[2568,128]{1,0:T(8,128)}, f32[2568,128]{1,0:T(8,128)S(1)}, u32[]{:S(2)}, u32[]{:S(2)}) collective-permute-start(f32[2568,128]{1,0:T(8,128)} %broadcast_select_fusion), channel_id=1, source_target_pairs={{0,32},{1,33},{2,34},{3,35},{4,36},{5,37},{6,38},{7,39},{8,40},{9,... | collective-permute-start | bytes 3944456 | tf_op jit(solution)/shard_map/ppermute | solution.py:49
  140.2 0.1 pad_add_fusion.refs_0_
  140.3 7.8 %step_2.1.refs_8_ = f32[3072,128]{1,0:T(8,128)} custom-call(s32[2]{0:T(128)S(1)} %add_convert_fusion.refs_0_, s32[24]{0:T(128)S(1)} %bitcast.15, s32[24]{0:T(128)S(1)} %bitcast.18, f32[520,128]{1,0:T(8,128)} %collective-permute-done.3.refs_3_, f32[520,128]{1,0:T(8,128)S(1)} %collective-permute-done.1.refs_4_, ...), custom_call_target="tpu_custom_call", output_to_operand_aliasing={{}: (8, {})} | custom-call | flops 100000000 | bytes 1000000 | tf_op jit(solution)/shard_map/step_2/pallas_call | solution.py:183
  148.2 5.4 %step_1.1 = f32[3072,128]{1,0:T(8,128)} custom-call(s32[2]{0:T(128)S(1)} %pad_add_fusion.refs_0_, s32[24]{0:T(128)S(1)} %bitcast.16, s32[24]{0:T(128)S(1)} %bitcast.19, f32[1040,128]{1,0:T(8,128)S(1)} %collective-permute-done.4.refs_3_, f32[520,128]{1,0:T(8,128)S(1)} %copy-done.1, f32[520,128]{1,0:T(8,128)S(1)} %copy-done.3, ...), custom_call_target="tpu_custom_call", output_to_operand_aliasing={{}: (8, {})} | custom-call | flops 100000000 | bytes 1000000 | tf_op jit(solution)/shard_map/step_1/pallas_call | solution.py:183
  (28 shorter events, 0.1 us)
Async XLA Ops:
  0.0 7.0 %copy-start.7 = (s32[1,1,20]{2,1,0:T(1,128)S(1)}, s32[1,1,20]{2,1,0:T(1,128)}, u32[]{:S(2)}) copy-start(s32[1,1,20]{2,1,0:T(1,128)} %param.16) | copy-start | bytes 244
  0.0 7.0 %copy-start.8 = (s32[1,1,20]{2,1,0:T(1,128)S(1)}, s32[1,1,20]{2,1,0:T(1,128)}, u32[]{:S(2)}) copy-start(s32[1,1,20]{2,1,0:T(1,128)} %param.15) | copy-start | bytes 244
  0.0 7.1 %copy-start.6 = (f32[1,1,20,128,128]{4,3,2,1,0:T(8,128)S(1)}, f32[1,1,20,128,128]{4,3,2,1,0:T(8,128)}, u32[]{:S(2)}) copy-start(f32[1,1,20,128,128]{4,3,2,1,0:T(8,128)} %param.14) | copy-start | bytes 3932164
  3.3 36.0 %collective-permute-start.1 = (f32[520,128]{1,0:T(8,128)S(1)}, f32[520,128]{1,0:T(8,128)S(1)}, u32[]{:S(2)}, u32[]{:S(2)}) collective-permute-start(f32[520,128]{1,0:T(8,128)S(1)} %get-tuple-element.34), channel_id=1, source_target_pairs={{0,3},{1,2},{2,0},{3,1},{4,7},{5,6},{6,4},{7,5},{8,11},{9,10},{10,... | collective-permute-start | bytes 798728 | tf_op jit(solution)/shard_map/ppermute | solution.py:49
  7.1 111.8 %copy-start.4 = (s32[1,1,24]{2,1,0:T(1,128)S(1)}, s32[1,1,24]{2,1,0:T(1,128)}, u32[]{:S(2)}) copy-start(s32[1,1,24]{2,1,0:T(1,128)} %param.18) | copy-start | bytes 292
  7.1 111.9 %copy-start.5 = (s32[1,1,24]{2,1,0:T(1,128)S(1)}, s32[1,1,24]{2,1,0:T(1,128)}, u32[]{:S(2)}) copy-start(s32[1,1,24]{2,1,0:T(1,128)} %param.19) | copy-start | bytes 292
  7.2 115.6 %collective-permute-start = (f32[2568,128]{1,0:T(8,128)S(1)}, f32[2568,128]{1,0:T(8,128)S(1)}, u32[]{:S(2)}, u32[]{:S(2)}) collective-permute-start(f32[2568,128]{1,0:T(8,128)S(1)} %select_maximum_fusion.refs_4_), channel_id=1, source_target_pairs={{64,0},{65,1},{66,2},{67,3},{68,4},{69,5},{70,6},{71,7},{72,8},{73... | collective-permute-start | bytes 3944456 | tf_op jit(solution)/shard_map/ppermute | solution.py:49
  8.5 124.0 %collective-permute-start.5 = (f32[2568,128]{1,0:T(8,128)S(1)}, f32[2568,128]{1,0:T(8,128)}, u32[]{:S(2)}, u32[]{:S(2)}) collective-permute-start(f32[2568,128]{1,0:T(8,128)S(1)} %select_maximum_fusion.refs_4_), channel_id=1, source_target_pairs={{0,960},{1,961},{2,962},{3,963},{4,964},{5,965},{6,966},{7,967},{8... | collective-permute-start | bytes 3944456 | tf_op jit(solution)/shard_map/ppermute | solution.py:49
  36.3 80.1 %collective-permute-start.3 = (f32[520,128]{1,0:T(8,128)}, f32[520,128]{1,0:T(8,128)}, u32[]{:S(2)}, u32[]{:S(2)}) collective-permute-start(f32[520,128]{1,0:T(8,128)} %get-tuple-element.33), channel_id=1, source_target_pairs={{0,30},{1,31},{2,0},{3,1},{4,2},{5,3},{6,4},{7,5},{8,6},{9,7},{10,... | collective-permute-start | bytes 798728 | tf_op jit(solution)/shard_map/ppermute | solution.py:49
  39.4 78.3 %collective-permute-start.2 = (f32[520,128]{1,0:T(8,128)S(1)}, f32[520,128]{1,0:T(8,128)}, u32[]{:S(2)}, u32[]{:S(2)}) collective-permute-start(f32[520,128]{1,0:T(8,128)S(1)} %collective-permute-done.1.refs_4_), channel_id=1, source_target_pairs={{2,31},{3,30},{6,3},{7,2},{10,7},{11,6},{14,11},{15,10},{18,15},{1... | collective-permute-start | bytes 798728 | tf_op jit(solution)/shard_map/ppermute | solution.py:49
  53.5 69.3 %collective-permute-start.4 = (f32[1040,128]{1,0:T(8,128)}, f32[1040,128]{1,0:T(8,128)S(1)}, u32[]{:S(2)}, u32[]{:S(2)}) collective-permute-start(f32[1040,128]{1,0:T(8,128)} %pad_maximum_fusion.refs_3_), channel_id=1, source_target_pairs={{1,0},{2,1},{3,2},{5,4},{6,5},{7,6},{9,8},{10,9},{11,10},{13,12},{... | collective-permute-start | bytes 1597448 | tf_op jit(solution)/shard_map/ppermute | solution.py:49
  116.3 10.4 %collective-permute-start.6 = (f32[520,128]{1,0:T(8,128)}, f32[520,128]{1,0:T(8,128)S(1)}, u32[]{:S(2)}, u32[]{:S(2)}) collective-permute-start(f32[520,128]{1,0:T(8,128)} %collective-permute-done.3.refs_3_), channel_id=1, source_target_pairs={{2,3},{6,7},{10,11},{14,15},{18,19},{22,23},{26,27},{30,31},{34,35... | collective-permute-start | bytes 798728 | tf_op jit(solution)/shard_map/ppermute | solution.py:49
  117.6 14.8 %collective-permute-start.7 = (f32[520,128]{1,0:T(8,128)}, f32[520,128]{1,0:T(8,128)S(1)}, u32[]{:S(2)}, u32[]{:S(2)}) collective-permute-start(f32[520,128]{1,0:T(8,128)} %collective-permute-done.2.refs_5_), channel_id=1, source_target_pairs={{2,3},{6,7},{10,11},{14,15},{18,19},{22,23},{26,27},{30,31},{34,35... | collective-permute-start | bytes 798728 | tf_op jit(solution)/shard_map/ppermute | solution.py:49
  126.8 8.6 %copy-start = (f32[520,128]{1,0:T(8,128)}, f32[520,128]{1,0:T(8,128)S(1)}, u32[]{:S(2)}) copy-start(f32[520,128]{1,0:T(8,128)S(1)} %collective-permute-done.6.refs_4_) | copy-start | bytes 798724
  132.5 2.9 %copy-start.2 = (f32[520,128]{1,0:T(8,128)}, f32[520,128]{1,0:T(8,128)S(1)}, u32[]{:S(2)}) copy-start(f32[520,128]{1,0:T(8,128)S(1)} %collective-permute-done.7.refs_5_) | copy-start | bytes 798724
  132.5 15.7 %collective-permute-start.9 = (f32[2568,128]{1,0:T(8,128)}, f32[2568,128]{1,0:T(8,128)}, u32[]{:S(2)}, u32[]{:S(2)}) collective-permute-start(f32[2568,128]{1,0:T(8,128)} %collective-permute-done.5.refs_7_), channel_id=1, source_target_pairs={{960,992},{961,993},{962,994},{963,995},{964,996},{965,997},{966,9... | collective-permute-start | bytes 3944456 | tf_op jit(solution)/shard_map/ppermute | solution.py:49
  135.4 12.8 %collective-permute-start.8 = (f32[2568,128]{1,0:T(8,128)}, f32[2568,128]{1,0:T(8,128)S(1)}, u32[]{:S(2)}, u32[]{:S(2)}) collective-permute-start(f32[2568,128]{1,0:T(8,128)} %broadcast_select_fusion), channel_id=1, source_target_pairs={{0,32},{1,33},{2,34},{3,35},{4,36},{5,37},{6,38},{7,39},{8,40},{9,... | collective-permute-start | bytes 3944456 | tf_op jit(solution)/shard_map/ppermute | solution.py:49
  140.3 7.9 %copy-start.1 = (f32[520,128]{1,0:T(8,128)S(1)}, f32[520,128]{1,0:T(8,128)}, u32[]{:S(2)}) copy-start(f32[520,128]{1,0:T(8,128)} %copy-done) | copy-start | bytes 798724
  140.3 7.9 %copy-start.3 = (f32[520,128]{1,0:T(8,128)S(1)}, f32[520,128]{1,0:T(8,128)}, u32[]{:S(2)}) copy-start(f32[520,128]{1,0:T(8,128)} %copy-done.2) | copy-start | bytes 798724

commit v5 on v3

--- a/solution.py
+++ b/solution.py
@@ -96,81 +96,96 @@
     return high, low
 
 
-def step_kernel(picks, n_left, n_right, first, *refs):
-    sides, out_rows, out_cols = refs[:3]
-    lefts = refs[3 : 3 + n_left]
-    rights = refs[3 + n_left : 3 + n_left + n_right]
+def step_kernel(passes, n_arrays, first, *refs):
+    flags, out_rows, out_cols = refs[:3]
+    arrays = refs[3 : 3 + n_arrays]
     (total, left_tile, right_tile, left_meta, right_meta, slot_of, by_inner, products, sems) = refs[-9:]
-    other_left, other_right = sides[0] == 1, sides[1] == 1
-
-    def left_at(pick, sem):
-        return pltpu.make_async_copy(lefts[pick[0]].at[pl.ds(pick[1] + HALF, PAD)], left_meta, sem)
-
-    def right_at(ref, sem):
-        return pltpu.make_async_copy(ref.at[pl.ds(RIGHT_ROWS, PAD)], right_meta, sem)
-
-    def either(condition, same, no, yes):
-        if same:
+
+    def either(flag, no, yes):
+        if flag is None:
             no()
         else:
-            pl.when(condition)(yes)
-            pl.when(jnp.logical_not(condition))(no)
-
-    either(
-        other_left,
-        picks[0][0] == picks[1][0],
-        lambda: left_at(picks[0][0], sems.at[0]).start(),
-        lambda: left_at(picks[1][0], sems.at[0]).start(),
-    )
-    either(
-        other_right,
-        n_right == 1,
-        lambda: right_at(rights[0], sems.at[1]).start(),
-        lambda: right_at(rights[-1], sems.at[1]).start(),
-    )
-    mark_slots(out_rows, out_cols, slot_of)
-    total[...] = jnp.zeros_like(total) if first else refs[3 + n_left + n_right][...]
-    left_at(picks[0][0], sems.at[0]).wait()
-    right_at(rights[0], sems.at[1]).wait()
-    count = list_products(left_meta, right_meta, slot_of, by_inner, products, 0)
-
-    def copy_tile(tile, ref, start):
-        tile[...] = ref[pl.ds(pl.multiple_of(start, 8), BS), :]
-
-    def copy_half(pick, start):
-        copy_tile(left_tile, lefts[pick[0]], pick[1] + start)
-
-    def body(i, carry):
-        code = products[i]
-        a = code // 1024
-        b = (code // 32) % 32
-        c = code % 32
-        upper = a // (MAXA // 2)
-        at = (a % (MAXA // 2)) * BS
-        for half in range(2):
-
-            @pl.when(upper == half)
-            def _():
-                one, other = picks[0][half], picks[1][half]
-                either(other_left, one == other, lambda: copy_half(one, at), lambda: copy_half(other, at))
-
-        either(
-            other_right,
-            n_right == 1,
-            lambda: copy_tile(right_tile, rights[0], b * BS),
-            lambda: copy_tile(right_tile, rights[-1], b * BS),
-        )
-        left_high_part, left_low_part = split(left_tile[...])
-        right_high_part, right_low_part = split(right_tile[...])
-        lhs = jnp.concatenate([left_high_part, left_low_part], axis=1)
-        both = jnp.concatenate([right_high_part, right_low_part], axis=1)
-        rhs = jnp.concatenate([both, both], axis=0)
-        pair = jnp.dot(lhs, rhs, preferred_element_type=jnp.float32)
-        place = pl.ds(pl.multiple_of(c * BS, BS), BS)
-        total[place, :] = total[place, :] + (pair[:, :BS] + pair[:, BS:])
-        return carry
-
-    lax.fori_loop(0, count, body, 0)
+            pl.when(flags[flag] == 0)(no)
+            pl.when(flags[flag] == 1)(yes)
+
+    def left_copy(half):
+        place, row = half
+        return pltpu.make_async_copy(arrays[place].at[pl.ds(row + HALF, PAD)], left_meta, sems.at[0])
+
+    def right_copy(place):
+        return pltpu.make_async_copy(arrays[place].at[pl.ds(RIGHT_ROWS, PAD)], right_meta, sems.at[1])
+
+    def start_metas(left_flag, right_flag, lefts, rights):
+        either(left_flag, lambda: left_copy(lefts[0][0]).start(), lambda: left_copy(lefts[1][0]).start())
+        either(right_flag, lambda: right_copy(rights[0]).start(), lambda: right_copy(rights[1]).start())
+
+    def finish(left_flag, right_flag, lefts, rights):
+        left_copy(lefts[0][0]).wait()
+        right_copy(rights[0]).wait()
+        count = list_products(left_meta, right_meta, slot_of, by_inner, products, 0)
+
+        def copy_tile(tile, place, start):
+            tile[...] = arrays[place][pl.ds(pl.multiple_of(start, 8), BS), :]
+
+        def copy_half(half, start):
+            copy_tile(left_tile, half[0], half[1] + start)
+
+        def body(i, carry):
+            code = products[i]
+            a = code // 1024
+            b = (code // 32) % 32
+            c = code % 32
+            upper = a // (MAXA // 2)
+            at = (a % (MAXA // 2)) * BS
+            for half in range(2):
+
+                @pl.when(upper == half)
+                def _():
+                    one, other = lefts[0][half], lefts[1][half]
+                    flag = None if one == other else left_flag
+                    either(flag, lambda: copy_half(one, at), lambda: copy_half(other, at))
+
+            either(
+                right_flag,
+                lambda: copy_tile(right_tile, rights[0], b * BS),
+                lambda: copy_tile(right_tile, rights[1], b * BS),
+            )
+            left_high_part, left_low_part = split(left_tile[...])
+            right_high_part, right_low_part = split(right_tile[...])
+            lhs = jnp.concatenate([left_high_part, left_low_part], axis=1)
+            both = jnp.concatenate([right_high_part, right_low_part], axis=1)
+            rhs = jnp.concatenate([both, both], axis=0)
+            pair = jnp.dot(lhs, rhs, preferred_element_type=jnp.float32)
+            place = pl.ds(pl.multiple_of(c * BS, BS), BS)
+            total[place, :] = total[place, :] + (pair[:, :BS] + pair[:, BS:])
+            return carry
+
+        lax.fori_loop(0, count, body, 0)
+
+    def run(index, prepare):
+        left_flag, right_flag, enable, lefts, rights = passes[index]
+
+        def whole():
+            start_metas(left_flag, right_flag, lefts, rights)
+            prepare()
+            finish(left_flag, right_flag, lefts, rights)
+
+        if enable is None:
+            whole()
+        else:
+            pl.when(flags[enable] == 1)(whole)
+
+    def prepare():
+        mark_slots(out_rows, out_cols, slot_of)
+        total[...] = jnp.zeros_like(total) if first else refs[3 + n_arrays][...]
+
+    if passes[0][2] is None:
+        run(0, prepare)
+    else:
+        prepare()
+        run(0, lambda: None)
+    for index in range(1, len(passes)):
+        run(index, lambda: None)
 
 
 WHOLE = ((0, 0), (0, LEFT_HALF))
@@ -178,10 +193,10 @@
 VMEM_SPEC = pl.BlockSpec(memory_space=pltpu.VMEM)
 
 
-def step_call(name, sides, out_rows, out_cols, lefts, picks, rights, before=None, flops=10**8):
-    operands = [sides, out_rows, out_cols, *lefts, *rights] + ([] if before is None else [before])
+def step_call(name, flags, out_rows, out_cols, arrays, passes, before=None, flops=10**8):
+    operands = [flags, out_rows, out_cols, *arrays] + ([] if before is None else [before])
     return pl.pallas_call(
-        functools.partial(step_kernel, picks, len(lefts), len(rights), before is None),
+        functools.partial(step_kernel, passes, len(arrays), before is None),
         out_shape=jax.ShapeDtypeStruct((CMAX * BS, BS), jnp.float32),
         in_specs=[SMEM_SPEC] * 3 + [VMEM_SPEC] * (len(operands) - 3),
         out_specs=VMEM_SPEC,
@@ -229,46 +244,49 @@
     x = lax.axis_index("col") % GROUP
     row = lax.axis_index("row")
     core = row % 2
-    last_chip = (row // 2 == N_ROW // 2 - 1).astype(jnp.int32)
+    last_chip = row // 2 == N_ROW // 2 - 1
     rows, cols = out_rows[0, 0], out_cols[0, 0]
 
+    flags = jnp.stack([x == 3, (core == 1) & last_chip, x >= 2, last_chip, ~last_chip]).astype(jnp.int32)
     high_far = send(high, along_x({0: 3, 1: 2, 2: 0, 3: 1}))
     right_near = send(right, route(lambda r, g, x: (r - 2, g, x) if r >= 2 else None))
-    near = send(left, along_x({1: 0, 2: 1, 3: 2}))
     low_far = send(low, route(lambda r, g, x: (r, g - 1, x + 2) if x < 2 else (r, g, x - 2)))
     across_high = send(high_far, to_previous_group({3: 2, 2: 3}))
     left, right, high_far = lax.optimization_barrier((left, right, high_far))
     right_wrap = send(right, route(lambda r, g, x: (r - 2, g, x) if r < 2 else None))
-    near, low_far = lax.optimization_barrier((near, low_far))
+    near = send(left, along_x({1: 0, 2: 1, 3: 2}))
+    total = step_call("step_0", flags, rows, cols, [left, right], ((None, None, None, (WHOLE, WHOLE), (1, 1)),), flops=2000000000)
+    low_far, total = lax.optimization_barrier((low_far, total))
     over_low = send(low_far, along_x({2: 3}))
-    left, across_high, low_far = lax.optimization_barrier((left, across_high, low_far))
+    across_high, low_far = lax.optimization_barrier((across_high, low_far))
     over_high = send(across_high, along_x({2: 3}))
-    total = step_call("step_0", jnp.zeros((2,), jnp.int32), rows, cols, [left], (WHOLE, WHOLE), [right], flops=10000000000)
-    right_near, total = lax.optimization_barrier((right_near, total))
+    right_near, total, across_high = lax.optimization_barrier((right_near, total, across_high))
     right_one = send(
         lax.select(core == 1, right, right_near),
         route(lambda r, g, x: (r ^ 1, g, x)),
     )
-    right_wrap, over_low, over_high, total = lax.optimization_barrier((right_wrap, over_low, over_high, total))
+    total = step_call(
+        "step_2",
+        flags,
+        rows,
+        cols,
+        [low_far, high_far, across_high, right_near],
+        ((2, None, 4, (((0, 0), (1, 0)), ((0, 0), (2, 0))), (3, 3)),),
+        total,
+        flops=10000000000,
+    )
+    right_wrap, over_low, over_high, total, near = lax.optimization_barrier((right_wrap, over_low, over_high, total, near))
     edge = send(right_wrap, route(lambda r, g, x: (r + 1, g, x) if r == N_ROW - 2 else None))
     total = step_call(
-        "step_2",
-        jnp.stack([(x >= 2).astype(jnp.int32), last_chip]),
+        "step_1",
+        flags,
         rows,
         cols,
-        [low_far, high_far, across_high],
-        (((0, 0), (1, 0)), ((0, 0), (2, 0))),
-        [right_near, right_wrap],
-        total,
-    )
-    total = step_call(
-        "step_1",
-        jnp.stack([(x == 3).astype(jnp.int32), last_chip * core]),
-        rows,
-        cols,
-        [near, over_low, over_high],
-        (WHOLE, ((1, 0), (2, 0))),
-        [right_one, edge],
+        [near, over_low, over_high, right_one, edge, low_far, high_far, across_high, right_wrap],
+        (
+            (0, 1, None, (((0, 0), (0, LEFT_HALF)), ((1, 0), (2, 0))), (3, 4)),
+            (2, None, 3, (((5, 0), (6, 0)), ((5, 0), (7, 0))), (8, 8)),
+        ),
         total,
     )
     return total.reshape(1, 1, CMAX, BS, BS)

time: 146 us -> 136 us (0.932)
  the two profiles are of different devices: /device:TPU:645 before, /device:TPU:725 now
where the time goes in v5:
time: 136 us
  starting transfers between devices  70.4 us (52%)
  waiting for transfers between devices  44.4 us (33%)
  Pallas kernels  16.2 us (12%)
  other arithmetic  3.24 us (2%)
  between operations  1.57 us (1%)
    ppermute x10, starting transfers between devices, send(): return lax.ppermute(block, AXES, pairs)  70.4 us
    ppermute x10, waiting for transfers between devices, send(): return lax.ppermute(block, AXES, pairs)  44.4 us
    pallas_call x3, Pallas kernels, step_call(): pl.pallas_call(functools.partial(step_kernel, passes, len(arrays), before...  16.2 us
  transfers between devices with their start and end apart: 10, of which 2 were waited for; matrix products, arithmetic and copies ran while one was open for 1% of the time, Pallas kernels for 7%

profile of v5, /device:TPU:725, one launch (start us, length us, event | category | flops | bytes accessed | tf_op | source)
XLA Modules:
  0.0 136.0 jit_solution(14883304638501791538)
XLA Ops:
  0.7 0.7 add_convert_fusion.1
  1.4 1.5 %select_maximum_fusion.refs_4_ = f32[2568,128]{1,0:T(8,128)S(1)} fusion(f32[1,41]{1,0:T(1,128)S(1)} %add_convert_fusion.1, f32[2560,128]{1,0:T(8,128)} %bitcast.25), kind=kLoop, calls=%fused_computation | loop fusion | flops 986112 | bytes 2625700 | tf_op jit(solution)/shard_map/concatenate | solution.py:243
  2.9 2.6 %collective-permute-start.6 = (f32[2568,128]{1,0:T(8,128)S(1)}, f32[2568,128]{1,0:T(8,128)S(1)}, u32[]{:S(2)}, u32[]{:S(2)}) collective-permute-start(f32[2568,128]{1,0:T(8,128)S(1)} %select_maximum_fusion.refs_4_), channel_id=1, source_target_pairs={{64,0},{65,1},{66,2},{67,3},{68,4},{69,5},{70,6},{71,7},{72,8},{73... | collective-permute-start | bytes 3944456 | tf_op jit(solution)/shard_map/ppermute | solution.py:49
  6.2 0.1 add_convert_fusion
  6.3 0.0 copy-start
  6.3 0.0 copy-start.1
  6.3 0.7 pad_maximum_fusion.1
  7.1 2.1 %collective-permute-start = (f32[520,128]{1,0:T(8,128)S(1)}, f32[520,128]{1,0:T(8,128)S(1)}, u32[]{:S(2)}, u32[]{:S(2)}) collective-permute-start(f32[520,128]{1,0:T(8,128)S(1)} %get-tuple-element.38), channel_id=1, source_target_pairs={{0,3},{1,2},{2,0},{3,1},{4,7},{5,6},{6,4},{7,5},{8,11},{9,10},{10,... | collective-permute-start | bytes 798728 | tf_op jit(solution)/shard_map/ppermute | solution.py:49
  9.2 4.4 %collective-permute-start.2 = (f32[520,128]{1,0:T(8,128)}, f32[520,128]{1,0:T(8,128)}, u32[]{:S(2)}, u32[]{:S(2)}) collective-permute-start(f32[520,128]{1,0:T(8,128)} %get-tuple-element.37), channel_id=1, source_target_pairs={{0,30},{1,31},{2,0},{3,1},{4,2},{5,3},{6,4},{7,5},{8,6},{9,7},{10,... | collective-permute-start | bytes 798728 | tf_op jit(solution)/shard_map/ppermute | solution.py:49
  13.6 2.3 %collective-permute-done.refs_4_.refs_9_ = f32[520,128]{1,0:T(8,128)S(1)} collective-permute-done((f32[520,128]{1,0:T(8,128)S(1)}, f32[520,128]{1,0:T(8,128)S(1)}, u32[]{:S(2)}, u32[]{:S(2)}) %collective-permute-start) | collective-permute-done | bytes 266272 | tf_op jit(solution)/shard_map/ppermute | solution.py:49
  15.9 2.8 %collective-permute-start.4 = (f32[520,128]{1,0:T(8,128)S(1)}, f32[520,128]{1,0:T(8,128)}, u32[]{:S(2)}, u32[]{:S(2)}) collective-permute-start(f32[520,128]{1,0:T(8,128)S(1)} %collective-permute-done.refs_4_.refs_9_), channel_id=1, source_target_pairs={{2,31},{3,30},{6,3},{7,2},{10,7},{11,6},{14,11},{15,10},{18,15},{1... | collective-permute-start | bytes 798728 | tf_op jit(solution)/shard_map/ppermute | solution.py:49
  18.8 0.1 stack.23
  18.9 2.2 %collective-permute-start.7 = (f32[1040,128]{1,0:T(8,128)S(1)}, f32[1040,128]{1,0:T(8,128)S(1)}, u32[]{:S(2)}, u32[]{:S(2)}) collective-permute-start(f32[1040,128]{1,0:T(8,128)S(1)} %pad_maximum_fusion.refs_3_), channel_id=1, source_target_pairs={{1,0},{2,1},{3,2},{5,4},{6,5},{7,6},{9,8},{10,9},{11,10},{13,12},{... | collective-permute-start | bytes 1597448 | tf_op jit(solution)/shard_map/ppermute | solution.py:49
  21.1 0.7 collective-permute-start.1
  21.9 3.8 %step_0.1.refs_7_ = f32[3072,128]{1,0:T(8,128)} custom-call(s32[5]{0:T(128)S(1)} %convert_element_type.27.refs_0_, s32[24]{0:T(128)S(1)} %bitcast.15, s32[24]{0:T(128)S(1)} %bitcast.18, f32[1040,128]{1,0:T(8,128)S(1)} %pad_maximum_fusion.refs_3_, f32[2568,128]{1,0:T(8,128)S(1)} %select_maximum_fusion.refs_4_), custom_call_target="tpu_custom_call" | custom-call | flops 2000000000 | bytes 1000000 | tf_op jit(solution)/shard_map/step_0/pallas_call | solution.py:198
  25.6 42.1 %collective-permute-done.2.refs_3_.refs_8_ = f32[520,128]{1,0:T(8,128)} collective-permute-done((f32[520,128]{1,0:T(8,128)}, f32[520,128]{1,0:T(8,128)}, u32[]{:S(2)}, u32[]{:S(2)}) %collective-permute-start.2) | collective-permute-done | bytes 266272 | tf_op jit(solution)/shard_map/ppermute | solution.py:49
  67.7 1.3 collective-permute-start.3
  69.0 0.0 collective-permute-done.4.refs_5_.refs_10_
  69.1 1.3 collective-permute-start.5
  70.4 0.2 broadcast_select_fusion
  70.6 52.1 %collective-permute-start.8 = (f32[2568,128]{1,0:T(8,128)S(1)}, f32[2568,128]{1,0:T(8,128)S(1)}, u32[]{:S(2)}, u32[]{:S(2)}) collective-permute-start(f32[2568,128]{1,0:T(8,128)S(1)} %broadcast_select_fusion), channel_id=1, source_target_pairs={{0,32},{1,33},{2,34},{3,35},{4,36},{5,37},{6,38},{7,39},{8,40},{9,... | collective-permute-start | bytes 3944456 | tf_op jit(solution)/shard_map/ppermute | solution.py:49
  122.7 5.4 %step_2.1.refs_12_ = f32[3072,128]{1,0:T(8,128)} custom-call(s32[5]{0:T(128)S(1)} %convert_element_type.27.refs_0_, s32[24]{0:T(128)S(1)} %bitcast.16, s32[24]{0:T(128)S(1)} %bitcast.19, f32[520,128]{1,0:T(8,128)} %collective-permute-done.2.refs_3_.refs_8_, f32[520,128]{1,0:T(8,128)S(1)} %collective-permute-done.refs_4_.refs_9_, ...), custom_call_target="tpu_custom_call", output_to_operand_aliasing={{}: (7, {})} | custom-call | flops 10000000000 | bytes 1000000 | tf_op jit(solution)/shard_map/step_2/pallas_call | solution.py:198
  128.1 0.7 collective-permute-start.9
  128.9 7.1 %step_1.1 = f32[3072,128]{1,0:T(8,128)} custom-call(s32[5]{0:T(128)S(1)} %convert_element_type.27.refs_0_, s32[24]{0:T(128)S(1)} %bitcast.17, s32[24]{0:T(128)S(1)} %bitcast.20, f32[1040,128]{1,0:T(8,128)S(1)} %collective-permute-done.7.refs_3_, f32[520,128]{1,0:T(8,128)S(1)} %collective-permute-done.3.refs_4_, ...), custom_call_target="tpu_custom_call", output_to_operand_aliasing={{}: (12, {})} | custom-call | flops 100000000 | bytes 1000000 | tf_op jit(solution)/shard_map/step_1/pallas_call | solution.py:198
  (19 shorter events, 0.1 us)
Async XLA Ops:
  1.4 4.8 %copy-start.3 = (s32[1,1,8]{2,1,0:T(1,128)S(1)}, s32[1,1,8]{2,1,0:T(1,128)}, u32[]{:S(2)}) copy-start(s32[1,1,8]{2,1,0:T(1,128)} %param.12) | copy-start | bytes 100
  1.4 4.8 %copy-start.4 = (s32[1,1,8]{2,1,0:T(1,128)S(1)}, s32[1,1,8]{2,1,0:T(1,128)}, u32[]{:S(2)}) copy-start(s32[1,1,8]{2,1,0:T(1,128)} %param.11) | copy-start | bytes 100
  1.4 4.9 %copy-start.2 = (f32[1,1,8,128,128]{4,3,2,1,0:T(8,128)S(1)}, f32[1,1,8,128,128]{4,3,2,1,0:T(8,128)}, u32[]{:S(2)}) copy-start(f32[1,1,8,128,128]{4,3,2,1,0:T(8,128)} %param.10) | copy-start | bytes 1572868
  2.9 67.5 %collective-permute-start.6 = (f32[2568,128]{1,0:T(8,128)S(1)}, f32[2568,128]{1,0:T(8,128)S(1)}, u32[]{:S(2)}, u32[]{:S(2)}) collective-permute-start(f32[2568,128]{1,0:T(8,128)S(1)} %select_maximum_fusion.refs_4_), channel_id=1, source_target_pairs={{64,0},{65,1},{66,2},{67,3},{68,4},{69,5},{70,6},{71,7},{72,8},{73... | collective-permute-start | bytes 3944456 | tf_op jit(solution)/shard_map/ppermute | solution.py:49
  6.3 15.5 %copy-start = (s32[1,1,24]{2,1,0:T(1,128)S(1)}, s32[1,1,24]{2,1,0:T(1,128)}, u32[]{:S(2)}) copy-start(s32[1,1,24]{2,1,0:T(1,128)} %param.18) | copy-start | bytes 292
  6.3 15.5 %copy-start.1 = (s32[1,1,24]{2,1,0:T(1,128)S(1)}, s32[1,1,24]{2,1,0:T(1,128)}, u32[]{:S(2)}) copy-start(s32[1,1,24]{2,1,0:T(1,128)} %param.19) | copy-start | bytes 292
  7.1 8.8 %collective-permute-start = (f32[520,128]{1,0:T(8,128)S(1)}, f32[520,128]{1,0:T(8,128)S(1)}, u32[]{:S(2)}, u32[]{:S(2)}) collective-permute-start(f32[520,128]{1,0:T(8,128)S(1)} %get-tuple-element.38), channel_id=1, source_target_pairs={{0,3},{1,2},{2,0},{3,1},{4,7},{5,6},{6,4},{7,5},{8,11},{9,10},{10,... | collective-permute-start | bytes 798728 | tf_op jit(solution)/shard_map/ppermute | solution.py:49
  9.2 58.5 %collective-permute-start.2 = (f32[520,128]{1,0:T(8,128)}, f32[520,128]{1,0:T(8,128)}, u32[]{:S(2)}, u32[]{:S(2)}) collective-permute-start(f32[520,128]{1,0:T(8,128)} %get-tuple-element.37), channel_id=1, source_target_pairs={{0,30},{1,31},{2,0},{3,1},{4,2},{5,3},{6,4},{7,5},{8,6},{9,7},{10,... | collective-permute-start | bytes 798728 | tf_op jit(solution)/shard_map/ppermute | solution.py:49
  15.9 53.1 %collective-permute-start.4 = (f32[520,128]{1,0:T(8,128)S(1)}, f32[520,128]{1,0:T(8,128)}, u32[]{:S(2)}, u32[]{:S(2)}) collective-permute-start(f32[520,128]{1,0:T(8,128)S(1)} %collective-permute-done.refs_4_.refs_9_), channel_id=1, source_target_pairs={{2,31},{3,30},{6,3},{7,2},{10,7},{11,6},{14,11},{15,10},{18,15},{1... | collective-permute-start | bytes 798728 | tf_op jit(solution)/shard_map/ppermute | solution.py:49
  18.9 109.2 %collective-permute-start.7 = (f32[1040,128]{1,0:T(8,128)S(1)}, f32[1040,128]{1,0:T(8,128)S(1)}, u32[]{:S(2)}, u32[]{:S(2)}) collective-permute-start(f32[1040,128]{1,0:T(8,128)S(1)} %pad_maximum_fusion.refs_3_), channel_id=1, source_target_pairs={{1,0},{2,1},{3,2},{5,4},{6,5},{7,6},{9,8},{10,9},{11,10},{13,12},{... | collective-permute-start | bytes 1597448 | tf_op jit(solution)/shard_map/ppermute | solution.py:49
  21.1 107.0 %collective-permute-start.1 = (f32[2568,128]{1,0:T(8,128)S(1)}, f32[2568,128]{1,0:T(8,128)S(1)}, u32[]{:S(2)}, u32[]{:S(2)}) collective-permute-start(f32[2568,128]{1,0:T(8,128)S(1)} %select_maximum_fusion.refs_4_), channel_id=1, source_target_pairs={{0,960},{1,961},{2,962},{3,963},{4,964},{5,965},{6,966},{7,967},{8... | collective-permute-start | bytes 3944456 | tf_op jit(solution)/shard_map/ppermute | solution.py:49
  67.7 60.4 %collective-permute-start.3 = (f32[520,128]{1,0:T(8,128)}, f32[520,128]{1,0:T(8,128)S(1)}, u32[]{:S(2)}, u32[]{:S(2)}) collective-permute-start(f32[520,128]{1,0:T(8,128)} %collective-permute-done.2.refs_3_.refs_8_), channel_id=1, source_target_pairs={{2,3},{6,7},{10,11},{14,15},{18,19},{22,23},{26,27},{30,31},{34,35... | collective-permute-start | bytes 798728 | tf_op jit(solution)/shard_map/ppermute | solution.py:49
  69.1 59.1 %collective-permute-start.5 = (f32[520,128]{1,0:T(8,128)}, f32[520,128]{1,0:T(8,128)S(1)}, u32[]{:S(2)}, u32[]{:S(2)}) collective-permute-start(f32[520,128]{1,0:T(8,128)} %collective-permute-done.4.refs_5_.refs_10_), channel_id=1, source_target_pairs={{2,3},{6,7},{10,11},{14,15},{18,19},{22,23},{26,27},{30,31},{34,35... | collective-permute-start | bytes 798728 | tf_op jit(solution)/shard_map/ppermute | solution.py:49
  70.6 58.3 %collective-permute-start.8 = (f32[2568,128]{1,0:T(8,128)S(1)}, f32[2568,128]{1,0:T(8,128)S(1)}, u32[]{:S(2)}, u32[]{:S(2)}) collective-permute-start(f32[2568,128]{1,0:T(8,128)S(1)} %broadcast_select_fusion), channel_id=1, source_target_pairs={{0,32},{1,33},{2,34},{3,35},{4,36},{5,37},{6,38},{7,39},{8,40},{9,... | collective-permute-start | bytes 3944456 | tf_op jit(solution)/shard_map/ppermute | solution.py:49
  128.1 0.8 collective-permute-start.9

commit v6 on v5

--- a/solution.py
+++ b/solution.py
@@ -9,6 +9,7 @@
 
 BS = 128
 MAXA = 8
+BATCH = 4
 MAXB = 20
 CMAX = 24
 ROWB = 8
@@ -127,40 +128,48 @@
         def copy_tile(tile, place, start):
             tile[...] = arrays[place][pl.ds(pl.multiple_of(start, 8), BS), :]
 
-        def copy_half(half, start):
-            copy_tile(left_tile, half[0], half[1] + start)
-
         def body(i, carry):
-            code = products[i]
-            a = code // 1024
-            b = (code // 32) % 32
-            c = code % 32
-            upper = a // (MAXA // 2)
-            at = (a % (MAXA // 2)) * BS
-            for half in range(2):
-
-                @pl.when(upper == half)
-                def _():
-                    one, other = lefts[0][half], lefts[1][half]
-                    flag = None if one == other else left_flag
-                    either(flag, lambda: copy_half(one, at), lambda: copy_half(other, at))
-
-            either(
-                right_flag,
-                lambda: copy_tile(right_tile, rights[0], b * BS),
-                lambda: copy_tile(right_tile, rights[1], b * BS),
-            )
-            left_high_part, left_low_part = split(left_tile[...])
-            right_high_part, right_low_part = split(right_tile[...])
-            lhs = jnp.concatenate([left_high_part, left_low_part], axis=1)
-            both = jnp.concatenate([right_high_part, right_low_part], axis=1)
-            rhs = jnp.concatenate([both, both], axis=0)
-            pair = jnp.dot(lhs, rhs, preferred_element_type=jnp.float32)
-            place = pl.ds(pl.multiple_of(c * BS, BS), BS)
-            total[place, :] = total[place, :] + (pair[:, :BS] + pair[:, BS:])
+            codes = [products[i * BATCH + k] for k in range(BATCH)]
+            for k, code in enumerate(codes):
+                a = code // 1024
+                b = (code // 32) % 32
+                upper = a // (MAXA // 2)
+                at = (a % (MAXA // 2)) * BS
+                for half in range(2):
+
+                    def copy_half(source, at=at, k=k):
+                        copy_tile(left_tile.at[k], source[0], source[1] + at)
+
+                    @pl.when(upper == half)
+                    def _(half=half, copy_half=copy_half):
+                        one, other = lefts[0][half], lefts[1][half]
+                        flag = None if one == other else left_flag
+                        either(flag, lambda: copy_half(one), lambda: copy_half(other))
+
+                either(
+                    right_flag,
+                    lambda b=b, k=k: copy_tile(right_tile.at[k], rights[0], b * BS),
+                    lambda b=b, k=k: copy_tile(right_tile.at[k], rights[1], b * BS),
+                )
+            values = []
+            for k in range(BATCH):
+                left_high_part, left_low_part = split(left_tile[k])
+                right_high_part, right_low_part = split(right_tile[k])
+                lhs = jnp.concatenate([left_high_part, left_low_part], axis=1)
+                both = jnp.concatenate([right_high_part, right_low_part], axis=1)
+                rhs = jnp.concatenate([both, both], axis=0)
+                pair = jnp.dot(lhs, rhs, preferred_element_type=jnp.float32)
+                values.append(pair[:, :BS] + pair[:, BS:])
+            for k, (code, value) in enumerate(zip(codes, values)):
+                place = pl.ds(pl.multiple_of((code % 32) * BS, BS), BS)
+                if k > 0:
+                    value = jnp.where(i * BATCH + k < count, value, 0.0)
+                total[place, :] = total[place, :] + value
             return carry
 
-        lax.fori_loop(0, count, body, 0)
+        for k in range(BATCH - 1):
+            products[count + k] = 0
+        lax.fori_loop(0, (count + BATCH - 1) // BATCH, body, 0)
 
     def run(index, prepare):
         left_flag, right_flag, enable, lefts, rights = passes[index]
@@ -202,8 +211,8 @@
         out_specs=VMEM_SPEC,
         input_output_aliases={} if before is None else {len(operands) - 1: 0},
         scratch_shapes=[
-            pltpu.VMEM((BS, BS), jnp.float32),
-            pltpu.VMEM((BS, BS), jnp.float32),
+            pltpu.VMEM((BATCH, BS, BS), jnp.float32),
+            pltpu.VMEM((BATCH, BS, BS), jnp.float32),
             pltpu.SMEM((PAD, BS), jnp.float32),
             pltpu.SMEM((PAD, BS), jnp.float32),
             pltpu.SMEM((ROWB * COLB,), jnp.int32),
@@ -255,12 +264,11 @@
     left, right, high_far = lax.optimization_barrier((left, right, high_far))
     right_wrap = send(right, route(lambda r, g, x: (r - 2, g, x) if r < 2 else None))
     near = send(left, along_x({1: 0, 2: 1, 3: 2}))
-    total = step_call("step_0", flags, rows, cols, [left, right], ((None, None, None, (WHOLE, WHOLE), (1, 1)),), flops=2000000000)
-    low_far, total = lax.optimization_barrier((low_far, total))
     over_low = send(low_far, along_x({2: 3}))
-    across_high, low_far = lax.optimization_barrier((across_high, low_far))
+    left, across_high, low_far = lax.optimization_barrier((left, across_high, low_far))
     over_high = send(across_high, along_x({2: 3}))
-    right_near, total, across_high = lax.optimization_barrier((right_near, total, across_high))
+    total = step_call("step_0", flags, rows, cols, [left, right], ((None, None, None, (WHOLE, WHOLE), (1, 1)),), flops=10000000000)
+    right_near, total = lax.optimization_barrier((right_near, total))
     right_one = send(
         lax.select(core == 1, right, right_near),
         route(lambda r, g, x: (r ^ 1, g, x)),

time: 136 us -> 139 us (1.022)
  the two profiles are of different devices: /device:TPU:725 before, /device:TPU:797 now
where the time goes in v6:
time: 139 us
  starting transfers between devices  68 us (49%)
  waiting for transfers between devices  51.3 us (37%)
  Pallas kernels  13.4 us (10%)
  other arithmetic  2.99 us (2%)
  between operations  1.68 us (1%)
    ppermute x10, starting transfers between devices, send(): return lax.ppermute(block, AXES, pairs)  68 us
    ppermute x10, waiting for transfers between devices, send(): return lax.ppermute(block, AXES, pairs)  51.3 us
    pallas_call x3, Pallas kernels, step_call(): pl.pallas_call(functools.partial(step_kernel, passes, len(arrays), before...  13.4 us
  transfers between devices with their start and end apart: 10, of which 2 were waited for; matrix products, arithmetic and copies ran while one was open for 1% of the time, Pallas kernels for 6%

profile of v6, /device:TPU:797, one launch (start us, length us, event | category | flops | bytes accessed | tf_op | source)
XLA Modules:
  0.0 138.6 jit_solution(16882188701589083727)
XLA Ops:
  0.8 1.1 fusion
  1.9 0.8 add_convert_fusion
  2.7 0.7 pad_maximum_fusion.1
  3.5 2.1 %collective-permute-start = (f32[520,128]{1,0:T(8,128)S(1)}, f32[520,128]{1,0:T(8,128)S(1)}, u32[]{:S(2)}, u32[]{:S(2)}) collective-permute-start(f32[520,128]{1,0:T(8,128)S(1)} %get-tuple-element.34), channel_id=1, source_target_pairs={{0,3},{1,2},{2,0},{3,1},{4,7},{5,6},{6,4},{7,5},{8,11},{9,10},{10,... | collective-permute-start | bytes 798728 | tf_op jit(solution)/shard_map/ppermute | solution.py:50
  6.3 0.1 add_convert_fusion.1
  6.3 0.1 select_maximum_fusion.refs_4_
  6.4 3.8 %collective-permute-start.6 = (f32[2568,128]{1,0:T(8,128)S(1)}, f32[2568,128]{1,0:T(8,128)S(1)}, u32[]{:S(2)}, u32[]{:S(2)}) collective-permute-start(f32[2568,128]{1,0:T(8,128)S(1)} %select_maximum_fusion.refs_4_), channel_id=1, source_target_pairs={{64,0},{65,1},{66,2},{67,3},{68,4},{69,5},{70,6},{71,7},{72,8},{73... | collective-permute-start | bytes 3944456 | tf_op jit(solution)/shard_map/ppermute | solution.py:50
  10.3 4.4 %collective-permute-start.2 = (f32[520,128]{1,0:T(8,128)}, f32[520,128]{1,0:T(8,128)S(1)}, u32[]{:S(2)}, u32[]{:S(2)}) collective-permute-start(f32[520,128]{1,0:T(8,128)} %get-tuple-element.33), channel_id=1, source_target_pairs={{0,30},{1,31},{2,0},{3,1},{4,2},{5,3},{6,4},{7,5},{8,6},{9,7},{10,... | collective-permute-start | bytes 798728 | tf_op jit(solution)/shard_map/ppermute | solution.py:50
  14.7 0.0 collective-permute-done.refs_4_.refs_9_
  14.7 4.3 %collective-permute-start.4 = (f32[520,128]{1,0:T(8,128)S(1)}, f32[520,128]{1,0:T(8,128)S(1)}, u32[]{:S(2)}, u32[]{:S(2)}) collective-permute-start(f32[520,128]{1,0:T(8,128)S(1)} %collective-permute-done.refs_4_.refs_9_), channel_id=1, source_target_pairs={{2,31},{3,30},{6,3},{7,2},{10,7},{11,6},{14,11},{15,10},{18,15},{1... | collective-permute-start | bytes 798728 | tf_op jit(solution)/shard_map/ppermute | solution.py:50
  19.0 0.1 stack.23
  19.1 1.1 pad_maximum_fusion.refs_3_
  20.2 1.9 %collective-permute-start.7 = (f32[1040,128]{1,0:T(8,128)S(1)}, f32[1040,128]{1,0:T(8,128)S(1)}, u32[]{:S(2)}, u32[]{:S(2)}) collective-permute-start(f32[1040,128]{1,0:T(8,128)S(1)} %pad_maximum_fusion.refs_3_), channel_id=1, source_target_pairs={{1,0},{2,1},{3,2},{5,4},{6,5},{7,6},{9,8},{10,9},{11,10},{13,12},{... | collective-permute-start | bytes 1597448 | tf_op jit(solution)/shard_map/ppermute | solution.py:50
  22.1 0.7 collective-permute-start.1
  22.9 49.9 %collective-permute-done.2.refs_3_.refs_8_ = f32[520,128]{1,0:T(8,128)S(1)} collective-permute-done((f32[520,128]{1,0:T(8,128)}, f32[520,128]{1,0:T(8,128)S(1)}, u32[]{:S(2)}, u32[]{:S(2)}) %collective-permute-start.2) | collective-permute-done | bytes 266272 | tf_op jit(solution)/shard_map/ppermute | solution.py:50
  72.7 3.5 %collective-permute-start.3 = (f32[520,128]{1,0:T(8,128)S(1)}, f32[520,128]{1,0:T(8,128)S(1)}, u32[]{:S(2)}, u32[]{:S(2)}) collective-permute-start(f32[520,128]{1,0:T(8,128)S(1)} %collective-permute-done.2.refs_3_.refs_8_), channel_id=1, source_target_pairs={{2,3},{6,7},{10,11},{14,15},{18,19},{22,23},{26,27},{30,31},{34,35... | collective-permute-start | bytes 798728 | tf_op jit(solution)/shard_map/ppermute | solution.py:50
  76.2 1.4 %collective-permute-done.4.refs_5_.refs_10_ = f32[520,128]{1,0:T(8,128)S(1)} collective-permute-done((f32[520,128]{1,0:T(8,128)S(1)}, f32[520,128]{1,0:T(8,128)S(1)}, u32[]{:S(2)}, u32[]{:S(2)}) %collective-permute-start.4) | collective-permute-done | bytes 266272 | tf_op jit(solution)/shard_map/ppermute | solution.py:50
  77.6 3.1 %collective-permute-start.5 = (f32[520,128]{1,0:T(8,128)S(1)}, f32[520,128]{1,0:T(8,128)S(1)}, u32[]{:S(2)}, u32[]{:S(2)}) collective-permute-start(f32[520,128]{1,0:T(8,128)S(1)} %collective-permute-done.4.refs_5_.refs_10_), channel_id=1, source_target_pairs={{2,3},{6,7},{10,11},{14,15},{18,19},{22,23},{26,27},{30,31},{34,35... | collective-permute-start | bytes 798728 | tf_op jit(solution)/shard_map/ppermute | solution.py:50
  80.8 3.5 %step_0.1.refs_7_ = f32[3072,128]{1,0:T(8,128)} custom-call(s32[5]{0:T(128)S(1)} %convert_element_type.27.refs_0_, s32[24]{0:T(128)S(1)} %bitcast.15, s32[24]{0:T(128)S(1)} %bitcast.18, f32[1040,128]{1,0:T(8,128)S(1)} %pad_maximum_fusion.refs_3_, f32[2568,128]{1,0:T(8,128)S(1)} %select_maximum_fusion.refs_4_), custom_call_target="tpu_custom_call" | custom-call | flops 10000000000 | bytes 1000000 | tf_op jit(solution)/shard_map/step_0/pallas_call | solution.py:207
  84.3 0.2 broadcast_select_fusion
  84.4 43.4 %collective-permute-start.8 = (f32[2568,128]{1,0:T(8,128)S(1)}, f32[2568,128]{1,0:T(8,128)S(1)}, u32[]{:S(2)}, u32[]{:S(2)}) collective-permute-start(f32[2568,128]{1,0:T(8,128)S(1)} %broadcast_select_fusion), channel_id=1, source_target_pairs={{0,32},{1,33},{2,34},{3,35},{4,36},{5,37},{6,38},{7,39},{8,40},{9,... | collective-permute-start | bytes 3944456 | tf_op jit(solution)/shard_map/ppermute | solution.py:50
  127.8 4.8 %step_2.1.refs_12_ = f32[3072,128]{1,0:T(8,128)} custom-call(s32[5]{0:T(128)S(1)} %convert_element_type.27.refs_0_, s32[24]{0:T(128)S(1)} %bitcast.16, s32[24]{0:T(128)S(1)} %bitcast.19, f32[520,128]{1,0:T(8,128)S(1)} %collective-permute-done.2.refs_3_.refs_8_, f32[520,128]{1,0:T(8,128)S(1)} %collective-permute-done.refs_4_.refs_9_, ...), custom_call_target="tpu_custom_call", output_to_operand_aliasing={{}: (7, {})} | custom-call | flops 10000000000 | bytes 1000000 | tf_op jit(solution)/shard_map/step_2/pallas_call | solution.py:207
  132.7 0.7 collective-permute-start.9
  133.5 5.1 %step_1.1 = f32[3072,128]{1,0:T(8,128)} custom-call(s32[5]{0:T(128)S(1)} %convert_element_type.27.refs_0_, s32[24]{0:T(128)S(1)} %bitcast.17, s32[24]{0:T(128)S(1)} %bitcast.20, f32[1040,128]{1,0:T(8,128)S(1)} %collective-permute-done.7.refs_3_, f32[520,128]{1,0:T(8,128)S(1)} %collective-permute-done.3.refs_4_, ...), custom_call_target="tpu_custom_call", output_to_operand_aliasing={{}: (12, {})} | custom-call | flops 100000000 | bytes 1000000 | tf_op jit(solution)/shard_map/step_1/pallas_call | solution.py:207
  (23 shorter events, 0.1 us)
Async XLA Ops:
  0.0 6.2 %copy-start.5 = (s32[1,1,20]{2,1,0:T(1,128)S(1)}, s32[1,1,20]{2,1,0:T(1,128)}, u32[]{:S(2)}) copy-start(s32[1,1,20]{2,1,0:T(1,128)} %param.16) | copy-start | bytes 244
  0.0 6.2 %copy-start.6 = (s32[1,1,20]{2,1,0:T(1,128)S(1)}, s32[1,1,20]{2,1,0:T(1,128)}, u32[]{:S(2)}) copy-start(s32[1,1,20]{2,1,0:T(1,128)} %param.15) | copy-start | bytes 244
  0.0 6.3 %copy-start.4 = (f32[1,1,20,128,128]{4,3,2,1,0:T(8,128)S(1)}, f32[1,1,20,128,128]{4,3,2,1,0:T(8,128)}, u32[]{:S(2)}) copy-start(f32[1,1,20,128,128]{4,3,2,1,0:T(8,128)} %param.14) | copy-start | bytes 3932164
  1.8 1.6 %copy-start.2 = (f32[1,1,4,128,128]{4,3,2,1,0:T(8,128)}, f32[1,1,4,128,128]{4,3,2,1,0:T(8,128)S(1)}, u32[]{:S(2)}) copy-start(f32[1,1,4,128,128]{4,3,2,1,0:T(8,128)S(1)} %get-tuple-element.31) | copy-start | bytes 786436
  1.8 1.6 %copy-start.3 = (f32[1,1,4,128,128]{4,3,2,1,0:T(8,128)}, f32[1,1,4,128,128]{4,3,2,1,0:T(8,128)S(1)}, u32[]{:S(2)}) copy-start(f32[1,1,4,128,128]{4,3,2,1,0:T(8,128)S(1)} %get-tuple-element.32) | copy-start | bytes 786436
  3.5 11.2 %collective-permute-start = (f32[520,128]{1,0:T(8,128)S(1)}, f32[520,128]{1,0:T(8,128)S(1)}, u32[]{:S(2)}, u32[]{:S(2)}) collective-permute-start(f32[520,128]{1,0:T(8,128)S(1)} %get-tuple-element.34), channel_id=1, source_target_pairs={{0,3},{1,2},{2,0},{3,1},{4,7},{5,6},{6,4},{7,5},{8,11},{9,10},{10,... | collective-permute-start | bytes 798728 | tf_op jit(solution)/shard_map/ppermute | solution.py:50
  6.3 74.4 %copy-start = (s32[1,1,24]{2,1,0:T(1,128)S(1)}, s32[1,1,24]{2,1,0:T(1,128)}, u32[]{:S(2)}) copy-start(s32[1,1,24]{2,1,0:T(1,128)} %param.18) | copy-start | bytes 292
  6.3 74.4 %copy-start.1 = (s32[1,1,24]{2,1,0:T(1,128)S(1)}, s32[1,1,24]{2,1,0:T(1,128)}, u32[]{:S(2)}) copy-start(s32[1,1,24]{2,1,0:T(1,128)} %param.19) | copy-start | bytes 292
  6.4 77.8 %collective-permute-start.6 = (f32[2568,128]{1,0:T(8,128)S(1)}, f32[2568,128]{1,0:T(8,128)S(1)}, u32[]{:S(2)}, u32[]{:S(2)}) collective-permute-start(f32[2568,128]{1,0:T(8,128)S(1)} %select_maximum_fusion.refs_4_), channel_id=1, source_target_pairs={{64,0},{65,1},{66,2},{67,3},{68,4},{69,5},{70,6},{71,7},{72,8},{73... | collective-permute-start | bytes 3944456 | tf_op jit(solution)/shard_map/ppermute | solution.py:50
  10.3 62.5 %collective-permute-start.2 = (f32[520,128]{1,0:T(8,128)}, f32[520,128]{1,0:T(8,128)S(1)}, u32[]{:S(2)}, u32[]{:S(2)}) collective-permute-start(f32[520,128]{1,0:T(8,128)} %get-tuple-element.33), channel_id=1, source_target_pairs={{0,30},{1,31},{2,0},{3,1},{4,2},{5,3},{6,4},{7,5},{8,6},{9,7},{10,... | collective-permute-start | bytes 798728 | tf_op jit(solution)/shard_map/ppermute | solution.py:50
  14.7 62.9 %collective-permute-start.4 = (f32[520,128]{1,0:T(8,128)S(1)}, f32[520,128]{1,0:T(8,128)S(1)}, u32[]{:S(2)}, u32[]{:S(2)}) collective-permute-start(f32[520,128]{1,0:T(8,128)S(1)} %collective-permute-done.refs_4_.refs_9_), channel_id=1, source_target_pairs={{2,31},{3,30},{6,3},{7,2},{10,7},{11,6},{14,11},{15,10},{18,15},{1... | collective-permute-start | bytes 798728 | tf_op jit(solution)/shard_map/ppermute | solution.py:50
  20.2 112.5 %collective-permute-start.7 = (f32[1040,128]{1,0:T(8,128)S(1)}, f32[1040,128]{1,0:T(8,128)S(1)}, u32[]{:S(2)}, u32[]{:S(2)}) collective-permute-start(f32[1040,128]{1,0:T(8,128)S(1)} %pad_maximum_fusion.refs_3_), channel_id=1, source_target_pairs={{1,0},{2,1},{3,2},{5,4},{6,5},{7,6},{9,8},{10,9},{11,10},{13,12},{... | collective-permute-start | bytes 1597448 | tf_op jit(solution)/shard_map/ppermute | solution.py:50
  22.1 110.6 %collective-permute-start.1 = (f32[2568,128]{1,0:T(8,128)S(1)}, f32[2568,128]{1,0:T(8,128)S(1)}, u32[]{:S(2)}, u32[]{:S(2)}) collective-permute-start(f32[2568,128]{1,0:T(8,128)S(1)} %select_maximum_fusion.refs_4_), channel_id=1, source_target_pairs={{0,960},{1,961},{2,962},{3,963},{4,964},{5,965},{6,966},{7,967},{8... | collective-permute-start | bytes 3944456 | tf_op jit(solution)/shard_map/ppermute | solution.py:50
  72.7 59.9 %collective-permute-start.3 = (f32[520,128]{1,0:T(8,128)S(1)}, f32[520,128]{1,0:T(8,128)S(1)}, u32[]{:S(2)}, u32[]{:S(2)}) collective-permute-start(f32[520,128]{1,0:T(8,128)S(1)} %collective-permute-done.2.refs_3_.refs_8_), channel_id=1, source_target_pairs={{2,3},{6,7},{10,11},{14,15},{18,19},{22,23},{26,27},{30,31},{34,35... | collective-permute-start | bytes 798728 | tf_op jit(solution)/shard_map/ppermute | solution.py:50
  77.6 55.0 %collective-permute-start.5 = (f32[520,128]{1,0:T(8,128)S(1)}, f32[520,128]{1,0:T(8,128)S(1)}, u32[]{:S(2)}, u32[]{:S(2)}) collective-permute-start(f32[520,128]{1,0:T(8,128)S(1)} %collective-permute-done.4.refs_5_.refs_10_), channel_id=1, source_target_pairs={{2,3},{6,7},{10,11},{14,15},{18,19},{22,23},{26,27},{30,31},{34,35... | collective-permute-start | bytes 798728 | tf_op jit(solution)/shard_map/ppermute | solution.py:50
  84.4 49.0 %collective-permute-start.8 = (f32[2568,128]{1,0:T(8,128)S(1)}, f32[2568,128]{1,0:T(8,128)S(1)}, u32[]{:S(2)}, u32[]{:S(2)}) collective-permute-start(f32[2568,128]{1,0:T(8,128)S(1)} %broadcast_select_fusion), channel_id=1, source_target_pairs={{0,32},{1,33},{2,34},{3,35},{4,36},{5,37},{6,38},{7,39},{8,40},{9,... | collective-permute-start | bytes 3944456 | tf_op jit(solution)/shard_map/ppermute | solution.py:50
  132.7 0.8 collective-permute-start.9

commit v7 on v6

--- a/solution.py
+++ b/solution.py
@@ -262,13 +262,15 @@
     low_far = send(low, route(lambda r, g, x: (r, g - 1, x + 2) if x < 2 else (r, g, x - 2)))
     across_high = send(high_far, to_previous_group({3: 2, 2: 3}))
     left, right, high_far = lax.optimization_barrier((left, right, high_far))
+    left, right, right_near = lax.optimization_barrier((left, right, right_near))
     right_wrap = send(right, route(lambda r, g, x: (r - 2, g, x) if r < 2 else None))
+    total = step_call("step_0", flags, rows, cols, [left, right], ((None, None, None, (WHOLE, WHOLE), (1, 1)),), flops=10000000000)
+    left, total = lax.optimization_barrier((left, total))
     near = send(left, along_x({1: 0, 2: 1, 3: 2}))
+    low_far, total = lax.optimization_barrier((low_far, total))
     over_low = send(low_far, along_x({2: 3}))
-    left, across_high, low_far = lax.optimization_barrier((left, across_high, low_far))
+    across_high, low_far = lax.optimization_barrier((across_high, low_far))
     over_high = send(across_high, along_x({2: 3}))
-    total = step_call("step_0", flags, rows, cols, [left, right], ((None, None, None, (WHOLE, WHOLE), (1, 1)),), flops=10000000000)
-    right_near, total = lax.optimization_barrier((right_near, total))
     right_one = send(
         lax.select(core == 1, right, right_near),
         route(lambda r, g, x: (r ^ 1, g, x)),
@@ -281,9 +283,9 @@
         [low_far, high_far, across_high, right_near],
         ((2, None, 4, (((0, 0), (1, 0)), ((0, 0), (2, 0))), (3, 3)),),
         total,
-        flops=10000000000,
+        flops=3000000000,
     )
-    right_wrap, over_low, over_high, total, near = lax.optimization_barrier((right_wrap, over_low, over_high, total, near))
+    right_wrap, over_low, over_high, total, right_one, near = lax.optimization_barrier((right_wrap, over_low, over_high, total, right_one, near))
     edge = send(right_wrap, route(lambda r, g, x: (r + 1, g, x) if r == N_ROW - 2 else None))
     total = step_call(
         "step_1",

time: 139 us -> 132 us (0.950)
  the two profiles are of different devices: /device:TPU:797 before, /device:TPU:1009 now
where the time goes in v7:
time: 132 us; the launch traced here: 131 us
  waiting for transfers between devices  82.7 us (63%)
  starting transfers between devices  28.9 us (22%)
  Pallas kernels  13.8 us (10%)
  other arithmetic  4.32 us (3%)
  between operations  1.55 us (1%)
    ppermute x10, waiting for transfers between devices, send(): return lax.ppermute(block, AXES, pairs)  82.7 us
    ppermute x10, starting transfers between devices, send(): return lax.ppermute(block, AXES, pairs)  28.9 us
    pallas_call x3, Pallas kernels, step_call(): pl.pallas_call(functools.partial(step_kernel, passes, len(arrays), before...  13.8 us
  transfers between devices with their start and end apart: 10, of which 4 were waited for; matrix products, arithmetic and copies ran while one was open for 2% of the time, Pallas kernels for 5%

profile of v7, /device:TPU:1009, one launch (start us, length us, event | category | flops | bytes accessed | tf_op | source)
XLA Modules:
  0.0 131.5 jit_solution(3866641574529055172)
XLA Ops:
  0.7 0.7 add_convert_fusion.1
  1.4 1.5 %select_maximum_fusion.refs_4_ = f32[2568,128]{1,0:T(8,128)S(1)} fusion(f32[1,41]{1,0:T(1,128)S(1)} %add_convert_fusion.1, f32[2560,128]{1,0:T(8,128)} %bitcast.25), kind=kLoop, calls=%fused_computation | loop fusion | flops 986112 | bytes 2625700 | tf_op jit(solution)/shard_map/concatenate | solution.py:252
  2.9 2.7 %collective-permute-start.1 = (f32[2568,128]{1,0:T(8,128)S(1)}, f32[2568,128]{1,0:T(8,128)S(1)}, u32[]{:S(2)}, u32[]{:S(2)}) collective-permute-start(f32[2568,128]{1,0:T(8,128)S(1)} %select_maximum_fusion.refs_4_), channel_id=1, source_target_pairs={{64,0},{65,1},{66,2},{67,3},{68,4},{69,5},{70,6},{71,7},{72,8},{73... | collective-permute-start | bytes 3944456 | tf_op jit(solution)/shard_map/ppermute | solution.py:50
  6.3 0.1 add_convert_fusion
  6.4 0.9 pad_maximum_fusion.1
  7.3 4.4 %collective-permute-start = (f32[520,128]{1,0:T(8,128)}, f32[520,128]{1,0:T(8,128)S(1)}, u32[]{:S(2)}, u32[]{:S(2)}) collective-permute-start(f32[520,128]{1,0:T(8,128)} %get-tuple-element.44), channel_id=1, source_target_pairs={{0,3},{1,2},{2,0},{3,1},{4,7},{5,6},{6,4},{7,5},{8,11},{9,10},{10,... | collective-permute-start | bytes 798728 | tf_op jit(solution)/shard_map/ppermute | solution.py:50
  11.7 11.3 %collective-permute-start.3 = (f32[520,128]{1,0:T(8,128)}, f32[520,128]{1,0:T(8,128)S(1)}, u32[]{:S(2)}, u32[]{:S(2)}) collective-permute-start(f32[520,128]{1,0:T(8,128)} %get-tuple-element.43), channel_id=1, source_target_pairs={{0,30},{1,31},{2,0},{3,1},{4,2},{5,3},{6,4},{7,5},{8,6},{9,7},{10,... | collective-permute-start | bytes 798728 | tf_op jit(solution)/shard_map/ppermute | solution.py:50
  23.0 0.1 stack.23
  23.2 1.0 pad_maximum_fusion.refs_3_
  24.2 0.7 collective-permute-start.5
  24.9 46.0 %collective-permute-done.1.refs_6_ = f32[2568,128]{1,0:T(8,128)S(1)} collective-permute-done((f32[2568,128]{1,0:T(8,128)S(1)}, f32[2568,128]{1,0:T(8,128)S(1)}, u32[]{:S(2)}, u32[]{:S(2)}) %collective-permute-start.1) | collective-permute-done | bytes 1314848 | tf_op jit(solution)/shard_map/ppermute | solution.py:50
  70.8 1.3 collective-permute-start.2
  72.1 0.2 broadcast_select_fusion
  72.3 4.6 %collective-permute-start.7 = (f32[2568,128]{1,0:T(8,128)S(1)}, f32[2568,128]{1,0:T(8,128)S(1)}, u32[]{:S(2)}, u32[]{:S(2)}) collective-permute-start(f32[2568,128]{1,0:T(8,128)S(1)} %broadcast_select_fusion), channel_id=1, source_target_pairs={{0,32},{1,33},{2,34},{3,35},{4,36},{5,37},{6,38},{7,39},{8,40},{9,... | collective-permute-start | bytes 3944456 | tf_op jit(solution)/shard_map/ppermute | solution.py:50
  76.9 3.5 %step_0.1.refs_7_ = f32[3072,128]{1,0:T(8,128)} custom-call(s32[5]{0:T(128)S(1)} %convert_element_type.27.refs_0_, s32[24]{0:T(128)S(1)} %bitcast.15, s32[24]{0:T(128)S(1)} %bitcast.18, f32[1040,128]{1,0:T(8,128)S(1)} %pad_maximum_fusion.refs_3_, f32[2568,128]{1,0:T(8,128)S(1)} %select_maximum_fusion.refs_4_), custom_call_target="tpu_custom_call" | custom-call | flops 10000000000 | bytes 1000000 | tf_op jit(solution)/shard_map/step_0/pallas_call | solution.py:207
  80.4 1.3 collective-permute-start.8
  81.7 0.7 collective-permute-start.4
  82.4 0.7 collective-permute-start.6
  83.1 3.0 %step_2.1.refs_12_ = f32[3072,128]{1,0:T(8,128)} custom-call(s32[5]{0:T(128)S(1)} %convert_element_type.27.refs_0_, s32[24]{0:T(128)S(1)} %bitcast.16, s32[24]{0:T(128)S(1)} %bitcast.19, f32[520,128]{1,0:T(8,128)S(1)} %collective-permute-done.3.refs_3_.refs_8_, f32[520,128]{1,0:T(8,128)S(1)} %collective-permute-done.refs_4_.refs_9_, ...), custom_call_target="tpu_custom_call", output_to_operand_aliasing={{}: (7, {})} | custom-call | flops 3000000000 | bytes 1000000 | tf_op jit(solution)/shard_map/step_2/pallas_call | solution.py:207
  86.2 11.3 %collective-permute-done.8.refs_3_ = f32[1040,128]{1,0:T(8,128)S(1)} collective-permute-done((f32[1040,128]{1,0:T(8,128)S(1)}, f32[1040,128]{1,0:T(8,128)S(1)}, u32[]{:S(2)}, u32[]{:S(2)}) %collective-permute-start.8) | collective-permute-done | bytes 532512 | tf_op jit(solution)/shard_map/ppermute | solution.py:50
  97.4 19.3 %collective-permute-done.2.refs_11_ = f32[2568,128]{1,0:T(8,128)S(1)} collective-permute-done((f32[2568,128]{1,0:T(8,128)S(1)}, f32[2568,128]{1,0:T(8,128)S(1)}, u32[]{:S(2)}, u32[]{:S(2)}) %collective-permute-start.2) | collective-permute-done | bytes 1314848 | tf_op jit(solution)/shard_map/ppermute | solution.py:50
  116.7 1.3 collective-permute-start.9
  118.0 6.1 %collective-permute-done.9.refs_7_ = f32[2568,128]{1,0:T(8,128)S(1)} collective-permute-done((f32[2568,128]{1,0:T(8,128)S(1)}, f32[2568,128]{1,0:T(8,128)S(1)}, u32[]{:S(2)}, u32[]{:S(2)}) %collective-permute-start.9) | collective-permute-done | bytes 1314848 | tf_op jit(solution)/shard_map/ppermute | solution.py:50
  124.2 7.3 %step_1.1 = f32[3072,128]{1,0:T(8,128)} custom-call(s32[5]{0:T(128)S(1)} %convert_element_type.27.refs_0_, s32[24]{0:T(128)S(1)} %bitcast.17, s32[24]{0:T(128)S(1)} %bitcast.20, f32[1040,128]{1,0:T(8,128)S(1)} %collective-permute-done.8.refs_3_, f32[520,128]{1,0:T(8,128)S(1)} %collective-permute-done.4.refs_4_, ...), custom_call_target="tpu_custom_call", output_to_operand_aliasing={{}: (12, {})} | custom-call | flops 100000000 | bytes 1000000 | tf_op jit(solution)/shard_map/step_1/pallas_call | solution.py:207
  (21 shorter events, 0.1 us)
Async XLA Ops:
  1.4 4.8 %copy-start.4 = (s32[1,1,8]{2,1,0:T(1,128)S(1)}, s32[1,1,8]{2,1,0:T(1,128)}, u32[]{:S(2)}) copy-start(s32[1,1,8]{2,1,0:T(1,128)} %param.12) | copy-start | bytes 100
  1.4 4.9 %copy-start.5 = (s32[1,1,8]{2,1,0:T(1,128)S(1)}, s32[1,1,8]{2,1,0:T(1,128)}, u32[]{:S(2)}) copy-start(s32[1,1,8]{2,1,0:T(1,128)} %param.11) | copy-start | bytes 100
  1.4 4.9 %copy-start.3 = (f32[1,1,8,128,128]{4,3,2,1,0:T(8,128)S(1)}, f32[1,1,8,128,128]{4,3,2,1,0:T(8,128)}, u32[]{:S(2)}) copy-start(f32[1,1,8,128,128]{4,3,2,1,0:T(8,128)} %param.10) | copy-start | bytes 1572868
  2.9 68.0 %collective-permute-start.1 = (f32[2568,128]{1,0:T(8,128)S(1)}, f32[2568,128]{1,0:T(8,128)S(1)}, u32[]{:S(2)}, u32[]{:S(2)}) collective-permute-start(f32[2568,128]{1,0:T(8,128)S(1)} %select_maximum_fusion.refs_4_), channel_id=1, source_target_pairs={{64,0},{65,1},{66,2},{67,3},{68,4},{69,5},{70,6},{71,7},{72,8},{73... | collective-permute-start | bytes 3944456 | tf_op jit(solution)/shard_map/ppermute | solution.py:50
  6.4 0.9 copy-start.2
  7.3 16.9 %collective-permute-start = (f32[520,128]{1,0:T(8,128)}, f32[520,128]{1,0:T(8,128)S(1)}, u32[]{:S(2)}, u32[]{:S(2)}) collective-permute-start(f32[520,128]{1,0:T(8,128)} %get-tuple-element.44), channel_id=1, source_target_pairs={{0,3},{1,2},{2,0},{3,1},{4,7},{5,6},{6,4},{7,5},{8,11},{9,10},{10,... | collective-permute-start | bytes 798728 | tf_op jit(solution)/shard_map/ppermute | solution.py:50
  11.7 70.1 %collective-permute-start.3 = (f32[520,128]{1,0:T(8,128)}, f32[520,128]{1,0:T(8,128)S(1)}, u32[]{:S(2)}, u32[]{:S(2)}) collective-permute-start(f32[520,128]{1,0:T(8,128)} %get-tuple-element.43), channel_id=1, source_target_pairs={{0,30},{1,31},{2,0},{3,1},{4,2},{5,3},{6,4},{7,5},{8,6},{9,7},{10,... | collective-permute-start | bytes 798728 | tf_op jit(solution)/shard_map/ppermute | solution.py:50
  24.1 52.8 %copy-start = (s32[1,1,24]{2,1,0:T(1,128)S(1)}, s32[1,1,24]{2,1,0:T(1,128)}, u32[]{:S(2)}) copy-start(s32[1,1,24]{2,1,0:T(1,128)} %param.18) | copy-start | bytes 292
  24.2 52.8 %copy-start.1 = (s32[1,1,24]{2,1,0:T(1,128)S(1)}, s32[1,1,24]{2,1,0:T(1,128)}, u32[]{:S(2)}) copy-start(s32[1,1,24]{2,1,0:T(1,128)} %param.19) | copy-start | bytes 292
  24.2 58.2 %collective-permute-start.5 = (f32[520,128]{1,0:T(8,128)S(1)}, f32[520,128]{1,0:T(8,128)S(1)}, u32[]{:S(2)}, u32[]{:S(2)}) collective-permute-start(f32[520,128]{1,0:T(8,128)S(1)} %collective-permute-done.refs_4_.refs_9_), channel_id=1, source_target_pairs={{2,31},{3,30},{6,3},{7,2},{10,7},{11,6},{14,11},{15,10},{18,15},{1... | collective-permute-start | bytes 798728 | tf_op jit(solution)/shard_map/ppermute | solution.py:50
  70.8 45.9 %collective-permute-start.2 = (f32[2568,128]{1,0:T(8,128)S(1)}, f32[2568,128]{1,0:T(8,128)S(1)}, u32[]{:S(2)}, u32[]{:S(2)}) collective-permute-start(f32[2568,128]{1,0:T(8,128)S(1)} %select_maximum_fusion.refs_4_), channel_id=1, source_target_pairs={{0,960},{1,961},{2,962},{3,963},{4,964},{5,965},{6,966},{7,967},{8... | collective-permute-start | bytes 3944456 | tf_op jit(solution)/shard_map/ppermute | solution.py:50
  72.3 25.1 %collective-permute-start.7 = (f32[2568,128]{1,0:T(8,128)S(1)}, f32[2568,128]{1,0:T(8,128)S(1)}, u32[]{:S(2)}, u32[]{:S(2)}) collective-permute-start(f32[2568,128]{1,0:T(8,128)S(1)} %broadcast_select_fusion), channel_id=1, source_target_pairs={{0,32},{1,33},{2,34},{3,35},{4,36},{5,37},{6,38},{7,39},{8,40},{9,... | collective-permute-start | bytes 3944456 | tf_op jit(solution)/shard_map/ppermute | solution.py:50
  80.4 17.0 %collective-permute-start.8 = (f32[1040,128]{1,0:T(8,128)S(1)}, f32[1040,128]{1,0:T(8,128)S(1)}, u32[]{:S(2)}, u32[]{:S(2)}) collective-permute-start(f32[1040,128]{1,0:T(8,128)S(1)} %pad_maximum_fusion.refs_3_), channel_id=1, source_target_pairs={{1,0},{2,1},{3,2},{5,4},{6,5},{7,6},{9,8},{10,9},{11,10},{13,12},{... | collective-permute-start | bytes 1597448 | tf_op jit(solution)/shard_map/ppermute | solution.py:50
  81.7 4.4 %collective-permute-start.4 = (f32[520,128]{1,0:T(8,128)S(1)}, f32[520,128]{1,0:T(8,128)S(1)}, u32[]{:S(2)}, u32[]{:S(2)}) collective-permute-start(f32[520,128]{1,0:T(8,128)S(1)} %collective-permute-done.3.refs_3_.refs_8_), channel_id=1, source_target_pairs={{2,3},{6,7},{10,11},{14,15},{18,19},{22,23},{26,27},{30,31},{34,35... | collective-permute-start | bytes 798728 | tf_op jit(solution)/shard_map/ppermute | solution.py:50
  82.4 3.7 %collective-permute-start.6 = (f32[520,128]{1,0:T(8,128)S(1)}, f32[520,128]{1,0:T(8,128)S(1)}, u32[]{:S(2)}, u32[]{:S(2)}) collective-permute-start(f32[520,128]{1,0:T(8,128)S(1)} %collective-permute-done.5.refs_5_.refs_10_), channel_id=1, source_target_pairs={{2,3},{6,7},{10,11},{14,15},{18,19},{22,23},{26,27},{30,31},{34,35... | collective-permute-start | bytes 798728 | tf_op jit(solution)/shard_map/ppermute | solution.py:50
  116.7 7.4 %collective-permute-start.9 = (f32[2568,128]{1,0:T(8,128)S(1)}, f32[2568,128]{1,0:T(8,128)S(1)}, u32[]{:S(2)}, u32[]{:S(2)}) collective-permute-start(f32[2568,128]{1,0:T(8,128)S(1)} %collective-permute-done.2.refs_11_), channel_id=1, source_target_pairs={{960,992},{961,993},{962,994},{963,995},{964,996},{965,997},{966,9... | collective-permute-start | bytes 3944456 | tf_op jit(solution)/shard_map/ppermute | solution.py:50

commit v8 on v7

--- a/solution.py
+++ b/solution.py
@@ -36,6 +36,12 @@
                 r, g, x = target
                 pairs.append((row * N_COL + col, (r % N_ROW) * N_COL + (g % N_GROUP) * GROUP + x))
     return pairs
+
+
+def ring(row, group, x):
+    if row >= 2:
+        return row - 2, group, x
+    return (N_ROW - 1, group ^ 1, x) if row == 1 else None
 
 
 def along_x(moves):
@@ -256,25 +262,26 @@
     last_chip = row // 2 == N_ROW // 2 - 1
     rows, cols = out_rows[0, 0], out_cols[0, 0]
 
-    flags = jnp.stack([x == 3, (core == 1) & last_chip, x >= 2, last_chip, ~last_chip]).astype(jnp.int32)
+    flags = jnp.stack([x == 3, (core == 1) & last_chip, x >= 2, last_chip, ~last_chip, core == 1]).astype(jnp.int32)
     high_far = send(high, along_x({0: 3, 1: 2, 2: 0, 3: 1}))
-    right_near = send(right, route(lambda r, g, x: (r - 2, g, x) if r >= 2 else None))
+    right_near = send(right, route(ring))
     low_far = send(low, route(lambda r, g, x: (r, g - 1, x + 2) if x < 2 else (r, g, x - 2)))
     across_high = send(high_far, to_previous_group({3: 2, 2: 3}))
     left, right, high_far = lax.optimization_barrier((left, right, high_far))
     left, right, right_near = lax.optimization_barrier((left, right, right_near))
-    right_wrap = send(right, route(lambda r, g, x: (r - 2, g, x) if r < 2 else None))
-    total = step_call("step_0", flags, rows, cols, [left, right], ((None, None, None, (WHOLE, WHOLE), (1, 1)),), flops=10000000000)
-    left, total = lax.optimization_barrier((left, total))
+    right_wrap = send(right, route(lambda r, g, x: (N_ROW - 2, g, x) if r == 0 else None))
+    right_cross = send(right_near, route(lambda r, g, x: (r, g ^ 1, x) if r == N_ROW - 1 else None))
+    right_one = send(
+        lax.select(core == 1, right, right_near),
+        route(lambda r, g, x: (r ^ 1, g, x)),
+    )
+    total = step_call("step_0", flags, rows, cols, [left, right], ((None, None, None, (WHOLE, WHOLE), (1, 1)),), flops=15000000000)
+    left, total, right_one = lax.optimization_barrier((left, total, right_one))
     near = send(left, along_x({1: 0, 2: 1, 3: 2}))
     low_far, total = lax.optimization_barrier((low_far, total))
     over_low = send(low_far, along_x({2: 3}))
     across_high, low_far = lax.optimization_barrier((across_high, low_far))
     over_high = send(across_high, along_x({2: 3}))
-    right_one = send(
-        lax.select(core == 1, right, right_near),
-        route(lambda r, g, x: (r ^ 1, g, x)),
-    )
     total = step_call(
         "step_2",
         flags,
@@ -285,17 +292,17 @@
         total,
         flops=3000000000,
     )
-    right_wrap, over_low, over_high, total, right_one, near = lax.optimization_barrier((right_wrap, over_low, over_high, total, right_one, near))
+    right_wrap, over_low, over_high, total, near, right_cross = lax.optimization_barrier((right_wrap, over_low, over_high, total, near, right_cross))
     edge = send(right_wrap, route(lambda r, g, x: (r + 1, g, x) if r == N_ROW - 2 else None))
     total = step_call(
         "step_1",
         flags,
         rows,
         cols,
-        [near, over_low, over_high, right_one, edge, low_far, high_far, across_high, right_wrap],
+        [near, over_low, over_high, right_one, edge, low_far, high_far, across_high, right_wrap, right_cross],
         (
             (0, 1, None, (((0, 0), (0, LEFT_HALF)), ((1, 0), (2, 0))), (3, 4)),
-            (2, None, 3, (((5, 0), (6, 0)), ((5, 0), (7, 0))), (8, 8)),
+            (2, 5, 3, (((5, 0), (6, 0)), ((5, 0), (7, 0))), (8, 9)),
         ),
         total,
     )

time: 132 us -> 125 us (0.947)
  the two profiles are of different devices: /device:TPU:1009 before, /device:TPU:993 now
where the time goes in v8:
time: 125 us
  starting transfers between devices  55.8 us (45%)
  waiting for transfers between devices  49.1 us (39%)
  Pallas kernels  13.6 us (11%)
  other arithmetic  4.33 us (3%)
  between operations  1.56 us (1%)
    ppermute x11, starting transfers between devices, send(): return lax.ppermute(block, AXES, pairs)  55.8 us
    ppermute x11, waiting for transfers between devices, send(): return lax.ppermute(block, AXES, pairs)  49.1 us
    pallas_call x3, Pallas kernels, step_call(): pl.pallas_call(functools.partial(step_kernel, passes, len(arrays), before...  13.6 us
  transfers between devices with their start and end apart: 11, of which 3 were waited for; matrix products, arithmetic and copies ran while one was open for 2% of the time, Pallas kernels for 5%

profile of v8, /device:TPU:993, one launch (start us, length us, event | category | flops | bytes accessed | tf_op | source)
XLA Modules:
  0.0 124.5 jit_solution(6230385782914006918)
XLA Ops:
  0.7 0.7 add_convert_fusion.1
  1.4 1.5 %select_maximum_fusion.refs_4_ = f32[2568,128]{1,0:T(8,128)S(1)} fusion(f32[1,41]{1,0:T(1,128)S(1)} %add_convert_fusion.1, f32[2560,128]{1,0:T(8,128)} %bitcast.26), kind=kLoop, calls=%fused_computation | loop fusion | flops 986112 | bytes 2625700 | tf_op jit(solution)/shard_map/concatenate | solution.py:258
  2.9 2.6 %collective-permute-start.1 = (f32[2568,128]{1,0:T(8,128)S(1)}, f32[2568,128]{1,0:T(8,128)S(1)}, u32[]{:S(2)}, u32[]{:S(2)}) collective-permute-start(f32[2568,128]{1,0:T(8,128)S(1)} %select_maximum_fusion.refs_4_), channel_id=1, source_target_pairs={{32,996},{33,997},{34,998},{35,999},{36,992},{37,993},{38,994},{39... | collective-permute-start | bytes 3944456 | tf_op jit(solution)/shard_map/ppermute | solution.py:56
  6.2 0.1 add_convert_fusion
  6.3 0.9 pad_maximum_fusion.1
  7.2 4.4 %collective-permute-start = (f32[520,128]{1,0:T(8,128)}, f32[520,128]{1,0:T(8,128)S(1)}, u32[]{:S(2)}, u32[]{:S(2)}) collective-permute-start(f32[520,128]{1,0:T(8,128)} %get-tuple-element.46), channel_id=1, source_target_pairs={{0,3},{1,2},{2,0},{3,1},{4,7},{5,6},{6,4},{7,5},{8,11},{9,10},{10,... | collective-permute-start | bytes 798728 | tf_op jit(solution)/shard_map/ppermute | solution.py:56
  11.6 11.5 %collective-permute-start.3 = (f32[520,128]{1,0:T(8,128)}, f32[520,128]{1,0:T(8,128)S(1)}, u32[]{:S(2)}, u32[]{:S(2)}) collective-permute-start(f32[520,128]{1,0:T(8,128)} %get-tuple-element.45), channel_id=1, source_target_pairs={{0,30},{1,31},{2,0},{3,1},{4,2},{5,3},{6,4},{7,5},{8,6},{9,7},{10,... | collective-permute-start | bytes 798728 | tf_op jit(solution)/shard_map/ppermute | solution.py:56
  23.2 0.1 stack.27
  23.3 1.0 pad_maximum_fusion.refs_3_
  24.3 0.7 collective-permute-start.6
  25.0 21.9 %collective-permute-done.1.refs_6_ = f32[2568,128]{1,0:T(8,128)S(1)} collective-permute-done((f32[2568,128]{1,0:T(8,128)S(1)}, f32[2568,128]{1,0:T(8,128)S(1)}, u32[]{:S(2)}, u32[]{:S(2)}) %collective-permute-start.1) | collective-permute-done | bytes 1314848 | tf_op jit(solution)/shard_map/ppermute | solution.py:56
  46.9 0.7 collective-permute-start.2
  47.7 0.2 broadcast_select_fusion
  47.8 1.9 %collective-permute-start.9 = (f32[2568,128]{1,0:T(8,128)S(1)}, f32[2568,128]{1,0:T(8,128)S(1)}, u32[]{:S(2)}, u32[]{:S(2)}) collective-permute-start(f32[2568,128]{1,0:T(8,128)S(1)} %collective-permute-done.1.refs_6_), channel_id=1, source_target_pairs={{992,996},{993,997},{994,998},{995,999},{996,992},{997,993},{998,9... | collective-permute-start | bytes 3944456 | tf_op jit(solution)/shard_map/ppermute | solution.py:56
  49.8 30.0 %collective-permute-start.4 = (f32[2568,128]{1,0:T(8,128)S(1)}, f32[2568,128]{1,0:T(8,128)S(1)}, u32[]{:S(2)}, u32[]{:S(2)}) collective-permute-start(f32[2568,128]{1,0:T(8,128)S(1)} %broadcast_select_fusion), channel_id=1, source_target_pairs={{0,32},{1,33},{2,34},{3,35},{4,36},{5,37},{6,38},{7,39},{8,40},{9,... | collective-permute-start | bytes 3944456 | tf_op jit(solution)/shard_map/ppermute | solution.py:56
  79.8 3.5 %step_0.1.refs_7_ = f32[3072,128]{1,0:T(8,128)} custom-call(s32[6]{0:T(128)S(1)} %convert_element_type.27.refs_0_, s32[24]{0:T(128)S(1)} %bitcast.16, s32[24]{0:T(128)S(1)} %bitcast.19, f32[1040,128]{1,0:T(8,128)S(1)} %pad_maximum_fusion.refs_3_, f32[2568,128]{1,0:T(8,128)S(1)} %select_maximum_fusion.refs_4_), custom_call_target="tpu_custom_call" | custom-call | flops 15000000512 | bytes 1000000 | tf_op jit(solution)/shard_map/step_0/pallas_call | solution.py:213
  83.3 1.3 %collective-permute-start.8 = (f32[1040,128]{1,0:T(8,128)S(1)}, f32[1040,128]{1,0:T(8,128)S(1)}, u32[]{:S(2)}, u32[]{:S(2)}) collective-permute-start(f32[1040,128]{1,0:T(8,128)S(1)} %pad_maximum_fusion.refs_3_), channel_id=1, source_target_pairs={{1,0},{2,1},{3,2},{5,4},{6,5},{7,6},{9,8},{10,9},{11,10},{13,12},{... | collective-permute-start | bytes 1597448 | tf_op jit(solution)/shard_map/ppermute | solution.py:56
  84.6 0.7 collective-permute-start.5
  85.3 0.7 collective-permute-start.7
  86.0 3.0 %step_2.1.refs_13_ = f32[3072,128]{1,0:T(8,128)} custom-call(s32[6]{0:T(128)S(1)} %convert_element_type.27.refs_0_, s32[24]{0:T(128)S(1)} %bitcast.17, s32[24]{0:T(128)S(1)} %bitcast.20, f32[520,128]{1,0:T(8,128)S(1)} %collective-permute-done.3.refs_3_.refs_8_, f32[520,128]{1,0:T(8,128)S(1)} %collective-permute-done.refs_4_.refs_9_, ...), custom_call_target="tpu_custom_call", output_to_operand_aliasing={{}: (7, {})} | custom-call | flops 3000000000 | bytes 1000000 | tf_op jit(solution)/shard_map/step_2/pallas_call | solution.py:213
  89.1 14.8 %collective-permute-done.9.refs_12_ = f32[2568,128]{1,0:T(8,128)S(1)} collective-permute-done((f32[2568,128]{1,0:T(8,128)S(1)}, f32[2568,128]{1,0:T(8,128)S(1)}, u32[]{:S(2)}, u32[]{:S(2)}) %collective-permute-start.9) | collective-permute-done | bytes 1314848 | tf_op jit(solution)/shard_map/ppermute | solution.py:56
  103.8 1.3 %collective-permute-start.10 = (f32[2568,128]{1,0:T(8,128)S(1)}, f32[2568,128]{1,0:T(8,128)S(1)}, u32[]{:S(2)}, u32[]{:S(2)}) collective-permute-start(f32[2568,128]{1,0:T(8,128)S(1)} %collective-permute-done.2.refs_11_), channel_id=1, source_target_pairs={{960,992},{961,993},{962,994},{963,995},{964,996},{965,997},{966,9... | collective-permute-start | bytes 3944456 | tf_op jit(solution)/shard_map/ppermute | solution.py:56
  105.1 12.4 %collective-permute-done.10.refs_7_ = f32[2568,128]{1,0:T(8,128)S(1)} collective-permute-done((f32[2568,128]{1,0:T(8,128)S(1)}, f32[2568,128]{1,0:T(8,128)S(1)}, u32[]{:S(2)}, u32[]{:S(2)}) %collective-permute-start.10) | collective-permute-done | bytes 1314848 | tf_op jit(solution)/shard_map/ppermute | solution.py:56
  117.5 7.1 %step_1.1 = f32[3072,128]{1,0:T(8,128)} custom-call(s32[6]{0:T(128)S(1)} %convert_element_type.27.refs_0_, s32[24]{0:T(128)S(1)} %bitcast.18, s32[24]{0:T(128)S(1)} %bitcast.21, f32[1040,128]{1,0:T(8,128)S(1)} %collective-permute-done.8.refs_3_, f32[520,128]{1,0:T(8,128)S(1)} %collective-permute-done.5.refs_4_, ...), custom_call_target="tpu_custom_call", output_to_operand_aliasing={{}: (13, {})} | custom-call | flops 100000000 | bytes 1000000 | tf_op jit(solution)/shard_map/step_1/pallas_call | solution.py:213
  (23 shorter events, 0.1 us)
Async XLA Ops:
  1.4 4.8 %copy-start.4 = (s32[1,1,8]{2,1,0:T(1,128)S(1)}, s32[1,1,8]{2,1,0:T(1,128)}, u32[]{:S(2)}) copy-start(s32[1,1,8]{2,1,0:T(1,128)} %param.12) | copy-start | bytes 100
  1.4 4.8 %copy-start.5 = (s32[1,1,8]{2,1,0:T(1,128)S(1)}, s32[1,1,8]{2,1,0:T(1,128)}, u32[]{:S(2)}) copy-start(s32[1,1,8]{2,1,0:T(1,128)} %param.11) | copy-start | bytes 100
  1.4 4.9 %copy-start.3 = (f32[1,1,8,128,128]{4,3,2,1,0:T(8,128)S(1)}, f32[1,1,8,128,128]{4,3,2,1,0:T(8,128)}, u32[]{:S(2)}) copy-start(f32[1,1,8,128,128]{4,3,2,1,0:T(8,128)} %param.10) | copy-start | bytes 1572868
  2.9 44.0 %collective-permute-start.1 = (f32[2568,128]{1,0:T(8,128)S(1)}, f32[2568,128]{1,0:T(8,128)S(1)}, u32[]{:S(2)}, u32[]{:S(2)}) collective-permute-start(f32[2568,128]{1,0:T(8,128)S(1)} %select_maximum_fusion.refs_4_), channel_id=1, source_target_pairs={{32,996},{33,997},{34,998},{35,999},{36,992},{37,993},{38,994},{39... | collective-permute-start | bytes 3944456 | tf_op jit(solution)/shard_map/ppermute | solution.py:56
  6.3 0.9 copy-start.2
  7.2 17.1 %collective-permute-start = (f32[520,128]{1,0:T(8,128)}, f32[520,128]{1,0:T(8,128)S(1)}, u32[]{:S(2)}, u32[]{:S(2)}) collective-permute-start(f32[520,128]{1,0:T(8,128)} %get-tuple-element.46), channel_id=1, source_target_pairs={{0,3},{1,2},{2,0},{3,1},{4,7},{5,6},{6,4},{7,5},{8,11},{9,10},{10,... | collective-permute-start | bytes 798728 | tf_op jit(solution)/shard_map/ppermute | solution.py:56
  11.6 73.1 %collective-permute-start.3 = (f32[520,128]{1,0:T(8,128)}, f32[520,128]{1,0:T(8,128)S(1)}, u32[]{:S(2)}, u32[]{:S(2)}) collective-permute-start(f32[520,128]{1,0:T(8,128)} %get-tuple-element.45), channel_id=1, source_target_pairs={{0,30},{1,31},{2,0},{3,1},{4,2},{5,3},{6,4},{7,5},{8,6},{9,7},{10,... | collective-permute-start | bytes 798728 | tf_op jit(solution)/shard_map/ppermute | solution.py:56
  24.3 55.5 %copy-start = (s32[1,1,24]{2,1,0:T(1,128)S(1)}, s32[1,1,24]{2,1,0:T(1,128)}, u32[]{:S(2)}) copy-start(s32[1,1,24]{2,1,0:T(1,128)} %param.18) | copy-start | bytes 292
  24.3 55.5 %copy-start.1 = (s32[1,1,24]{2,1,0:T(1,128)S(1)}, s32[1,1,24]{2,1,0:T(1,128)}, u32[]{:S(2)}) copy-start(s32[1,1,24]{2,1,0:T(1,128)} %param.19) | copy-start | bytes 292
  24.3 61.0 %collective-permute-start.6 = (f32[520,128]{1,0:T(8,128)S(1)}, f32[520,128]{1,0:T(8,128)S(1)}, u32[]{:S(2)}, u32[]{:S(2)}) collective-permute-start(f32[520,128]{1,0:T(8,128)S(1)} %collective-permute-done.refs_4_.refs_9_), channel_id=1, source_target_pairs={{2,31},{3,30},{6,3},{7,2},{10,7},{11,6},{14,11},{15,10},{18,15},{1... | collective-permute-start | bytes 798728 | tf_op jit(solution)/shard_map/ppermute | solution.py:56
  46.9 42.1 %collective-permute-start.2 = (f32[2568,128]{1,0:T(8,128)S(1)}, f32[2568,128]{1,0:T(8,128)S(1)}, u32[]{:S(2)}, u32[]{:S(2)}) collective-permute-start(f32[2568,128]{1,0:T(8,128)S(1)} %select_maximum_fusion.refs_4_), channel_id=1, source_target_pairs={{0,960},{1,961},{2,962},{3,963},{4,964},{5,965},{6,966},{7,967},{8... | collective-permute-start | bytes 3944456 | tf_op jit(solution)/shard_map/ppermute | solution.py:56
  47.8 56.0 %collective-permute-start.9 = (f32[2568,128]{1,0:T(8,128)S(1)}, f32[2568,128]{1,0:T(8,128)S(1)}, u32[]{:S(2)}, u32[]{:S(2)}) collective-permute-start(f32[2568,128]{1,0:T(8,128)S(1)} %collective-permute-done.1.refs_6_), channel_id=1, source_target_pairs={{992,996},{993,997},{994,998},{995,999},{996,992},{997,993},{998,9... | collective-permute-start | bytes 3944456 | tf_op jit(solution)/shard_map/ppermute | solution.py:56
  49.8 33.6 %collective-permute-start.4 = (f32[2568,128]{1,0:T(8,128)S(1)}, f32[2568,128]{1,0:T(8,128)S(1)}, u32[]{:S(2)}, u32[]{:S(2)}) collective-permute-start(f32[2568,128]{1,0:T(8,128)S(1)} %broadcast_select_fusion), channel_id=1, source_target_pairs={{0,32},{1,33},{2,34},{3,35},{4,36},{5,37},{6,38},{7,39},{8,40},{9,... | collective-permute-start | bytes 3944456 | tf_op jit(solution)/shard_map/ppermute | solution.py:56
  83.3 20.5 %collective-permute-start.8 = (f32[1040,128]{1,0:T(8,128)S(1)}, f32[1040,128]{1,0:T(8,128)S(1)}, u32[]{:S(2)}, u32[]{:S(2)}) collective-permute-start(f32[1040,128]{1,0:T(8,128)S(1)} %pad_maximum_fusion.refs_3_), channel_id=1, source_target_pairs={{1,0},{2,1},{3,2},{5,4},{6,5},{7,6},{9,8},{10,9},{11,10},{13,12},{... | collective-permute-start | bytes 1597448 | tf_op jit(solution)/shard_map/ppermute | solution.py:56
  84.6 19.2 %collective-permute-start.5 = (f32[520,128]{1,0:T(8,128)S(1)}, f32[520,128]{1,0:T(8,128)S(1)}, u32[]{:S(2)}, u32[]{:S(2)}) collective-permute-start(f32[520,128]{1,0:T(8,128)S(1)} %collective-permute-done.3.refs_3_.refs_8_), channel_id=1, source_target_pairs={{2,3},{6,7},{10,11},{14,15},{18,19},{22,23},{26,27},{30,31},{34,35... | collective-permute-start | bytes 798728 | tf_op jit(solution)/shard_map/ppermute | solution.py:56
  85.3 18.5 %collective-permute-start.7 = (f32[520,128]{1,0:T(8,128)S(1)}, f32[520,128]{1,0:T(8,128)S(1)}, u32[]{:S(2)}, u32[]{:S(2)}) collective-permute-start(f32[520,128]{1,0:T(8,128)S(1)} %collective-permute-done.6.refs_5_.refs_10_), channel_id=1, source_target_pairs={{2,3},{6,7},{10,11},{14,15},{18,19},{22,23},{26,27},{30,31},{34,35... | collective-permute-start | bytes 798728 | tf_op jit(solution)/shard_map/ppermute | solution.py:56
  103.8 13.7 %collective-permute-start.10 = (f32[2568,128]{1,0:T(8,128)S(1)}, f32[2568,128]{1,0:T(8,128)S(1)}, u32[]{:S(2)}, u32[]{:S(2)}) collective-permute-start(f32[2568,128]{1,0:T(8,128)S(1)} %collective-permute-done.2.refs_11_), channel_id=1, source_target_pairs={{960,992},{961,993},{962,994},{963,995},{964,996},{965,997},{966,9... | collective-permute-start | bytes 3944456 | tf_op jit(solution)/shard_map/ppermute | solution.py:56

commit v9 on v8

--- a/solution.py
+++ b/solution.py
@@ -265,11 +265,11 @@
     flags = jnp.stack([x == 3, (core == 1) & last_chip, x >= 2, last_chip, ~last_chip, core == 1]).astype(jnp.int32)
     high_far = send(high, along_x({0: 3, 1: 2, 2: 0, 3: 1}))
     right_near = send(right, route(ring))
+    right_wrap = send(right, route(lambda r, g, x: (N_ROW - 2, g, x) if r == 0 else None))
     low_far = send(low, route(lambda r, g, x: (r, g - 1, x + 2) if x < 2 else (r, g, x - 2)))
     across_high = send(high_far, to_previous_group({3: 2, 2: 3}))
     left, right, high_far = lax.optimization_barrier((left, right, high_far))
     left, right, right_near = lax.optimization_barrier((left, right, right_near))
-    right_wrap = send(right, route(lambda r, g, x: (N_ROW - 2, g, x) if r == 0 else None))
     right_cross = send(right_near, route(lambda r, g, x: (r, g ^ 1, x) if r == N_ROW - 1 else None))
     right_one = send(
         lax.select(core == 1, right, right_near),

time: 125 us -> 127 us (1.016)
  the two profiles are of different devices: /device:TPU:993 before, /device:TPU:30 now
where the time goes in v9:
time: 127 us
  starting transfers between devices  59 us (46%)
  waiting for transfers between devices  46.6 us (37%)
  Pallas kernels  13.9 us (11%)
  other arithmetic  5.62 us (4%)
  between operations  1.58 us (1%)
    ppermute x11, starting transfers between devices, send(): return lax.ppermute(block, AXES, pairs)  59 us
    ppermute x11, waiting for transfers between devices, send(): return lax.ppermute(block, AXES, pairs)  46.6 us
    pallas_call x3, Pallas kernels, step_call(): pl.pallas_call(functools.partial(step_kernel, passes, len(arrays), before...  13.9 us
  transfers between devices with their start and end apart: 11, of which 2 were waited for; matrix products, arithmetic and copies ran while one was open for 3% of the time, Pallas kernels for 7%

profile of v9, /device:TPU:30, one launch (start us, length us, event | category | flops | bytes accessed | tf_op | source)
XLA Modules:
  0.0 126.9 jit_solution(15279648145420116548)
XLA Ops:
  0.7 0.7 add_convert_fusion
  1.4 1.5 %select_maximum_fusion.refs_4_ = f32[2568,128]{1,0:T(8,128)S(1)} fusion(f32[1,41]{1,0:T(1,128)S(1)} %add_convert_fusion, f32[2560,128]{1,0:T(8,128)} %bitcast.26), kind=kLoop, calls=%fused_computation | loop fusion | flops 986112 | bytes 2625700 | tf_op jit(solution)/shard_map/concatenate | solution.py:258
  2.9 1.3 %collective-permute-start.3 = (f32[2568,128]{1,0:T(8,128)S(1)}, f32[2568,128]{1,0:T(8,128)}, u32[]{:S(2)}, u32[]{:S(2)}) collective-permute-start(f32[2568,128]{1,0:T(8,128)S(1)} %select_maximum_fusion.refs_4_), channel_id=1, source_target_pairs={{32,996},{33,997},{34,998},{35,999},{36,992},{37,993},{38,994},{39... | collective-permute-start | bytes 3944456 | tf_op jit(solution)/shard_map/ppermute | solution.py:56
  4.8 0.1 add_convert_fusion.1
  5.0 0.9 pad_maximum_fusion.1
  5.9 3.3 %collective-permute-start.2 = (f32[520,128]{1,0:T(8,128)}, f32[520,128]{1,0:T(8,128)S(1)}, u32[]{:S(2)}, u32[]{:S(2)}) collective-permute-start(f32[520,128]{1,0:T(8,128)} %get-tuple-element.45), channel_id=1, source_target_pairs={{0,3},{1,2},{2,0},{3,1},{4,7},{5,6},{6,4},{7,5},{8,11},{9,10},{10,... | collective-permute-start | bytes 798728 | tf_op jit(solution)/shard_map/ppermute | solution.py:56
  9.2 28.3 %collective-permute-start = (f32[2568,128]{1,0:T(8,128)S(1)}, f32[2568,128]{1,0:T(8,128)S(1)}, u32[]{:S(2)}, u32[]{:S(2)}) collective-permute-start(f32[2568,128]{1,0:T(8,128)S(1)} %select_maximum_fusion.refs_4_), channel_id=1, source_target_pairs={{0,960},{1,961},{2,962},{3,963},{4,964},{5,965},{6,966},{7,967},{8... | collective-permute-start | bytes 3944456 | tf_op jit(solution)/shard_map/ppermute | solution.py:56
  37.5 3.4 %collective-permute-start.1 = (f32[520,128]{1,0:T(8,128)}, f32[520,128]{1,0:T(8,128)S(1)}, u32[]{:S(2)}, u32[]{:S(2)}) collective-permute-start(f32[520,128]{1,0:T(8,128)} %get-tuple-element.46), channel_id=1, source_target_pairs={{0,30},{1,31},{2,0},{3,1},{4,2},{5,3},{6,4},{7,5},{8,6},{9,7},{10,... | collective-permute-start | bytes 798728 | tf_op jit(solution)/shard_map/ppermute | solution.py:56
  40.9 0.1 stack.27
  41.0 1.0 pad_maximum_fusion.refs_3_
  42.0 0.0 copy-start
  42.1 13.6 %collective-permute-start.6 = (f32[520,128]{1,0:T(8,128)S(1)}, f32[520,128]{1,0:T(8,128)S(1)}, u32[]{:S(2)}, u32[]{:S(2)}) collective-permute-start(f32[520,128]{1,0:T(8,128)S(1)} %collective-permute-done.2.refs_4_.refs_9_), channel_id=1, source_target_pairs={{2,31},{3,30},{6,3},{7,2},{10,7},{11,6},{14,11},{15,10},{18,15},{1... | collective-permute-start | bytes 798728 | tf_op jit(solution)/shard_map/ppermute | solution.py:56
  55.7 0.7 collective-permute-start.9
  56.4 1.5 %broadcast_select_fusion = f32[2568,128]{1,0:T(8,128)S(1)} fusion(f32[2568,128]{1,0:T(8,128)S(1)} %select_maximum_fusion.refs_4_, f32[2568,128]{1,0:T(8,128)} %collective-permute-done.3.refs_6_, pred[]{:T(512)} %eq.15), kind=kLoop, calls=%fused_computation.2 | loop fusion | flops 328704 | bytes 3944449 | tf_op jit(solution)/shard_map/select_n | solution.py:275
  57.9 1.9 %collective-permute-start.4 = (f32[2568,128]{1,0:T(8,128)S(1)}, f32[2568,128]{1,0:T(8,128)S(1)}, u32[]{:S(2)}, u32[]{:S(2)}) collective-permute-start(f32[2568,128]{1,0:T(8,128)S(1)} %broadcast_select_fusion), channel_id=1, source_target_pairs={{0,32},{1,33},{2,34},{3,35},{4,36},{5,37},{6,38},{7,39},{8,40},{9,... | collective-permute-start | bytes 3944456 | tf_op jit(solution)/shard_map/ppermute | solution.py:56
  59.8 3.1 %step_0.1.refs_7_ = f32[3072,128]{1,0:T(8,128)} custom-call(s32[6]{0:T(128)S(1)} %convert_element_type.27.refs_0_, s32[24]{0:T(128)S(1)} %bitcast.16, s32[24]{0:T(128)S(1)} %bitcast.19, f32[1040,128]{1,0:T(8,128)S(1)} %pad_maximum_fusion.refs_3_, f32[2568,128]{1,0:T(8,128)S(1)} %select_maximum_fusion.refs_4_), custom_call_target="tpu_custom_call" | custom-call | flops 15000000512 | bytes 1000000 | tf_op jit(solution)/shard_map/step_0/pallas_call | solution.py:213
  63.0 3.1 %collective-permute-start.8 = (f32[1040,128]{1,0:T(8,128)S(1)}, f32[1040,128]{1,0:T(8,128)S(1)}, u32[]{:S(2)}, u32[]{:S(2)}) collective-permute-start(f32[1040,128]{1,0:T(8,128)S(1)} %pad_maximum_fusion.refs_3_), channel_id=1, source_target_pairs={{1,0},{2,1},{3,2},{5,4},{6,5},{7,6},{9,8},{10,9},{11,10},{13,12},{... | collective-permute-start | bytes 1597448 | tf_op jit(solution)/shard_map/ppermute | solution.py:56
  66.1 43.3 %collective-permute-done.1.refs_3_.refs_8_ = f32[520,128]{1,0:T(8,128)S(1)} collective-permute-done((f32[520,128]{1,0:T(8,128)}, f32[520,128]{1,0:T(8,128)S(1)}, u32[]{:S(2)}, u32[]{:S(2)}) %collective-permute-start.1) | collective-permute-done | bytes 266272 | tf_op jit(solution)/shard_map/ppermute | solution.py:56
  109.4 1.3 %collective-permute-start.5 = (f32[520,128]{1,0:T(8,128)S(1)}, f32[520,128]{1,0:T(8,128)S(1)}, u32[]{:S(2)}, u32[]{:S(2)}) collective-permute-start(f32[520,128]{1,0:T(8,128)S(1)} %collective-permute-done.1.refs_3_.refs_8_), channel_id=1, source_target_pairs={{2,3},{6,7},{10,11},{14,15},{18,19},{22,23},{26,27},{30,31},{34,35... | collective-permute-start | bytes 798728 | tf_op jit(solution)/shard_map/ppermute | solution.py:56
  110.7 1.3 %collective-permute-start.7 = (f32[520,128]{1,0:T(8,128)S(1)}, f32[520,128]{1,0:T(8,128)S(1)}, u32[]{:S(2)}, u32[]{:S(2)}) collective-permute-start(f32[520,128]{1,0:T(8,128)S(1)} %collective-permute-done.6.refs_5_.refs_10_), channel_id=1, source_target_pairs={{2,3},{6,7},{10,11},{14,15},{18,19},{22,23},{26,27},{30,31},{34,35... | collective-permute-start | bytes 798728 | tf_op jit(solution)/shard_map/ppermute | solution.py:56
  112.0 5.2 %step_2.1.refs_13_ = f32[3072,128]{1,0:T(8,128)} custom-call(s32[6]{0:T(128)S(1)} %convert_element_type.27.refs_0_, s32[24]{0:T(128)S(1)} %bitcast.17, s32[24]{0:T(128)S(1)} %bitcast.20, f32[520,128]{1,0:T(8,128)S(1)} %collective-permute-done.1.refs_3_.refs_8_, ...), custom_call_target="tpu_custom_call", output_to_operand_aliasing={{}: (7, {})} | custom-call | flops 3000000000 | bytes 1000000 | tf_op jit(solution)/shard_map/step_2/pallas_call | solution.py:213
  117.2 3.3 %collective-permute-done.7.refs_5_ = f32[520,128]{1,0:T(8,128)S(1)} collective-permute-done((f32[520,128]{1,0:T(8,128)S(1)}, f32[520,128]{1,0:T(8,128)S(1)}, u32[]{:S(2)}, u32[]{:S(2)}) %collective-permute-start.7) | collective-permute-done | bytes 266272 | tf_op jit(solution)/shard_map/ppermute | solution.py:56
  120.5 0.7 collective-permute-start.10
  121.3 5.6 %step_1.1 = f32[3072,128]{1,0:T(8,128)} custom-call(s32[6]{0:T(128)S(1)} %convert_element_type.27.refs_0_, s32[24]{0:T(128)S(1)} %bitcast.18, s32[24]{0:T(128)S(1)} %bitcast.21, f32[1040,128]{1,0:T(8,128)S(1)} %collective-permute-done.8.refs_3_, f32[520,128]{1,0:T(8,128)S(1)} %collective-permute-done.5.refs_4_, ...), custom_call_target="tpu_custom_call", output_to_operand_aliasing={{}: (13, {})} | custom-call | flops 100000000 | bytes 1000000 | tf_op jit(solution)/shard_map/step_1/pallas_call | solution.py:213
  (23 shorter events, 0.1 us)
Async XLA Ops:
  1.4 3.4 %copy-start.4 = (s32[1,1,8]{2,1,0:T(1,128)S(1)}, s32[1,1,8]{2,1,0:T(1,128)}, u32[]{:S(2)}) copy-start(s32[1,1,8]{2,1,0:T(1,128)} %param.12) | copy-start | bytes 100
  1.4 3.4 %copy-start.5 = (s32[1,1,8]{2,1,0:T(1,128)S(1)}, s32[1,1,8]{2,1,0:T(1,128)}, u32[]{:S(2)}) copy-start(s32[1,1,8]{2,1,0:T(1,128)} %param.11) | copy-start | bytes 100
  1.4 3.5 %copy-start.3 = (f32[1,1,8,128,128]{4,3,2,1,0:T(8,128)S(1)}, f32[1,1,8,128,128]{4,3,2,1,0:T(8,128)}, u32[]{:S(2)}) copy-start(f32[1,1,8,128,128]{4,3,2,1,0:T(8,128)} %param.10) | copy-start | bytes 1572868
  2.9 52.8 %collective-permute-start.3 = (f32[2568,128]{1,0:T(8,128)S(1)}, f32[2568,128]{1,0:T(8,128)}, u32[]{:S(2)}, u32[]{:S(2)}) collective-permute-start(f32[2568,128]{1,0:T(8,128)S(1)} %select_maximum_fusion.refs_4_), channel_id=1, source_target_pairs={{32,996},{33,997},{34,998},{35,999},{36,992},{37,993},{38,994},{39... | collective-permute-start | bytes 3944456 | tf_op jit(solution)/shard_map/ppermute | solution.py:56
  5.0 0.9 copy-start.2
  5.9 36.2 %collective-permute-start.2 = (f32[520,128]{1,0:T(8,128)}, f32[520,128]{1,0:T(8,128)S(1)}, u32[]{:S(2)}, u32[]{:S(2)}) collective-permute-start(f32[520,128]{1,0:T(8,128)} %get-tuple-element.45), channel_id=1, source_target_pairs={{0,3},{1,2},{2,0},{3,1},{4,7},{5,6},{6,4},{7,5},{8,11},{9,10},{10,... | collective-permute-start | bytes 798728 | tf_op jit(solution)/shard_map/ppermute | solution.py:56
  9.2 108.0 %collective-permute-start = (f32[2568,128]{1,0:T(8,128)S(1)}, f32[2568,128]{1,0:T(8,128)S(1)}, u32[]{:S(2)}, u32[]{:S(2)}) collective-permute-start(f32[2568,128]{1,0:T(8,128)S(1)} %select_maximum_fusion.refs_4_), channel_id=1, source_target_pairs={{0,960},{1,961},{2,962},{3,963},{4,964},{5,965},{6,966},{7,967},{8... | collective-permute-start | bytes 3944456 | tf_op jit(solution)/shard_map/ppermute | solution.py:56
  37.5 71.9 %collective-permute-start.1 = (f32[520,128]{1,0:T(8,128)}, f32[520,128]{1,0:T(8,128)S(1)}, u32[]{:S(2)}, u32[]{:S(2)}) collective-permute-start(f32[520,128]{1,0:T(8,128)} %get-tuple-element.46), channel_id=1, source_target_pairs={{0,30},{1,31},{2,0},{3,1},{4,2},{5,3},{6,4},{7,5},{8,6},{9,7},{10,... | collective-permute-start | bytes 798728 | tf_op jit(solution)/shard_map/ppermute | solution.py:56
  42.0 17.8 %copy-start = (s32[1,1,24]{2,1,0:T(1,128)S(1)}, s32[1,1,24]{2,1,0:T(1,128)}, u32[]{:S(2)}) copy-start(s32[1,1,24]{2,1,0:T(1,128)} %param.18) | copy-start | bytes 292
  42.0 17.8 %copy-start.1 = (s32[1,1,24]{2,1,0:T(1,128)S(1)}, s32[1,1,24]{2,1,0:T(1,128)}, u32[]{:S(2)}) copy-start(s32[1,1,24]{2,1,0:T(1,128)} %param.19) | copy-start | bytes 292
  42.1 68.6 %collective-permute-start.6 = (f32[520,128]{1,0:T(8,128)S(1)}, f32[520,128]{1,0:T(8,128)S(1)}, u32[]{:S(2)}, u32[]{:S(2)}) collective-permute-start(f32[520,128]{1,0:T(8,128)S(1)} %collective-permute-done.2.refs_4_.refs_9_), channel_id=1, source_target_pairs={{2,31},{3,30},{6,3},{7,2},{10,7},{11,6},{14,11},{15,10},{18,15},{1... | collective-permute-start | bytes 798728 | tf_op jit(solution)/shard_map/ppermute | solution.py:56
  55.7 61.5 %collective-permute-start.9 = (f32[2568,128]{1,0:T(8,128)}, f32[2568,128]{1,0:T(8,128)S(1)}, u32[]{:S(2)}, u32[]{:S(2)}) collective-permute-start(f32[2568,128]{1,0:T(8,128)} %collective-permute-done.3.refs_6_), channel_id=1, source_target_pairs={{992,996},{993,997},{994,998},{995,999},{996,992},{997,993},{998,9... | collective-permute-start | bytes 3944456 | tf_op jit(solution)/shard_map/ppermute | solution.py:56
  57.9 5.1 %collective-permute-start.4 = (f32[2568,128]{1,0:T(8,128)S(1)}, f32[2568,128]{1,0:T(8,128)S(1)}, u32[]{:S(2)}, u32[]{:S(2)}) collective-permute-start(f32[2568,128]{1,0:T(8,128)S(1)} %broadcast_select_fusion), channel_id=1, source_target_pairs={{0,32},{1,33},{2,34},{3,35},{4,36},{5,37},{6,38},{7,39},{8,40},{9,... | collective-permute-start | bytes 3944456 | tf_op jit(solution)/shard_map/ppermute | solution.py:56
  63.0 57.6 %collective-permute-start.8 = (f32[1040,128]{1,0:T(8,128)S(1)}, f32[1040,128]{1,0:T(8,128)S(1)}, u32[]{:S(2)}, u32[]{:S(2)}) collective-permute-start(f32[1040,128]{1,0:T(8,128)S(1)} %pad_maximum_fusion.refs_3_), channel_id=1, source_target_pairs={{1,0},{2,1},{3,2},{5,4},{6,5},{7,6},{9,8},{10,9},{11,10},{13,12},{... | collective-permute-start | bytes 1597448 | tf_op jit(solution)/shard_map/ppermute | solution.py:56
  109.4 11.2 %collective-permute-start.5 = (f32[520,128]{1,0:T(8,128)S(1)}, f32[520,128]{1,0:T(8,128)S(1)}, u32[]{:S(2)}, u32[]{:S(2)}) collective-permute-start(f32[520,128]{1,0:T(8,128)S(1)} %collective-permute-done.1.refs_3_.refs_8_), channel_id=1, source_target_pairs={{2,3},{6,7},{10,11},{14,15},{18,19},{22,23},{26,27},{30,31},{34,35... | collective-permute-start | bytes 798728 | tf_op jit(solution)/shard_map/ppermute | solution.py:56
  110.7 9.9 %collective-permute-start.7 = (f32[520,128]{1,0:T(8,128)S(1)}, f32[520,128]{1,0:T(8,128)S(1)}, u32[]{:S(2)}, u32[]{:S(2)}) collective-permute-start(f32[520,128]{1,0:T(8,128)S(1)} %collective-permute-done.6.refs_5_.refs_10_), channel_id=1, source_target_pairs={{2,3},{6,7},{10,11},{14,15},{18,19},{22,23},{26,27},{30,31},{34,35... | collective-permute-start | bytes 798728 | tf_op jit(solution)/shard_map/ppermute | solution.py:56
  120.5 0.7 collective-permute-start.10

commit v10 on v8

--- a/solution.py
+++ b/solution.py
@@ -232,6 +232,21 @@
     )(*operands)
 
 
+def joined(blocks, meta):
+    def kernel(blocks_ref, meta_ref, out_ref):
+        out_ref[pl.ds(0, RIGHT_ROWS), :] = blocks_ref[...]
+        out_ref[pl.ds(RIGHT_ROWS, PAD), :] = meta_ref[...]
+
+    return pl.pallas_call(
+        kernel,
+        out_shape=jax.ShapeDtypeStruct((RIGHT_ROWS + PAD, BS), jnp.float32),
+        in_specs=[VMEM_SPEC] * 2,
+        out_specs=VMEM_SPEC,
+        compiler_params=pltpu.CompilerParams(vmem_limit_bytes=8 * 2**20),
+        name="joined",
+    )(blocks, meta)
+
+
 def meta_rows(*parts):
     line = jnp.concatenate(parts).astype(jnp.float32)
     return jnp.pad(line[None], ((0, PAD - 1), (0, BS - line.shape[0])))
@@ -255,7 +270,7 @@
     low = jnp.concatenate([blocks[:HALF], left_meta])
     high = jnp.concatenate([blocks[HALF:], left_meta])
     left = jnp.concatenate([low, high])
-    right = jnp.concatenate([right_blocks.reshape(RIGHT_ROWS, BS), right_meta])
+    right = joined(right_blocks.reshape(RIGHT_ROWS, BS), right_meta)
     x = lax.axis_index("col") % GROUP
     row = lax.axis_index("row")
     core = row % 2

time: 125 us -> 125 us (level)
  other arithmetic: 4.33 us -> 2.86 us
  local copies, waits for them, and re-layouts: 0.18 us -> 1.5 us
    concatenate x1 -> x0, other arithmetic: 1.46 us -> none  [shards(): right = jnp.concatenate([right_blocks.reshape(RIGHT_ROWS, BS), right_meta])]
    unnamed x12 -> x14, local copies, waits for them, and re-layouts: 0.03 us -> 1.34 us
where the time goes in v10:
time: 125 us
  starting transfers between devices  56 us (45%)
  waiting for transfers between devices  49.4 us (40%)
  Pallas kernels  13.3 us (11%)
  other arithmetic  2.86 us (2%)
  between operations  1.56 us (1%)
  local copies, waits for them, and re-layouts  1.5 us (1%)
    ppermute x11, starting transfers between devices, send(): return lax.ppermute(block, AXES, pairs)  56 us
    ppermute x11, waiting for transfers between devices, send(): return lax.ppermute(block, AXES, pairs)  49.4 us
    pallas_call x3, Pallas kernels, step_call(): pl.pallas_call(functools.partial(step_kernel, passes, len(arrays), before...  13.2 us
  transfers between devices with their start and end apart: 11, of which 3 were waited for; matrix products, arithmetic and copies ran while one was open for 2% of the time, Pallas kernels for 5%

profile of v10, /device:TPU:993, one launch (start us, length us, event | category | flops | bytes accessed | tf_op | source)
XLA Modules:
  0.0 124.6 jit_solution(6447116454300898891)
XLA Ops:
  0.7 0.7 add_convert_fusion.1
  1.4 1.3 %copy-done = f32[1,1,20,128,128]{4,3,2,1,0:T(8,128)S(1)} copy-done((f32[1,1,20,128,128]{4,3,2,1,0:T(8,128)S(1)}, f32[1,1,20,128,128]{4,3,2,1,0:T(8,128)}, u32[]{:S(2)}) %copy-start) | copy-done | bytes 1310744
  2.7 0.1 joined.1.refs_4_
  2.8 2.8 %collective-permute-start.1 = (f32[2568,128]{1,0:T(8,128)S(1)}, f32[2568,128]{1,0:T(8,128)S(1)}, u32[]{:S(2)}, u32[]{:S(2)}) collective-permute-start(f32[2568,128]{1,0:T(8,128)S(1)} %joined.1.refs_4_), channel_id=1, source_target_pairs={{32,996},{33,997},{34,998},{35,999},{36,992},{37,993},{38,994},{39... | collective-permute-start | bytes 3944456 | tf_op jit(solution)/shard_map/ppermute | solution.py:56
  6.4 0.9 pad_maximum_fusion.1
  7.3 4.4 %collective-permute-start = (f32[520,128]{1,0:T(8,128)}, f32[520,128]{1,0:T(8,128)S(1)}, u32[]{:S(2)}, u32[]{:S(2)}) collective-permute-start(f32[520,128]{1,0:T(8,128)} %get-tuple-element.46), channel_id=1, source_target_pairs={{0,3},{1,2},{2,0},{3,1},{4,7},{5,6},{6,4},{7,5},{8,11},{9,10},{10,... | collective-permute-start | bytes 798728 | tf_op jit(solution)/shard_map/ppermute | solution.py:56
  11.7 11.5 %collective-permute-start.3 = (f32[520,128]{1,0:T(8,128)}, f32[520,128]{1,0:T(8,128)S(1)}, u32[]{:S(2)}, u32[]{:S(2)}) collective-permute-start(f32[520,128]{1,0:T(8,128)} %get-tuple-element.45), channel_id=1, source_target_pairs={{0,30},{1,31},{2,0},{3,1},{4,2},{5,3},{6,4},{7,5},{8,6},{9,7},{10,... | collective-permute-start | bytes 798728 | tf_op jit(solution)/shard_map/ppermute | solution.py:56
  23.2 0.1 stack.27
  23.3 1.0 pad_maximum_fusion.refs_3_
  24.4 0.7 collective-permute-start.6
  25.1 21.9 %collective-permute-done.1.refs_6_ = f32[2568,128]{1,0:T(8,128)S(1)} collective-permute-done((f32[2568,128]{1,0:T(8,128)S(1)}, f32[2568,128]{1,0:T(8,128)S(1)}, u32[]{:S(2)}, u32[]{:S(2)}) %collective-permute-start.1) | collective-permute-done | bytes 1314848 | tf_op jit(solution)/shard_map/ppermute | solution.py:56
  47.0 0.7 collective-permute-start.2
  47.7 0.2 broadcast_select_fusion
  47.9 1.9 %collective-permute-start.9 = (f32[2568,128]{1,0:T(8,128)S(1)}, f32[2568,128]{1,0:T(8,128)S(1)}, u32[]{:S(2)}, u32[]{:S(2)}) collective-permute-start(f32[2568,128]{1,0:T(8,128)S(1)} %collective-permute-done.1.refs_6_), channel_id=1, source_target_pairs={{992,996},{993,997},{994,998},{995,999},{996,992},{997,993},{998,9... | collective-permute-start | bytes 3944456 | tf_op jit(solution)/shard_map/ppermute | solution.py:56
  49.8 30.0 %collective-permute-start.4 = (f32[2568,128]{1,0:T(8,128)S(1)}, f32[2568,128]{1,0:T(8,128)S(1)}, u32[]{:S(2)}, u32[]{:S(2)}) collective-permute-start(f32[2568,128]{1,0:T(8,128)S(1)} %broadcast_select_fusion), channel_id=1, source_target_pairs={{0,32},{1,33},{2,34},{3,35},{4,36},{5,37},{6,38},{7,39},{8,40},{9,... | collective-permute-start | bytes 3944456 | tf_op jit(solution)/shard_map/ppermute | solution.py:56
  79.9 3.1 %step_0.1.refs_7_ = f32[3072,128]{1,0:T(8,128)} custom-call(s32[6]{0:T(128)S(1)} %convert_element_type.27.refs_0_, s32[24]{0:T(128)S(1)} %bitcast.17, s32[24]{0:T(128)S(1)} %bitcast.20, f32[1040,128]{1,0:T(8,128)S(1)} %pad_maximum_fusion.refs_3_, f32[2568,128]{1,0:T(8,128)S(1)} %joined.1.refs_4_), custom_call_target="tpu_custom_call" | custom-call | flops 15000000512 | bytes 1000000 | tf_op jit(solution)/shard_map/step_0/pallas_call | solution.py:213
  83.0 1.3 %collective-permute-start.8 = (f32[1040,128]{1,0:T(8,128)S(1)}, f32[1040,128]{1,0:T(8,128)S(1)}, u32[]{:S(2)}, u32[]{:S(2)}) collective-permute-start(f32[1040,128]{1,0:T(8,128)S(1)} %pad_maximum_fusion.refs_3_), channel_id=1, source_target_pairs={{1,0},{2,1},{3,2},{5,4},{6,5},{7,6},{9,8},{10,9},{11,10},{13,12},{... | collective-permute-start | bytes 1597448 | tf_op jit(solution)/shard_map/ppermute | solution.py:56
  84.3 0.7 collective-permute-start.5
  85.0 0.7 collective-permute-start.7
  85.7 3.0 %step_2.1.refs_13_ = f32[3072,128]{1,0:T(8,128)} custom-call(s32[6]{0:T(128)S(1)} %convert_element_type.27.refs_0_, s32[24]{0:T(128)S(1)} %bitcast.18, s32[24]{0:T(128)S(1)} %bitcast.21, f32[520,128]{1,0:T(8,128)S(1)} %collective-permute-done.3.refs_3_.refs_8_, f32[520,128]{1,0:T(8,128)S(1)} %collective-permute-done.refs_4_.refs_9_, ...), custom_call_target="tpu_custom_call", output_to_operand_aliasing={{}: (7, {})} | custom-call | flops 3000000000 | bytes 1000000 | tf_op jit(solution)/shard_map/step_2/pallas_call | solution.py:213
  88.8 15.1 %collective-permute-done.9.refs_12_ = f32[2568,128]{1,0:T(8,128)S(1)} collective-permute-done((f32[2568,128]{1,0:T(8,128)S(1)}, f32[2568,128]{1,0:T(8,128)S(1)}, u32[]{:S(2)}, u32[]{:S(2)}) %collective-permute-start.9) | collective-permute-done | bytes 1314848 | tf_op jit(solution)/shard_map/ppermute | solution.py:56
  103.9 1.3 %collective-permute-start.10 = (f32[2568,128]{1,0:T(8,128)S(1)}, f32[2568,128]{1,0:T(8,128)S(1)}, u32[]{:S(2)}, u32[]{:S(2)}) collective-permute-start(f32[2568,128]{1,0:T(8,128)S(1)} %collective-permute-done.2.refs_11_), channel_id=1, source_target_pairs={{960,992},{961,993},{962,994},{963,995},{964,996},{965,997},{966,9... | collective-permute-start | bytes 3944456 | tf_op jit(solution)/shard_map/ppermute | solution.py:56
  105.2 12.4 %collective-permute-done.10.refs_7_ = f32[2568,128]{1,0:T(8,128)S(1)} collective-permute-done((f32[2568,128]{1,0:T(8,128)S(1)}, f32[2568,128]{1,0:T(8,128)S(1)}, u32[]{:S(2)}, u32[]{:S(2)}) %collective-permute-start.10) | collective-permute-done | bytes 1314848 | tf_op jit(solution)/shard_map/ppermute | solution.py:56
  117.6 7.1 %step_1.1 = f32[3072,128]{1,0:T(8,128)} custom-call(s32[6]{0:T(128)S(1)} %convert_element_type.27.refs_0_, s32[24]{0:T(128)S(1)} %bitcast.19, s32[24]{0:T(128)S(1)} %bitcast.22, f32[1040,128]{1,0:T(8,128)S(1)} %collective-permute-done.8.refs_3_, f32[520,128]{1,0:T(8,128)S(1)} %collective-permute-done.5.refs_4_, ...), custom_call_target="tpu_custom_call", output_to_operand_aliasing={{}: (13, {})} | custom-call | flops 100000000 | bytes 1000000 | tf_op jit(solution)/shard_map/step_1/pallas_call | solution.py:213
  (26 shorter events, 0.2 us)
Async XLA Ops:
  1.4 1.3 %copy-start = (f32[1,1,20,128,128]{4,3,2,1,0:T(8,128)S(1)}, f32[1,1,20,128,128]{4,3,2,1,0:T(8,128)}, u32[]{:S(2)}) copy-start(f32[1,1,20,128,128]{4,3,2,1,0:T(8,128)} %param.14) | copy-start | bytes 3932164
  2.7 3.5 %copy-start.5 = (s32[1,1,8]{2,1,0:T(1,128)S(1)}, s32[1,1,8]{2,1,0:T(1,128)}, u32[]{:S(2)}) copy-start(s32[1,1,8]{2,1,0:T(1,128)} %param.12) | copy-start | bytes 100
  2.7 3.5 %copy-start.6 = (s32[1,1,8]{2,1,0:T(1,128)S(1)}, s32[1,1,8]{2,1,0:T(1,128)}, u32[]{:S(2)}) copy-start(s32[1,1,8]{2,1,0:T(1,128)} %param.11) | copy-start | bytes 100
  2.7 3.6 %copy-start.4 = (f32[1,1,8,128,128]{4,3,2,1,0:T(8,128)S(1)}, f32[1,1,8,128,128]{4,3,2,1,0:T(8,128)}, u32[]{:S(2)}) copy-start(f32[1,1,8,128,128]{4,3,2,1,0:T(8,128)} %param.10) | copy-start | bytes 1572868
  2.8 44.2 %collective-permute-start.1 = (f32[2568,128]{1,0:T(8,128)S(1)}, f32[2568,128]{1,0:T(8,128)S(1)}, u32[]{:S(2)}, u32[]{:S(2)}) collective-permute-start(f32[2568,128]{1,0:T(8,128)S(1)} %joined.1.refs_4_), channel_id=1, source_target_pairs={{32,996},{33,997},{34,998},{35,999},{36,992},{37,993},{38,994},{39... | collective-permute-start | bytes 3944456 | tf_op jit(solution)/shard_map/ppermute | solution.py:56
  6.4 0.9 copy-start.3
  7.3 17.1 %collective-permute-start = (f32[520,128]{1,0:T(8,128)}, f32[520,128]{1,0:T(8,128)S(1)}, u32[]{:S(2)}, u32[]{:S(2)}) collective-permute-start(f32[520,128]{1,0:T(8,128)} %get-tuple-element.46), channel_id=1, source_target_pairs={{0,3},{1,2},{2,0},{3,1},{4,7},{5,6},{6,4},{7,5},{8,11},{9,10},{10,... | collective-permute-start | bytes 798728 | tf_op jit(solution)/shard_map/ppermute | solution.py:56
  11.7 72.7 %collective-permute-start.3 = (f32[520,128]{1,0:T(8,128)}, f32[520,128]{1,0:T(8,128)S(1)}, u32[]{:S(2)}, u32[]{:S(2)}) collective-permute-start(f32[520,128]{1,0:T(8,128)} %get-tuple-element.45), channel_id=1, source_target_pairs={{0,30},{1,31},{2,0},{3,1},{4,2},{5,3},{6,4},{7,5},{8,6},{9,7},{10,... | collective-permute-start | bytes 798728 | tf_op jit(solution)/shard_map/ppermute | solution.py:56
  24.3 55.5 %copy-start.1 = (s32[1,1,24]{2,1,0:T(1,128)S(1)}, s32[1,1,24]{2,1,0:T(1,128)}, u32[]{:S(2)}) copy-start(s32[1,1,24]{2,1,0:T(1,128)} %param.18) | copy-start | bytes 292
  24.3 55.5 %copy-start.2 = (s32[1,1,24]{2,1,0:T(1,128)S(1)}, s32[1,1,24]{2,1,0:T(1,128)}, u32[]{:S(2)}) copy-start(s32[1,1,24]{2,1,0:T(1,128)} %param.19) | copy-start | bytes 292
  24.4 60.7 %collective-permute-start.6 = (f32[520,128]{1,0:T(8,128)S(1)}, f32[520,128]{1,0:T(8,128)S(1)}, u32[]{:S(2)}, u32[]{:S(2)}) collective-permute-start(f32[520,128]{1,0:T(8,128)S(1)} %collective-permute-done.refs_4_.refs_9_), channel_id=1, source_target_pairs={{2,31},{3,30},{6,3},{7,2},{10,7},{11,6},{14,11},{15,10},{18,15},{1... | collective-permute-start | bytes 798728 | tf_op jit(solution)/shard_map/ppermute | solution.py:56
  47.0 41.8 %collective-permute-start.2 = (f32[2568,128]{1,0:T(8,128)S(1)}, f32[2568,128]{1,0:T(8,128)S(1)}, u32[]{:S(2)}, u32[]{:S(2)}) collective-permute-start(f32[2568,128]{1,0:T(8,128)S(1)} %joined.1.refs_4_), channel_id=1, source_target_pairs={{0,960},{1,961},{2,962},{3,963},{4,964},{5,965},{6,966},{7,967},{8... | collective-permute-start | bytes 3944456 | tf_op jit(solution)/shard_map/ppermute | solution.py:56
  47.9 56.0 %collective-permute-start.9 = (f32[2568,128]{1,0:T(8,128)S(1)}, f32[2568,128]{1,0:T(8,128)S(1)}, u32[]{:S(2)}, u32[]{:S(2)}) collective-permute-start(f32[2568,128]{1,0:T(8,128)S(1)} %collective-permute-done.1.refs_6_), channel_id=1, source_target_pairs={{992,996},{993,997},{994,998},{995,999},{996,992},{997,993},{998,9... | collective-permute-start | bytes 3944456 | tf_op jit(solution)/shard_map/ppermute | solution.py:56
  49.8 33.2 %collective-permute-start.4 = (f32[2568,128]{1,0:T(8,128)S(1)}, f32[2568,128]{1,0:T(8,128)S(1)}, u32[]{:S(2)}, u32[]{:S(2)}) collective-permute-start(f32[2568,128]{1,0:T(8,128)S(1)} %broadcast_select_fusion), channel_id=1, source_target_pairs={{0,32},{1,33},{2,34},{3,35},{4,36},{5,37},{6,38},{7,39},{8,40},{9,... | collective-permute-start | bytes 3944456 | tf_op jit(solution)/shard_map/ppermute | solution.py:56
  83.0 20.9 %collective-permute-start.8 = (f32[1040,128]{1,0:T(8,128)S(1)}, f32[1040,128]{1,0:T(8,128)S(1)}, u32[]{:S(2)}, u32[]{:S(2)}) collective-permute-start(f32[1040,128]{1,0:T(8,128)S(1)} %pad_maximum_fusion.refs_3_), channel_id=1, source_target_pairs={{1,0},{2,1},{3,2},{5,4},{6,5},{7,6},{9,8},{10,9},{11,10},{13,12},{... | collective-permute-start | bytes 1597448 | tf_op jit(solution)/shard_map/ppermute | solution.py:56
  84.3 19.5 %collective-permute-start.5 = (f32[520,128]{1,0:T(8,128)S(1)}, f32[520,128]{1,0:T(8,128)S(1)}, u32[]{:S(2)}, u32[]{:S(2)}) collective-permute-start(f32[520,128]{1,0:T(8,128)S(1)} %collective-permute-done.3.refs_3_.refs_8_), channel_id=1, source_target_pairs={{2,3},{6,7},{10,11},{14,15},{18,19},{22,23},{26,27},{30,31},{34,35... | collective-permute-start | bytes 798728 | tf_op jit(solution)/shard_map/ppermute | solution.py:56
  85.0 18.8 %collective-permute-start.7 = (f32[520,128]{1,0:T(8,128)S(1)}, f32[520,128]{1,0:T(8,128)S(1)}, u32[]{:S(2)}, u32[]{:S(2)}) collective-permute-start(f32[520,128]{1,0:T(8,128)S(1)} %collective-permute-done.6.refs_5_.refs_10_), channel_id=1, source_target_pairs={{2,3},{6,7},{10,11},{14,15},{18,19},{22,23},{26,27},{30,31},{34,35... | collective-permute-start | bytes 798728 | tf_op jit(solution)/shard_map/ppermute | solution.py:56
  103.9 13.7 %collective-permute-start.10 = (f32[2568,128]{1,0:T(8,128)S(1)}, f32[2568,128]{1,0:T(8,128)S(1)}, u32[]{:S(2)}, u32[]{:S(2)}) collective-permute-start(f32[2568,128]{1,0:T(8,128)S(1)} %collective-permute-done.2.refs_11_), channel_id=1, source_target_pairs={{960,992},{961,993},{962,994},{963,995},{964,996},{965,997},{966,9... | collective-permute-start | bytes 3944456 | tf_op jit(solution)/shard_map/ppermute | solution.py:56
